TPU v7x, 32 devices: a whole 2x2x4 slice. The times are simulated.
32 devices in a mesh: xy: 8 (over z, y), gz: 4 (over x, core).
Axes of the slice: x: 2, y: 2, z: 4, core: 2. Of those that a mesh axis runs over, the one named last changes fastest.
Arguments:
- head_old: float32 [32, 64, 512], P('gz', 'xy'), may hold values from -0.12 to -0.02
- soil_type: int32 [32, 64, 512], P('gz', 'xy'), may hold values from 0 to 11
- soil_table: float32 [5, 12], replicated, may hold values from 0.03 to 2.2, as said below
- land_mask: int32 [64, 512], P('xy'), may hold values 0 or 1
- sun_bin: int32 [64, 512], P('xy'), may hold values from 0 to 23
Outputs:
- head_new: float32 [32, 64, 512], P('gz', 'xy')
Inputs may be any that keep to these rules, and one draw needn't show every extreme that they name: `soil_table`: row 0 lies in 0.03 to 0.10, row 1 in 0.35 to 0.50, row 2 in 0.5 to 2.0, row 3 in 1.4 to 2.2, row 4 in 0.3 to 1.0.
All inputs are finite; a program needn't handle non-finite values. No bound on the sum of `land_mask` on one device may be relied on, other than what follows from the above.
Results may differ from a plain program's by a relative error of at most 0.00017.
Values sent between devices are 32-bit elements; how exact they have to be, the bound alone decides.
No kernel may reach another device: no remote copies, remote signals or barrier semaphores. Data moves between devices by JAX's collectives and lax.ppermute only.
A program may use at most 128 MiB of HBM per device.

v0:
```python
import math

import jax
import jax.numpy as jnp
from jax import lax
from jax.sharding import PartitionSpec as P

LEVELS = 3
NEWTON = 2


dt_step = 20.0
et_peak = 0.008
gravity = 0.1
root_decay = 3.0


def with_halo(x, sides, width):
    for axis, dim in sides:
        size, length = (lax.axis_size(axis), x.shape[dim])
        up = [(i, (i + 1) % size) for i in range(size - 1)]
        down = [(j, i) for i, j in up]
        last = lax.slice_in_dim(x, length - width, length, axis=dim)
        initial = lax.slice_in_dim(x, 0, width, axis=dim)
        before = lax.ppermute(last, axis, up)
        after = lax.ppermute(initial, axis, down)
        x = jnp.concatenate([before, x, after], axis=dim)
    return x


def from_root(value, axis, source):
    kept = jnp.where(lax.axis_index(axis) == source, value, 0).astype(value.dtype)
    return lax.psum(kept, axis)


def lookup(soil_type, soil_table):
    columns = []
    for position in range(5):
        looked = jnp.zeros(soil_type.shape, jnp.float32)
        for category in range(soil_table.shape[1]):
            looked = looked + jnp.where(soil_type == category, soil_table[position, category], 0.0)
        columns.append(looked)
    return columns


def soil_state(pressure, params):
    water_resid, water_sat, alpha_coef, shape_coef, k_sat = params
    expon_m = 1.0 - 1.0 / shape_coef
    scaled = jnp.abs(alpha_coef * pressure)
    power_p = jnp.power(scaled, shape_coef)
    base_one = 1.0 + power_p
    saturation = jnp.power(base_one, -expon_m)
    slope = (
        expon_m
        * shape_coef
        * alpha_coef
        * jnp.power(scaled, shape_coef - 1.0)
        * jnp.power(base_one, -expon_m - 1.0)
    )
    content = water_resid + (water_sat - water_resid) * saturation
    capacity = (water_sat - water_resid) * slope
    relative = jnp.sqrt(saturation) * jnp.square(1.0 - jnp.power(power_p / base_one, expon_m))
    conduct = k_sat * relative
    return (saturation, slope, content, capacity, conduct)


def pair_sum(tensor, position):
    extent = tensor.shape
    split_shape = extent[:position] + (extent[position] // 2, 2) + extent[position + 1 :]
    return jnp.sum(tensor.reshape(split_shape), axis=position + 1)


def make_stencil(storage, face_across, face_vertical, face_along):
    diagonal = (
        storage
        + face_across[:, :-1, :]
        + face_across[:, 1:, :]
        + face_vertical[:-1]
        + face_vertical[1:]
    )
    diagonal = diagonal + face_along[..., :-1] + face_along[..., 1:]
    return (storage, face_across, face_vertical, face_along, diagonal)


def coarsen(stencil):
    storage, face_across, face_vertical, face_along, diagonal = stencil
    store_new = pair_sum(pair_sum(pair_sum(storage, 0), 1), 2)
    across_new = pair_sum(pair_sum(face_across[:, ::2, :], 0), 2)
    vertical_new = pair_sum(pair_sum(face_vertical[::2], 1), 2)
    along_new = pair_sum(pair_sum(face_along[..., ::2], 0), 1)
    return make_stencil(store_new, across_new, vertical_new, along_new)


def restrict(residual):
    return pair_sum(pair_sum(pair_sum(residual, 0), 1), 2)


def prolong(coarse):
    return jnp.repeat(jnp.repeat(jnp.repeat(coarse, 2, axis=0), 2, axis=1), 2, axis=2)


def global_parity(extent):
    layer_count, row_count, col_count = extent
    layer_at = lax.axis_index("gz") * layer_count + lax.iota(jnp.int32, layer_count)
    row_at = lax.axis_index("xy") * row_count + lax.iota(jnp.int32, row_count)
    col_at = lax.iota(jnp.int32, col_count)
    return jnp.remainder(layer_at[:, None, None] + row_at[None, :, None] + col_at[None, None, :], 2)


def neighbour_sum(padded, stencil):
    storage, face_across, face_vertical, face_along, diagonal = stencil
    pad_across = padded[1:-1]
    pad_vertical = padded[:, 1:-1]
    field = padded[1:-1, 1:-1]
    pad_along = jnp.pad(field, ((0, 0), (0, 0), (1, 1)))
    total = (
        face_across[:, :-1, :] * pad_across[:, :-2, :]
        + face_across[:, 1:, :] * pad_across[:, 2:, :]
    )
    total = total + face_vertical[:-1] * pad_vertical[:-2] + face_vertical[1:] * pad_vertical[2:]
    total = (
        total
        + face_along[..., :-1] * pad_along[..., :-2]
        + face_along[..., 1:] * pad_along[..., 2:]
    )
    return total


def all_faces(correction):
    return with_halo(correction, (("xy", 1), ("gz", 0)), 1)


def colour_update(correction, source, stencil, target, colour):
    padded = all_faces(correction)
    updated = (source + neighbour_sum(padded, stencil)) / stencil[4]
    return jnp.where(colour == target, updated, correction)


def solve_blocks(block_rhs, block_store, block_across, block_vertical, slab_count):
    across_up = jnp.concatenate([block_across[slab_count:], jnp.zeros((slab_count,), jnp.float32)])
    vertical_up = jnp.concatenate([block_vertical[1:], jnp.zeros((1,), jnp.float32)])
    diagonal = block_store + block_across + across_up + block_vertical + vertical_up
    matrix = (
        jnp.diag(diagonal)
        - jnp.diag(block_across[slab_count:], slab_count)
        - jnp.diag(block_across[slab_count:], -slab_count)
    )
    matrix = matrix - jnp.diag(block_vertical[1:], 1) - jnp.diag(block_vertical[1:], -1)
    factor = jnp.linalg.cholesky(matrix)
    return jax.scipy.linalg.cho_solve((factor, True), block_rhs)


def block_correction(residual, stencil):
    storage, face_across, face_vertical, face_along, diagonal = stencil
    terms = (
        jnp.sum(residual).reshape(1),
        jnp.sum(storage).reshape(1),
        jnp.sum(face_across[:, 0, :]).reshape(1),
        jnp.sum(face_vertical[0]).reshape(1),
    )
    block_rhs, block_store, block_across, block_vertical = (
        lax.all_gather(terms[0], ("xy", "gz"), axis=0, tiled=True),
        lax.all_gather(terms[1], ("xy", "gz"), axis=0, tiled=True),
        lax.all_gather(terms[2], ("xy", "gz"), axis=0, tiled=True),
        lax.all_gather(terms[3], ("xy", "gz"), axis=0, tiled=True),
    )
    slab_count = lax.axis_size("gz")
    flat_index = lax.axis_index("xy") * slab_count + lax.axis_index("gz")

    def solve_here():
        return solve_blocks(block_rhs, block_store, block_across, block_vertical, slab_count)

    def nothing_here():
        return jnp.zeros_like(block_rhs)

    answer = lax.cond(flat_index == 0, solve_here, nothing_here)
    answer = from_root(answer, ("xy", "gz"), 0)
    return lax.dynamic_slice_in_dim(answer, flat_index, 1)


def coarse_step(stencils, residual, level_index):
    if level_index + 1 < len(stencils):
        return prolong(vcycle(stencils, restrict(residual), level_index + 1))
    return block_correction(residual, stencils[level_index])


def vcycle(stencils, source, level_index):
    stencil = stencils[level_index]
    diagonal = stencil[4]
    colour = global_parity(source.shape)
    correction = jnp.where(colour == 0, source / diagonal, 0.0)
    correction = colour_update(correction, source, stencil, 1, colour)
    padded = all_faces(correction)
    residual = source - (diagonal * correction - neighbour_sum(padded, stencil))
    correction = correction + coarse_step(stencils, residual, level_index)
    correction = colour_update(correction, source, stencil, 0, colour)
    correction = colour_update(correction, source, stencil, 1, colour)
    return correction


def per_device(head_old, soil_type, soil_table, land_mask, sun_bin):
    layer_count, row_count, col_count = head_old.shape
    strip_index = lax.axis_index("xy")
    slab_index = lax.axis_index("gz")
    strip_total = lax.axis_size("xy")
    slab_total = lax.axis_size("gz")
    total_layers = layer_count * slab_total
    params = lookup(soil_type, soil_table)
    layer_depth = (slab_index * layer_count + lax.iota(jnp.int32, layer_count)).astype(jnp.float32)
    root_share = jnp.exp(-root_decay * layer_depth / total_layers)
    sun_share = jnp.maximum(0.0, jnp.sin(math.pi * (sun_bin.astype(jnp.float32) - 6.0) / 12.0))
    forcing = et_peak * sun_share * land_mask.astype(jnp.float32)
    sink_rate = forcing[None] * root_share[:, None, None]
    content_old = soil_state(head_old, params)[2]
    layer_ghost = (slab_index * layer_count - 1 + lax.iota(jnp.int32, layer_count + 2)).astype(
        jnp.float32
    )
    across_faces = lax.iota(jnp.int32, row_count + 1)
    keep_across = jnp.logical_not(
        (across_faces == 0) & (strip_index == 0)
        | (across_faces == row_count) & (strip_index == strip_total - 1)
    )
    vertical_faces = lax.iota(jnp.int32, layer_count + 1)
    keep_vertical = jnp.logical_not(
        (vertical_faces == 0) & (slab_index == 0)
        | (vertical_faces == layer_count) & (slab_index == slab_total - 1)
    )
    pressure = head_old
    for newton_step in range(NEWTON):
        saturation, slope, content, capacity, conduct = soil_state(pressure, params)
        stacked = with_halo(jnp.stack([pressure, conduct]), (("xy", 2), ("gz", 1)), 1)
        head_pad = stacked[0]
        cond_pad = stacked[1]
        face_across = jnp.where(
            keep_across[None, :, None], 0.5 * (cond_pad[1:-1, :-1, :] + cond_pad[1:-1, 1:, :]), 0.0
        )
        face_vertical = jnp.where(
            keep_vertical[:, None, None],
            0.5 * (cond_pad[:-1, 1:-1, :] + cond_pad[1:, 1:-1, :]),
            0.0,
        )
        zero_y = jnp.zeros_like(conduct[..., :1])
        face_along = jnp.concatenate(
            [zero_y, 0.5 * (conduct[..., :-1] + conduct[..., 1:]), zero_y], axis=2
        )
        pad_across = head_pad[1:-1]
        flux_across = face_across * (pad_across[:, :-1, :] - pad_across[:, 1:, :])
        pad_vertical = head_pad[:, 1:-1] - gravity * layer_ghost[:, None, None]
        flux_vertical = face_vertical * (pad_vertical[:-1] - pad_vertical[1:])
        pad_along = jnp.pad(pressure, ((0, 0), (0, 0), (1, 1)))
        flux_along = face_along * (pad_along[..., :-1] - pad_along[..., 1:])
        residual = (content - content_old) / dt_step + sink_rate * saturation
        residual = residual + (flux_across[:, 1:, :] - flux_across[:, :-1, :])
        residual = residual + (flux_along[..., 1:] - flux_along[..., :-1])
        residual = residual + (flux_vertical[1:] - flux_vertical[:-1])
        storage = capacity / dt_step + sink_rate * slope
        stencils = [make_stencil(storage, face_across, face_vertical, face_along)]
        for level_step in range(LEVELS - 1):
            stencils.append(coarsen(stencils[-1]))
        pressure = pressure + vcycle(stencils, -residual, 0)
    return pressure


def solution(mesh):
    in_specs = (P("gz", "xy", None), P("gz", "xy", None), P(), P("xy", None), P("xy", None))
    out_specs = P("gz", "xy", None)
    return jax.shard_map(
        per_device, mesh=mesh, in_specs=in_specs, out_specs=out_specs, check_vma=False
    )
```

profile of v0, /device:TPU:1, one launch (start us, length us, event | category | flops | bytes accessed | tf_op | source)
XLA Modules:
  0.0 758.3 jit_solution(4854550986227901179)
XLA Ops:
  8.6 32.7 %fusion.389 = (f32[]{:T(128)}, f32[8,8,512]{2,1,0:T(8,128)S(1)}, f32[8,8,512]{2,1,0:T(8,128)S(1)}, f32[8,8,512]{2,1,0:T(8,128)S(1)}, pred[8,8,512]{2,1,0:T(8,128...) fusion(f32[8]{0:T(128)S(1)} %multiply_exponential_fusion, ...), kind=kLoop, calls=%fused_computation.887 | loop fusion | flops 4030463 | bytes 1065188 | tf_op jit(solution)/shard_map/reduce_sum | solution.py:157
  41.4 9.9 %fusion.88 = (f32[8,8,512]{2,1,0:T(8,128)S(1)}, f32[8,8,512]{2,1,0:T(8,128)}) fusion(f32[8,8,512]{2,1,0:T(8,128)S(1)} %get-tuple-element.58, f32[8,8,512]{2,1,0:T(8,128)S(1)} %get-tuple-element.57, f32[8,8,512]{2,1,0:T(8,128)} %param.12, pred[8,8,512]{2,1,0:T(8,128)(4,1)S(1)} %get-tuple-element.70, f32[]{:T(128)} %bitcast.74, ...), kind=kLoop, calls=%fused_computation.193 | loop fusion | flops 1114112 | bytes 1048624 | tf_op jit(solution)/shard_map/mul | solution.py:63
  51.3 4.0 collective-permute-start
  66.7 4.0 collective-permute-start.2
  72.6 3.6 collective-permute-done.3
  77.1 15.9 %divide_select_fusion.1 = (f32[8,8,512]{2,1,0:T(8,128)S(1)}, f32[8,8,512]{2,1,0:T(8,128)S(1)}, f32[8,8,512]{2,1,0:T(8,128)S(1)}) fusion(f32[9,8,512]{2,1,0:T(8,128)S(1)} %get-tuple-element.77, f32[8,9,512]{2,1,0:T(8,128)S(1)} %get-tuple-element.75, f32[8,8,511]{2,1,0:T(8,128)S(1)} %fusion.166, s32[8,8]{1,0:T(8,128)S(1)} %broadcast_add_fusion, ...), kind=kLoop, calls=%fused_computation.357 | loop fusion | flops 2883584 | bytes 2769024 | tf_op jit(solution)/shard_map/jit(_where)/select_n | solution.py:191
  93.0 4.3 collective-permute-start.4
  99.1 3.4 collective-permute-done.5
  111.7 5.1 collective-permute-start.8
  146.2 4.0 collective-permute-start.12
  154.6 4.6 collective-permute-start.14
  172.7 3.4 collective-permute-start.18
  181.8 3.6 collective-permute-start.20
  189.8 3.4 collective-permute-start.22
  198.2 3.6 collective-permute-start.24
  206.1 3.4 collective-permute-start.26
  215.7 37.7 %all-reduce.47 = (f32[32]{0:T(128)S(1)}, f32[32]{0:T(128)S(1)}, f32[32]{0:T(128)S(1)}, f32[32]{0:T(128)S(1)}) all-reduce(f32[32]{0:T(128)S(1)} %dynamic-update-slice.2, f32[32]{0:T(128)S(1)} %dynamic-update-slice.3, f32[32]{0:T(128)S(1)} %dynamic-update-slice.4, f32[32]{0:T(128)S(1)} %dynamic-update-slice.5), channel_id=1, replica_groups=mesh['xy'=8,'gz'=4] {'xy','gz'}, use_global_device_ids=true, to_apply=%add.38 | all-reduce | flops 128 | bytes 1024 | tf_op jit(solution)/shard_map/cond | solution.py:176
  253.5 44.1 %psum.14 = f32[32]{0:T(128)S(1)} all-reduce(f32[32]{0:T(128)S(1)} %broadcast_select_fusion.1), channel_id=1, replica_groups=mesh['xy'=8,'gz'=4] {'xy','gz'}, use_global_device_ids=true, to_apply=%region_32.35 | all-reduce | flops 32 | bytes 256 | tf_op jit(solution)/shard_map/psum | solution.py:33
  302.4 4.8 collective-permute-done.29
  307.2 6.4 collective-permute-start.30
  318.7 4.5 collective-permute-start.32
  327.5 3.4 collective-permute-start.34
  340.4 3.0 collective-permute-done.37
  343.4 3.4 collective-permute-start.38
  348.7 3.0 collective-permute-done.39
  352.0 3.7 collective-permute-start.40
  357.0 3.0 collective-permute-done.41
  360.1 3.4 collective-permute-start.42
  377.6 3.1 collective-permute-done.45
  380.8 3.5 collective-permute-start.46
  386.3 3.3 collective-permute-done.47
  394.9 3.1 collective-permute-done.49
  398.1 3.3 collective-permute-start.50
  403.4 3.3 collective-permute-done.51
  406.8 16.9 %fusion.383 = (f32[]{:T(128)}, f32[8,8,512]{2,1,0:T(8,128)S(1)}, f32[8,8,512]{2,1,0:T(8,128)S(1)}) fusion(f32[8]{0:T(128)S(1)} %copy-done.75, f32[8,512]{1,0:T(8,128)S(1)} %copy-done.47, f32[8,8,512]{2,1,0:T(8,128)S(1)} %get-tuple-element.58, f32[8,8,512]{2,1,0:T(8,128)S(1)} %get-tuple-element.57, pred[8,8,512]{2,1,0:T(8,128)(4,1)S(1)} %copy-done.23, ...), kind=kLoop, calls=%fused_computation.886 | loop fusion | flops 3473407 | bytes 2187396 | tf_op jit(solution)/shard_map/reduce_sum | solution.py:157
  441.0 3.2 collective-permute-done.55
  445.2 16.2 %divide_select_fusion = (f32[8,8,512]{2,1,0:T(8,128)S(1)}, f32[8,8,512]{2,1,0:T(8,128)S(1)}, f32[8,8,512]{2,1,0:T(8,128)S(1)}) fusion(f32[9,8,512]{2,1,0:T(8,128)S(1)} %get-tuple-element.54, f32[8,9,512]{2,1,0:T(8,128)S(1)} %get-tuple-element.52, f32[8,8,511]{2,1,0:T(8,128)S(1)} %fusion.137, s32[8,8]{1,0:T(8,128)S(1)} %copy-done.52, ...), kind=kLoop, calls=%fused_computation.354 | loop fusion | flops 3047424 | bytes 2900096 | tf_op jit(solution)/shard_map/jit(_where)/select_n | solution.py:191
  461.4 4.2 collective-permute-start.56
  470.1 3.3 collective-permute-start.58
  479.0 3.4 collective-permute-start.60
  487.0 3.3 collective-permute-start.62
  503.6 3.3 collective-permute-start.64
  511.2 5.1 collective-permute-start.66
  521.4 3.4 collective-permute-start.68
  529.2 3.4 collective-permute-start.70
  545.0 3.4 collective-permute-start.74
  560.3 3.4 collective-permute-start.78
  570.3 35.7 %all-reduce.46 = (f32[32]{0:T(128)S(1)}, f32[32]{0:T(128)S(1)}, f32[32]{0:T(128)S(1)}, f32[32]{0:T(128)S(1)}) all-reduce(f32[32]{0:T(128)S(1)} %dynamic-update-slice.6, f32[32]{0:T(128)S(1)} %dynamic-update-slice.7, f32[32]{0:T(128)S(1)} %dynamic-update-slice.8, f32[32]{0:T(128)S(1)} %dynamic-update-slice.9), channel_id=1, replica_groups=mesh['xy'=8,'gz'=4] {'xy','gz'}, use_global_device_ids=true, to_apply=%add.42 | all-reduce | flops 128 | bytes 1024 | tf_op jit(solution)/shard_map/cond | solution.py:176
  606.0 44.2 %psum.15 = f32[32]{0:T(128)S(1)} all-reduce(f32[32]{0:T(128)S(1)} %broadcast_select_fusion), channel_id=1, replica_groups=mesh['xy'=8,'gz'=4] {'xy','gz'}, use_global_device_ids=true, to_apply=%region_63.66 | all-reduce | flops 32 | bytes 256 | tf_op jit(solution)/shard_map/psum | solution.py:33
  655.3 4.8 collective-permute-done.81
  660.1 6.4 collective-permute-start.82
  671.5 4.5 collective-permute-start.84
  680.4 3.4 collective-permute-start.86
  693.2 3.0 collective-permute-done.89
  696.3 3.4 collective-permute-start.90
  704.7 3.7 collective-permute-start.92
  709.8 3.0 collective-permute-done.93
  712.8 3.4 collective-permute-start.94
  728.7 3.1 collective-permute-done.97
  731.9 3.4 collective-permute-start.98
  737.2 3.3 collective-permute-done.99
  745.2 3.1 collective-permute-done.101
  748.4 3.3 collective-permute-start.102
  753.7 3.3 collective-permute-done.103
  (645 shorter events, 297.6 us)
Async XLA Ops:
  51.3 15.2 %collective-permute-start = (f32[2,8,1,512]{3,1,2,0:T(8,128)S(1)}, f32[2,8,1,512]{3,1,2,0:T(8,128)S(1)}, u32[]{:S(2)}, u32[]{:S(2)}) collective-permute-start(f32[2,8,1,512]{3,1,2,0:T(8,128)S(1)} %copy.1868), channel_id=1, source_target_pairs={{0,4},{4,8},{8,12},{12,16},{16,20},{20,24},{24,28},{1,5},{5,9},{9,... | collective-permute-start | bytes 98312 | tf_op jit(solution)/shard_map/ppermute | solution.py:25
  55.3 11.2 %collective-permute-start.1 = (f32[2,8,1,512]{3,1,2,0:T(8,128)S(1)}, f32[2,8,1,512]{3,1,2,0:T(8,128)S(1)}, u32[]{:S(2)}, u32[]{:S(2)}) collective-permute-start(f32[2,8,1,512]{3,1,2,0:T(8,128)S(1)} %copy.1869), channel_id=1, source_target_pairs={{4,0},{8,4},{12,8},{16,12},{20,16},{24,20},{28,24},{5,1},{9,5},{13... | collective-permute-start | bytes 98312 | tf_op jit(solution)/shard_map/ppermute | solution.py:26
  66.7 6.0 collective-permute-start.2
  70.6 5.6 collective-permute-start.3
  93.0 6.0 collective-permute-start.4
  97.3 5.2 collective-permute-start.5
  102.6 5.3 collective-permute-start.6
  105.6 5.2 collective-permute-start.7
  111.7 10.6 %collective-permute-start.8 = (f32[8,1,512]{2,0,1:T(8,128)}, f32[8,1,512]{2,0,1:T(8,128)}, u32[]{:S(2)}, u32[]{:S(2)}) collective-permute-start(f32[8,1,512]{2,0,1:T(8,128)} %copy.1878), channel_id=1, source_target_pairs={{0,4},{4,8},{8,12},{12,16},{16,20},{20,24},{24,28},{1,5},{5,9},{9,... | collective-permute-start | bytes 49160 | tf_op jit(solution)/shard_map/ppermute | solution.py:25
  117.4 5.7 collective-permute-start.9
  124.5 14.3 %collective-permute-start.10 = (f32[1,10,512]{2,1,0:T(8,128)}, f32[1,10,512]{2,1,0:T(8,128)}, u32[]{:S(2)}, u32[]{:S(2)}) collective-permute-start(f32[1,10,512]{2,1,0:T(8,128)} %get-tuple-element.134), channel_id=1, source_target_pairs={{0,1},{1,2},{2,3},{4,5},{5,6},{6,7},{8,9},{9,10},{10,11},{12,13},{... | collective-permute-start | bytes 61448 | tf_op jit(solution)/shard_map/ppermute | solution.py:25
  126.9 11.8 %collective-permute-start.11 = (f32[1,10,512]{2,1,0:T(8,128)}, f32[1,10,512]{2,1,0:T(8,128)}, u32[]{:S(2)}, u32[]{:S(2)}) collective-permute-start(f32[1,10,512]{2,1,0:T(8,128)} %get-tuple-element.135), channel_id=1, source_target_pairs={{1,0},{2,1},{3,2},{5,4},{6,5},{7,6},{9,8},{10,9},{11,10},{13,12},{... | collective-permute-start | bytes 61448 | tf_op jit(solution)/shard_map/ppermute | solution.py:26
  146.2 5.7 collective-permute-start.12
  154.6 7.4 collective-permute-start.14
  159.2 5.0 collective-permute-start.15
  172.7 6.0 collective-permute-start.18
  176.1 5.1 collective-permute-start.19
  181.8 5.0 collective-permute-start.20
  189.8 6.1 collective-permute-start.22
  198.2 5.5 collective-permute-start.24
  206.1 7.4 collective-permute-start.26
  301.1 6.1 collective-permute-start.29
  307.2 8.4 %collective-permute-start.30 = (f32[1,4,128]{2,1,0:T(4,128)S(1)}, f32[1,4,128]{2,1,0:T(4,128)S(1)}, u32[]{:S(2)}, u32[]{:S(2)}) collective-permute-start(f32[1,4,128]{2,1,0:T(4,128)S(1)} %get-tuple-element.210), channel_id=1, source_target_pairs={{0,1},{1,2},{2,3},{4,5},{5,6},{6,7},{8,9},{9,10},{10,11},{12,13},{... | collective-permute-start | bytes 6152 | tf_op jit(solution)/shard_map/ppermute | solution.py:25
  318.7 5.8 collective-permute-start.32
  327.5 5.5 collective-permute-start.34
  343.4 5.3 collective-permute-start.38
  346.8 5.0 collective-permute-start.39
  352.0 5.0 collective-permute-start.40
  360.1 5.3 collective-permute-start.42
  363.4 5.0 collective-permute-start.43
  380.8 5.4 collective-permute-start.46
  384.4 5.2 collective-permute-start.47
  398.1 5.3 collective-permute-start.50
  401.4 5.2 collective-permute-start.51
  428.0 8.2 %collective-permute-start.52 = (f32[2,8,1,512]{3,1,2,0:T(8,128)S(1)}, f32[2,8,1,512]{3,1,2,0:T(8,128)S(1)}, u32[]{:S(2)}, u32[]{:S(2)}) collective-permute-start(f32[2,8,1,512]{3,1,2,0:T(8,128)S(1)} %copy.1942), channel_id=1, source_target_pairs={{0,4},{4,8},{8,12},{12,16},{16,20},{20,24},{24,28},{1,5},{5,9},{9,... | collective-permute-start | bytes 98312 | tf_op jit(solution)/shard_map/ppermute | solution.py:25
  430.5 5.7 collective-permute-start.53
  438.6 5.6 collective-permute-start.55
  461.4 6.0 collective-permute-start.56
  470.1 5.6 collective-permute-start.58
  473.4 5.2 collective-permute-start.59
  479.0 7.9 %collective-permute-start.60 = (f32[8,1,512]{2,0,1:T(8,128)S(1)}, f32[8,1,512]{2,0,1:T(8,128)S(1)}, u32[]{:S(2)}, u32[]{:S(2)}) collective-permute-start(f32[8,1,512]{2,0,1:T(8,128)S(1)} %copy.1952), channel_id=1, source_target_pairs={{0,4},{4,8},{8,12},{12,16},{16,20},{20,24},{24,28},{1,5},{5,9},{9,... | collective-permute-start | bytes 49160 | tf_op jit(solution)/shard_map/ppermute | solution.py:25
  487.0 12.2 %collective-permute-start.62 = (f32[1,10,512]{2,1,0:T(8,128)S(1)}, f32[1,10,512]{2,1,0:T(8,128)S(1)}, u32[]{:S(2)}, u32[]{:S(2)}) collective-permute-start(f32[1,10,512]{2,1,0:T(8,128)S(1)} %get-tuple-element.124), channel_id=1, source_target_pairs={{0,1},{1,2},{2,3},{4,5},{5,6},{6,7},{8,9},{9,10},{10,11},{12,13},{... | collective-permute-start | bytes 61448 | tf_op jit(solution)/shard_map/ppermute | solution.py:25
  490.3 8.9 %collective-permute-start.63 = (f32[1,10,512]{2,1,0:T(8,128)S(1)}, f32[1,10,512]{2,1,0:T(8,128)S(1)}, u32[]{:S(2)}, u32[]{:S(2)}) collective-permute-start(f32[1,10,512]{2,1,0:T(8,128)S(1)} %get-tuple-element.125), channel_id=1, source_target_pairs={{1,0},{2,1},{3,2},{5,4},{6,5},{7,6},{9,8},{10,9},{11,10},{13,12},{... | collective-permute-start | bytes 61448 | tf_op jit(solution)/shard_map/ppermute | solution.py:26
  503.6 5.0 collective-permute-start.64
  511.2 7.9 %collective-permute-start.66 = (f32[1,6,256]{2,1,0:T(8,128)S(1)}, f32[1,6,256]{2,1,0:T(8,128)S(1)}, u32[]{:S(2)}, u32[]{:S(2)}) collective-permute-start(f32[1,6,256]{2,1,0:T(8,128)S(1)} %get-tuple-element.168), channel_id=1, source_target_pairs={{0,1},{1,2},{2,3},{4,5},{5,6},{6,7},{8,9},{9,10},{10,11},{12,13},{... | collective-permute-start | bytes 18440 | tf_op jit(solution)/shard_map/ppermute | solution.py:25
  516.3 5.0 collective-permute-start.67
  521.4 5.1 collective-permute-start.68
  529.2 5.8 collective-permute-start.70
  532.6 5.0 collective-permute-start.71
  545.0 6.1 collective-permute-start.74
  560.3 7.3 collective-permute-start.78
  654.0 6.1 collective-permute-start.81
  660.1 8.4 %collective-permute-start.82 = (f32[1,4,128]{2,1,0:T(4,128)S(1)}, f32[1,4,128]{2,1,0:T(4,128)S(1)}, u32[]{:S(2)}, u32[]{:S(2)}) collective-permute-start(f32[1,4,128]{2,1,0:T(4,128)S(1)} %get-tuple-element.200), channel_id=1, source_target_pairs={{0,1},{1,2},{2,3},{4,5},{5,6},{6,7},{8,9},{9,10},{10,11},{12,13},{... | collective-permute-start | bytes 6152 | tf_op jit(solution)/shard_map/ppermute | solution.py:25
  671.5 5.8 collective-permute-start.84
  680.4 5.3 collective-permute-start.86
  696.3 5.3 collective-permute-start.90
  699.7 5.0 collective-permute-start.91
  704.7 5.0 collective-permute-start.92
  712.8 5.3 collective-permute-start.94
  716.2 5.0 collective-permute-start.95
  731.9 5.3 collective-permute-start.98
  735.3 5.2 collective-permute-start.99
  748.4 5.3 collective-permute-start.102
  751.7 5.2 collective-permute-start.103
  (123 other events, 3164.3 us)
where the time goes:
time: 772 us; the launch traced here: 758 us
  starting transfers between devices  267 us (35%)
  blocking collectives  162 us (21%)
  waiting for transfers between devices  133 us (17%)
  other arithmetic  126 us (16%)
  local copies, waits for them, and re-layouts  66.3 us (9%)
    ppermute x52, starting transfers between devices, with_halo(): before = lax.ppermute(last, axis, up)  182 us
    ppermute x52, waiting for transfers between devices, with_halo(): after = lax.ppermute(initial, axis, down)  133 us
    psum x2, blocking collectives, from_root(): return lax.psum(kept, axis)  88.3 us
    ppermute x52, starting transfers between devices, with_halo(): after = lax.ppermute(initial, axis, down)  85.2 us
    cond x2, blocking collectives, block_correction(): answer = lax.cond(flat_index == 0, solve_here, nothing_here)  73.5 us
    reduce_sum x2, other arithmetic, block_correction(): jnp.sum(storage).reshape(1)  49.6 us
    select_n x6, other arithmetic, vcycle(): correction = jnp.where(colour == 0, source / diagonal, 0.0)  33.2 us
    unnamed x200, local copies, waits for them, and re-layouts  18.8 us
  transfers between devices with their start and end apart: 104, of which 46 were waited for; matrix products, arithmetic and copies ran while one was open for 7% of the time, Pallas kernels for 0%

commit v1 on v0

v1 whole, which is shorter than its diff:
```python
import functools
import math

import jax
import jax.numpy as jnp
from jax import lax
from jax.experimental import pallas as pl
from jax.experimental.pallas import tpu as pltpu
from jax.sharding import PartitionSpec as P

DT = 20.0
ET_PEAK = 0.008
GRAVITY = 0.1
ROOT_DECAY = 3.0
HI = lax.Precision.HIGHEST


def roll(value, shift, axis):
    return pltpu.roll(value, shift % value.shape[axis], axis)


def spread_pairs(value, low, step, axis):
    return value + jnp.where(low, roll(value, -step, axis), roll(value, step, axis))


def neighbour_sum(e, below, above, fx, fy, fz, fz_up, step):
    total = fx * roll(e, step, 0) + roll(fx * e, -step, 0)
    total = total + (fy * roll(e, step, 1) + roll(fy * e, -step, 1))
    return total + (fz * below + fz_up * above)


def look_up(table, row, index):
    picked = jnp.broadcast_to(table[row : row + 1, :], (8, 128))
    rows = []
    for r in range(0, index.shape[0], 8):
        cols = []
        for c in range(0, index.shape[1], 128):
            at = index[r : r + 8, c : c + 128]
            cols.append(jnp.take_along_axis(picked, at, axis=1, mode="promise_in_bounds"))
        rows.append(jnp.concatenate(cols, axis=1))
    return jnp.concatenate(rows, axis=0)


def down_kernel(first, slabs, strips, zl, xl, *refs):
    where_ref, table_ref = refs[0], refs[1]
    refs = refs[2:]
    state_refs, refs = refs[:9], refs[9:]
    if first:
        head_refs = state_refs
        sat_old_ref = None
    else:
        head_refs, refs = refs[:9], refs[9:]
        sat_old_ref, refs = refs[0], refs[1:]
    payload_ref, refs = refs[0], refs[1:]
    outs0, refs = refs[:6], refs[6:]
    outs1, refs = refs[:5], refs[5:]
    head_out = None
    if first:
        head_out, refs = refs[0], refs[1:]
    head, cond, stor, grow, fx, fy, fz, src, inv, err = refs[:10]
    src1, stor1, fx1, fy1, fz1, inv1, err1, rows2 = refs[10:]

    strip, slab = where_ref[0], where_ref[1]
    zw, xw = 3 * zl, 3 * xl
    ny = head.shape[2]
    shape = (xw, ny)
    xi = lax.broadcasted_iota(jnp.int32, shape, 0)
    yi = lax.broadcasted_iota(jnp.int32, shape, 1)
    parity0 = (xi + yi) & 1
    parity1 = ((xi >> 1) + (yi >> 1)) & 1
    x_low, y_low = (xi & 1) == 0, (yi & 1) == 0
    x_low2, y_low2 = (xi & 2) == 0, (yi & 2) == 0
    edge_x = jnp.logical_or(
        jnp.logical_and(xi == xl, strip == 0), jnp.logical_and(xi == 2 * xl, strip == strips - 1)
    )
    edge_y = yi == 0

    def edge_z(z, width):
        return jnp.logical_or(
            jnp.logical_and(z == width, slab == 0),
            jnp.logical_and(z == 2 * width, slab == slabs - 1),
        )

    forcing = jnp.concatenate([r[2 * zl] for r in state_refs[3:6]], axis=0)
    table = table_ref[...]

    for zb in range(3):

        def soil_step(i, carry, zb=zb):
            z = zb * zl + i
            soil = jnp.concatenate([r[zl + i] for r in state_refs[3 * zb : 3 * zb + 3]], axis=0)
            p = jnp.concatenate([r[i] for r in head_refs[3 * zb : 3 * zb + 3]], axis=0)
            soil = soil.astype(jnp.int32)
            dtheta, alpha, shape_n, k_sat, expon_m = (look_up(table, k, soil) for k in range(5))
            layer = (slab * zl - zl + z).astype(jnp.float32)
            depth = jnp.full((1, ny), layer, jnp.float32)
            sink = forcing * jnp.exp(-ROOT_DECAY * depth / (slabs * zl))
            log_s = jnp.log(jnp.abs(alpha * p))
            log_p = shape_n * log_s
            log_b = jnp.log(1.0 + jnp.exp(log_p))
            root = jnp.exp(-0.5 * expon_m * log_b)
            sat = root * root
            slope = expon_m * shape_n * alpha * sat * jnp.exp((shape_n - 1.0) * log_s - log_b)
            cond[z] = k_sat * root * jnp.square(1.0 - jnp.exp(expon_m * (log_p - log_b)))
            stor[z] = slope * (dtheta / DT + sink)
            g = sink * sat
            if first:
                head_out[z] = sat
            else:
                g = g + dtheta * (sat - sat_old_ref[z]) / DT
            grow[z] = g
            head[z] = p
            return carry

        lax.fori_loop(0, zl, soil_step, 0)

    def face_z(z):
        both = 0.5 * (cond[jnp.maximum(z - 1, 0)] + cond[jnp.minimum(z, zw - 1)])
        closed = jnp.logical_or(edge_z(z, zl), jnp.logical_or(z == 0, z == zw))
        return both * jnp.where(closed, 0.0, 1.0)

    fz[0] = jnp.zeros(shape, jnp.float32)

    def face_step(z, carry):
        c, p = cond[z], head[z]
        across = jnp.where(edge_x, 0.0, 0.5 * (c + roll(c, 1, 0)))
        along = jnp.where(edge_y, 0.0, 0.5 * (c + roll(c, 1, 1)))
        low, high = fz[z], face_z(z + 1)
        flux_x = across * (roll(p, 1, 0) - p)
        flux_y = along * (roll(p, 1, 1) - p)
        p_low, p_high = head[jnp.maximum(z - 1, 0)], head[jnp.minimum(z + 1, zw - 1)]
        flux_low = low * (p_low - p + GRAVITY)
        flux_high = high * (p - p_high + GRAVITY)
        source = (flux_x - roll(flux_x, -1, 0)) + (flux_y - roll(flux_y, -1, 1))
        source = source + (flux_low - flux_high) - grow[z]
        diagonal = stor[z] + (across + roll(across, -1, 0)) + (along + roll(along, -1, 1))
        inverse = 1.0 / (diagonal + (low + high))
        fx[z], fy[z], fz[z + 1] = across, along, high
        src[z], inv[z] = source, inverse
        err[z] = jnp.where(parity0 == (z & 1), source * inverse, 0.0)
        return carry

    lax.fori_loop(0, zw, face_step, 0)

    def sum0(z):
        return neighbour_sum(
            err[z],
            err[jnp.maximum(z - 1, 0)],
            err[jnp.minimum(z + 1, zw - 1)],
            fx[z],
            fy[z],
            fz[z],
            fz[z + 1],
            1,
        )

    def smooth_step(z, carry):
        updated = (src[z] + sum0(z)) * inv[z]
        err[z] = jnp.where(parity0 == (z & 1), err[z], updated)
        return carry

    lax.fori_loop(1, zw - 1, smooth_step, 0)

    def coarse_step(k, carry):
        za, zb = 2 * k, 2 * k + 1
        resid = jnp.where(parity0 == 0, sum0(za), sum0(zb))
        src1[k] = spread_pairs(spread_pairs(resid, x_low, 1, 0), y_low, 1, 1)
        stor1[k] = spread_pairs(spread_pairs(stor[za] + stor[zb], x_low, 1, 0), y_low, 1, 1)
        across = spread_pairs(fx[za] + fx[zb], y_low, 1, 1)
        fx1[k] = jnp.where(x_low, across, roll(across, 1, 0))
        along = spread_pairs(fy[za] + fy[zb], x_low, 1, 0)
        fy1[k] = jnp.where(y_low, along, roll(along, 1, 1))
        fz1[k] = spread_pairs(spread_pairs(fz[za], x_low, 1, 0), y_low, 1, 1)
        return carry

    lax.fori_loop(1, zw // 2 - 1, coarse_step, 0)

    def first1(k, carry):
        across, along = fx1[k], fy1[k]
        diagonal = stor1[k] + (across + roll(across, -2, 0)) + (along + roll(along, -2, 1))
        inverse = 1.0 / (diagonal + (fz1[k] + fz1[k + 1]))
        inv1[k] = inverse
        err1[k] = jnp.where(parity1 == (k & 1), src1[k] * inverse, 0.0)
        return carry

    low1, high1 = zl // 2 - 2, zl + 2
    lax.fori_loop(low1, high1, first1, 0)

    def sum1(k):
        return neighbour_sum(
            err1[k], err1[k - 1], err1[k + 1], fx1[k], fy1[k], fz1[k], fz1[k + 1], 2
        )

    def second1(k, carry):
        updated = (src1[k] + sum1(k)) * inv1[k]
        err1[k] = jnp.where(parity1 == (k & 1), err1[k], updated)
        return carry

    lax.fori_loop(low1 + 1, high1 - 1, second1, 0)

    rows2[...] = jnp.zeros(rows2.shape, jnp.float32)
    own1 = zl // 2
    for k2 in range(zl // 4):
        ka, kb = own1 + 2 * k2, own1 + 2 * k2 + 1
        resid = jnp.where(parity1 == 0, sum1(ka), sum1(kb))
        terms = (
            spread_pairs(spread_pairs(resid, x_low2, 2, 0), y_low2, 2, 1),
            spread_pairs(spread_pairs(stor1[ka] + stor1[kb], x_low2, 2, 0), y_low2, 2, 1),
            spread_pairs(fx1[ka] + fx1[kb], y_low2, 2, 1),
            spread_pairs(fy1[ka] + fy1[kb], x_low2, 2, 0),
            spread_pairs(spread_pairs(fz1[ka], x_low2, 2, 0), y_low2, 2, 1),
        )
        for t, term in enumerate(terms):
            for x2 in range(xl // 4):
                at = (t * (xl // 4) + x2) * (zl // 4) + k2
                x = xl + 4 * x2
                rows2[at : at + 1, :] = term[x : x + 1, :]
    pick_shape = (ny, ny // 4)
    pick = lax.broadcasted_iota(jnp.int32, pick_shape, 0) == 4 * lax.broadcasted_iota(
        jnp.int32, pick_shape, 1
    )
    payload_ref[0 : rows2.shape[0], :] = jnp.dot(
        rows2[...], jnp.where(pick, 1.0, 0.0), precision=HI, preferred_element_type=jnp.float32
    )
    own = slice(xl, 2 * xl)
    here = [err1[own1 + k][own] for k in range(4)]
    xo, yo = x_low[own], y_low[own]
    plane = jnp.where(xo, jnp.where(yo, here[0], here[1]), jnp.where(yo, here[2], here[3]))
    base = rows2.shape[0]
    for c in range(ny // 128):
        payload_ref[base + 8 * c : base + 8 * c + 8, :] = plane[:, 128 * c : 128 * c + 128]

    def keep0(i, carry):
        for out, ref in zip(outs0, (err, src, inv, fx, fy, fz)):
            out[i] = ref[zl - 2 + i]
        return carry

    lax.fori_loop(0, zl + 4, keep0, 0)

    def keep1(i, carry):
        for out, ref in zip(outs1, (src1, inv1, fx1, fy1, fz1)):
            out[i] = ref[zl // 2 - 2 + i]
        return carry

    lax.fori_loop(0, zl // 2 + 5, keep1, 0)


def solve_blocks(rhs, store, across, vertical, scratch, answer):
    count = rhs.shape[0]
    sub = lax.broadcasted_iota(jnp.int32, (8, 128), 0)
    lane = lax.broadcasted_iota(jnp.int32, (8, 128), 1)
    real = (sub & 1) == 0
    same = lane == sub

    def forward(b, before):
        here_x = jnp.where(real, across[b], 0.0)
        next_x = jnp.where(real, across[b + 1], 0.0)
        low = jnp.where(real, vertical[b], 0.0)
        high = roll(low, -2, 0)
        diagonal = jnp.where(real, store[b] + here_x + next_x + low + high, 1.0)
        m = jnp.where(same, diagonal, 0.0)
        m = m - jnp.where(lane == sub - 2, low, 0.0) - jnp.where(lane == sub + 2, high, 0.0)
        m = m - jnp.where(lane == sub + 8, next_x, 0.0)
        m = m + jnp.where(jnp.logical_and(lane == 16, real), rhs[b], 0.0)
        carried = jnp.where(lane < 8, roll(before, -8, 1), jnp.where(lane == 16, before, 0.0))
        m = m + here_x * carried
        for z in range(0, 8, 2):
            row = m[z : z + 1, :]
            row = row / row[:, z : z + 1]
            m = jnp.where(sub == z, row, m - m[:, z : z + 1] * row)
        scratch[b] = m
        return m

    lax.fori_loop(0, count, forward, jnp.zeros((8, 128), jnp.float32))

    def backward(i, above):
        b = count - 1 - i
        m = scratch[b]
        row = jnp.sum(jnp.where(lane == sub + 8, above, 0.0), axis=0, keepdims=True)
        mask = jnp.logical_and(lane >= 8, lane < 16)
        taken = jnp.where(lane == 16, m, 0.0) - jnp.where(mask, m * row, 0.0)
        value = jnp.broadcast_to(jnp.sum(taken, axis=1, keepdims=True), (8, 128))
        answer[b] = jnp.where(real, value, roll(value, 1, 0))
        return value

    lax.fori_loop(0, count, backward, jnp.zeros((8, 128), jnp.float32))


def up_kernel(slabs, strips, zl, xl, counts, *refs):
    where_ref, refs = refs[0], refs[1:]
    pieces, refs = refs[: len(counts)], refs[len(counts) :]
    near, refs = refs[:3], refs[3:]
    e0_in, src0, inv0, fx0, fy0, fz0 = refs[:6]
    src1, inv1, fx1, fy1, fz1 = refs[6:11]
    head_ref, out_ref = refs[11], refs[12]
    a2, block, answer, e2, picked, wide, e1, e0 = refs[13:]
    strip, slab = where_ref[0], where_ref[1]
    x2, z2 = xl // 4, zl // 4
    rows2 = strips * x2
    ny = head_ref.shape[2]

    index = 0
    for ref, count in zip(pieces, counts):
        for j in range(count):
            at = jnp.bitwise_xor(strip, index)
            for g in range(slabs):
                piece = ref[j, jnp.bitwise_xor(slab, g)]
                for t in range(5):
                    for x in range(x2):
                        k = (t * x2 + x) * z2
                        a2[t, at * x2 + x, g * z2 : g * z2 + z2, :] = piece[k : k + z2, :]
            index += 1

    shape = (rows2, 8, 128)
    source, store, fx, fy, fz = (a2[t] for t in range(5))

    def shift_x(v, step):
        if step > 0:
            return jnp.concatenate([jnp.zeros_like(v[:1]), v[:-1]], axis=0)
        return jnp.concatenate([v[1:], jnp.zeros_like(v[:1])], axis=0)

    def along(v, step, axis):
        return pltpu.roll(v, step % v.shape[axis], axis)

    fx_up, fy_up, fz_up = shift_x(fx, -1), along(fy, -1, 2), along(fz, -1, 1)
    inverse = 1.0 / (store + (fx + fx_up) + (fy + fy_up) + (fz + fz_up))
    parity = (
        lax.broadcasted_iota(jnp.int32, shape, 0)
        + lax.broadcasted_iota(jnp.int32, shape, 1)
        + lax.broadcasted_iota(jnp.int32, shape, 2)
    ) & 1
    even = parity == 0

    def sum2(e):
        total = fx * shift_x(e, 1) + fx_up * shift_x(e, -1)
        total = total + (fy * along(e, 1, 2) + fy_up * along(e, -1, 2))
        return total + (fz * along(e, 1, 1) + fz_up * along(e, -1, 1))

    e = jnp.where(even, source * inverse, 0.0)
    e = jnp.where(even, e, (source + sum2(e)) * inverse)
    resid = jnp.where(even, sum2(e), 0.0)

    def blocks(v, both_rows, both_layers):
        v = v.reshape(strips, x2, 8, 128)
        v = v[:, 0] + v[:, 1] if both_rows else v[:, 0]
        v = jnp.sum(v, axis=2, keepdims=True)
        v = jnp.broadcast_to(v, (strips, 8, 128))
        return v + along(v, -1, 1) if both_layers else v

    block[0, 0:strips] = blocks(resid, True, True)
    block[1, 0:strips] = blocks(store, True, True)
    block[2, 0:strips] = blocks(fx, False, True)
    block[2, strips] = jnp.zeros((8, 128), jnp.float32)
    block[3, 0:strips] = blocks(fz, True, False)
    solve_blocks(
        block.at[0, 0:strips], block.at[1], block.at[2], block.at[3], block.at[4], answer
    )
    add = jnp.broadcast_to(answer[...][:, None], (strips, x2, 8, 128)).reshape(shape)
    e = e + add
    e = jnp.where(even, (source + sum2(e)) * inverse, e)
    e = jnp.where(even, e, (source + sum2(e)) * inverse)
    e2[...] = jnp.zeros(e2.shape, jnp.float32)
    e2[x2 : x2 + rows2, 8:16, :] = e

    picked[...] = jnp.zeros(picked.shape, jnp.float32)
    for z in range(3 * z2):
        for x in range(3 * x2):
            at = z * 3 * x2 + x
            picked[at : at + 1, :] = e2[
                strip * x2 + x, pl.ds(8 - z2 + slab * z2 + z, 1), :
            ]
    spread_shape = (ny // 4, ny)
    spread = lax.broadcasted_iota(jnp.int32, spread_shape, 0) == (
        lax.broadcasted_iota(jnp.int32, spread_shape, 1) >> 2
    )
    wide[...] = jnp.dot(
        picked[...], jnp.where(spread, 1.0, 0.0), precision=HI, preferred_element_type=jnp.float32
    )

    zl1 = zl // 2
    small = (xl, ny)
    xo = (lax.broadcasted_iota(jnp.int32, small, 0) & 1) == 0
    yo = (lax.broadcasted_iota(jnp.int32, small, 1) & 1) == 0
    for zb in range(3):
        g = slab + (zb - 1)
        inside = jnp.logical_and(g >= 0, g < slabs)
        m = jnp.bitwise_xor(slab, jnp.clip(g, 0, slabs - 1))
        keep = jnp.where(inside, 1.0, 0.0)
        for xb in range(3):
            tile = near[xb][m]
            plane = jnp.concatenate(
                [tile[8 * c : 8 * c + 8, :] for c in range(ny // 128)], axis=1
            )
            plane = plane * keep
            for k in range(4):
                xk, yk = k // 2, k % 2
                v = jnp.where(jnp.logical_and(xo == (xk == 0), yo == (yk == 0)), plane, 0.0)
                v = v + roll(v, 1 if xk == 0 else -1, 0)
                v = v + roll(v, 1 if yk == 0 else -1, 1)
                for h in range(xl // 4):
                    row = ((zb * zl1 + k) // 2) * 3 * x2 + xb * x2 + h
                    e1[zb * zl1 + k, xb * xl + 4 * h : xb * xl + 4 * h + 4, :] = (
                        v[4 * h : 4 * h + 4, :] + wide[row : row + 1, :]
                    )
    window = (3 * xl, ny)
    xi = lax.broadcasted_iota(jnp.int32, window, 0)
    yi = lax.broadcasted_iota(jnp.int32, window, 1)
    parity0 = (xi + yi) & 1
    parity1 = ((xi >> 1) + (yi >> 1)) & 1

    def level1(k, colour):
        i = k - (zl1 - 2)
        total = neighbour_sum(
            e1[k], e1[k - 1], e1[k + 1], fx1[i], fy1[i], fz1[i], fz1[i + 1], 2
        )
        updated = (src1[i] + total) * inv1[i]
        e1[k] = jnp.where(parity1 == ((k + colour) & 1), updated, e1[k])

    def up1(colour, reach):
        def step(k, carry):
            level1(k, colour)
            return carry

        lax.fori_loop(zl1 - reach, 2 * zl1 + reach, step, 0)

    up1(0, 2)
    up1(1, 1)

    def join(i, carry):
        e0[i] = e0_in[i] + e1[(zl - 2 + i) // 2]
        return carry

    lax.fori_loop(0, zl + 4, join, 0)

    def up0(colour, reach):
        def step(i, carry):
            total = neighbour_sum(
                e0[i], e0[i - 1], e0[i + 1], fx0[i], fy0[i], fz0[i], fz0[i + 1], 1
            )
            updated = (src0[i] + total) * inv0[i]
            e0[i] = jnp.where(parity0 == ((i + colour) & 1), updated, e0[i])
            return carry

        lax.fori_loop(2 - reach, zl + 2 + reach, step, 0)

    up0(0, 1)
    up0(1, 0)
    for z in range(zl):
        out_ref[z] = head_ref[z] + e0[z + 2][xl : 2 * xl]


VMEM = pl.BlockSpec(memory_space=pltpu.VMEM)
SMEM = pl.BlockSpec(memory_space=pltpu.SMEM)


def f32(*shape):
    return jax.ShapeDtypeStruct(shape, jnp.float32)


def down(first, slabs, strips, zl, xl, ny, where, table, state, head=None, sat_old=None):
    zw, xw = 3 * zl, 3 * xl
    rows2 = 5 * (xl // 4) * (zl // 4)
    rows2 = -(-rows2 // 8) * 8
    out_shape = [f32(rows2 + 8 * ny // 128, 128)]
    out_shape += [f32(zl + 4, xw, ny)] * 6 + [f32(zl // 2 + 5, xw, ny)] * 5
    operands = [where, table, *state]
    if first:
        out_shape.append(f32(zw, xw, ny))
    else:
        operands += [*head, sat_old]
    full, half = pltpu.VMEM((zw, xw, ny), jnp.float32), pltpu.VMEM((zw // 2, xw, ny), jnp.float32)
    tall = pltpu.VMEM((zw + 1, xw, ny), jnp.float32)
    return pl.pallas_call(
        functools.partial(down_kernel, first, slabs, strips, zl, xl),
        out_shape=out_shape,
        in_specs=[SMEM] + [VMEM] * (len(operands) - 1),
        out_specs=[VMEM] * len(out_shape),
        scratch_shapes=[full] * 6 + [tall] + [full] * 3 + [half] * 7
        + [pltpu.VMEM((rows2, ny), jnp.float32)],
        compiler_params=pltpu.CompilerParams(vmem_limit_bytes=44 * 1024 * 1024),
    )(*operands)


def up(slabs, strips, zl, xl, ny, where, pieces, near, kept, head):
    x2, z2 = xl // 4, zl // 4
    counts = [p.shape[0] for p in pieces]
    operands = [where, *pieces, *near, *kept, head]
    n = -(-9 * x2 * z2 // 8) * 8
    scratch = [
        pltpu.VMEM((5, strips * x2, 8, 128), jnp.float32),
        pltpu.VMEM((5, strips + 1, 8, 128), jnp.float32),
        pltpu.VMEM((strips, 8, 128), jnp.float32),
        pltpu.VMEM(((strips + 2) * x2, 24, 128), jnp.float32),
        pltpu.VMEM((n, ny // 4), jnp.float32),
        pltpu.VMEM((n, ny), jnp.float32),
        pltpu.VMEM((3 * zl // 2, 3 * xl, ny), jnp.float32),
        pltpu.VMEM((zl + 4, 3 * xl, ny), jnp.float32),
    ]
    return pl.pallas_call(
        functools.partial(up_kernel, slabs, strips, zl, xl, counts),
        out_shape=f32(zl, xl, ny),
        in_specs=[SMEM] + [VMEM] * (len(operands) - 1),
        out_specs=VMEM,
        scratch_shapes=scratch,
        compiler_params=pltpu.CompilerParams(vmem_limit_bytes=44 * 1024 * 1024),
    )(*operands)


def shifted(x, axis, step):
    size = lax.axis_size(axis)
    pairs = [(i, i + step) for i in range(size) if 0 <= i + step < size]
    return lax.ppermute(x, axis, pairs)


def swapped(x, axis, mask):
    return lax.ppermute(x, axis, [(i, i ^ mask) for i in range(lax.axis_size(axis))])


def neighbourhood(x):
    row = [shifted(x, "xy", 1), x, shifted(x, "xy", -1)]
    return (
        [shifted(v, "gz", 1) for v in row] + row + [shifted(v, "gz", -1) for v in row]
    )


def gather_strips(x):
    size = lax.axis_size("xy")
    x = x[None]
    if size == 8:
        pair = jnp.concatenate([x, swapped(x, "xy", 1)])
        return [pair] + [swapped(pair, "xy", m) for m in (2, 4, 6)]
    mask = 1
    while mask < size:
        x = jnp.concatenate([x, swapped(x, "xy", mask)])
        mask *= 2
    return [x]


def per_device(head_old, soil_type, soil_table, land_mask, sun_bin):
    zl, xl, ny = head_old.shape
    strips, slabs = lax.axis_size("xy"), lax.axis_size("gz")
    where = jnp.stack([lax.axis_index("xy"), lax.axis_index("gz")]).astype(jnp.int32)
    resid, sat, alpha, shape_n, k_sat = soil_table
    table = jnp.stack([sat - resid, alpha, shape_n, k_sat, 1.0 - 1.0 / shape_n])
    table = jnp.pad(table, ((0, 3), (0, 128 - table.shape[1])))
    sun_share = jnp.maximum(0.0, jnp.sin(math.pi * (sun_bin.astype(jnp.float32) - 6.0) / 12.0))
    forcing = ET_PEAK * sun_share * land_mask.astype(jnp.float32)
    own = jnp.concatenate([head_old, soil_type.astype(jnp.float32), forcing[None]])
    state = neighbourhood(own)
    sizes = (slabs, strips, zl, xl, ny)
    base = -(-5 * (xl // 4) * (zl // 4) // 8) * 8

    def finish(payload, kept, head):
        slab = [payload] + [swapped(payload, "gz", m) for m in range(1, slabs)]
        equations = jnp.stack([p[:base] for p in slab])
        corrections = jnp.stack([p[base:] for p in slab])
        pieces = gather_strips(equations)
        near = [shifted(corrections, "xy", 1), corrections, shifted(corrections, "xy", -1)]
        return up(*sizes, where, pieces, near, kept, head)

    payload, *kept, sat_old = down(True, *sizes, where, table, state)
    head = finish(payload, kept, head_old)
    payload, *kept = down(False, *sizes, where, table, state, neighbourhood(head), sat_old)
    return finish(payload, kept, head)


def solution(mesh):
    in_specs = (P("gz", "xy", None), P("gz", "xy", None), P(), P("xy", None), P("xy", None))
    out_specs = P("gz", "xy", None)
    return jax.shard_map(
        per_device, mesh=mesh, in_specs=in_specs, out_specs=out_specs, check_vma=False
    )
```

time: 772 us -> 161 us (0.21)
  the two profiles are of different devices: /device:TPU:1 before, /device:TPU:0 now
where the time goes in v1:
time: 161 us; the launch traced here: 160 us
  starting transfers between devices  82.6 us (51%)
  Pallas kernels  55.9 us (35%)
  waiting for transfers between devices  16.4 us (10%)
  other arithmetic  3.58 us (2%)
    ppermute x20, starting transfers between devices, shifted(): return lax.ppermute(x, axis, pairs)  53 us
    pallas_call x2, Pallas kernels, down(): pl.pallas_call(functools.partial(down_kernel, first, slabs, strips, zl, x...  37.1 us
    ppermute x14, starting transfers between devices, swapped(): lax.ppermute(x, axis, [(i, i ^ mask) for i in range(lax.axis_size(axis))])  29.6 us
    pallas_call x2, Pallas kernels, up(): pl.pallas_call(functools.partial(up_kernel, slabs, strips, zl, xl, counts...  18.8 us
    ppermute x14, waiting for transfers between devices, swapped(): lax.ppermute(x, axis, [(i, i ^ mask) for i in range(lax.axis_size(axis))])  10.3 us
    ppermute x20, waiting for transfers between devices, shifted(): return lax.ppermute(x, axis, pairs)  6.07 us
  transfers between devices with their start and end apart: 34, of which 13 were waited for; matrix products, arithmetic and copies ran while one was open for 1% of the time, Pallas kernels for 0%

profile of v1, /device:TPU:0, one launch (start us, length us, event | category | flops | bytes accessed | tf_op | source)
XLA Modules:
  0.0 159.6 jit_solution(17892166794676205382)
XLA Ops:
  0.0 0.9 convert_element_type.11
  0.9 0.8 multiply_bitcast_fusion
  1.7 0.9 pad_maximum_fusion.refs_6_
  2.7 1.3 collective-permute-start.3
  4.0 5.5 %collective-permute-start = (f32[17,8,512]{2,1,0:T(8,128)S(1)}, f32[17,8,512]{2,1,0:T(8,128)S(1)}, u32[]{:S(2)}, u32[]{:S(2)}) collective-permute-start(f32[17,8,512]{2,1,0:T(8,128)S(1)} %pad_maximum_fusion.refs_6_), channel_id=1, source_target_pairs={{0,4},{4,8},{8,12},{12,16},{16,20},{20,24},{24,28},{1,5},{5,9},{9,... | collective-permute-start | bytes 835592 | tf_op jit(solution)/shard_map/ppermute | solution.py:512
  9.5 1.3 collective-permute-start.6
  10.8 3.0 %collective-permute-start.2 = (f32[17,8,512]{2,1,0:T(8,128)S(1)}, f32[17,8,512]{2,1,0:T(8,128)S(1)}, u32[]{:S(2)}, u32[]{:S(2)}) collective-permute-start(f32[17,8,512]{2,1,0:T(8,128)S(1)} %pad_maximum_fusion.refs_6_), channel_id=1, source_target_pairs={{0,1},{1,2},{2,3},{4,5},{5,6},{6,7},{8,9},{9,10},{10,11},{12,13},{... | collective-permute-start | bytes 835592 | tf_op jit(solution)/shard_map/ppermute | solution.py:512
  13.8 0.3 collective-permute-done.3.refs_7_
  14.2 1.3 collective-permute-start.7
  15.5 3.8 %collective-permute-start.4 = (f32[17,8,512]{2,1,0:T(8,128)S(1)}, f32[17,8,512]{2,1,0:T(8,128)S(1)}, u32[]{:S(2)}, u32[]{:S(2)}) collective-permute-start(f32[17,8,512]{2,1,0:T(8,128)S(1)} %collective-permute-done.3.refs_7_), channel_id=1, source_target_pairs={{0,1},{1,2},{2,3},{4,5},{5,6},{6,7},{8,9},{9,10},{10,11},{12,13},{... | collective-permute-start | bytes 835592 | tf_op jit(solution)/shard_map/ppermute | solution.py:512
  19.3 1.0 collective-permute-done.refs_5_
  20.3 1.3 collective-permute-start.5
  21.6 3.3 %collective-permute-start.1 = (f32[17,8,512]{2,1,0:T(8,128)S(1)}, f32[17,8,512]{2,1,0:T(8,128)S(1)}, u32[]{:S(2)}, u32[]{:S(2)}) collective-permute-start(f32[17,8,512]{2,1,0:T(8,128)S(1)} %collective-permute-done.refs_5_), channel_id=1, source_target_pairs={{0,1},{1,2},{2,3},{4,5},{5,6},{6,7},{8,9},{9,10},{10,11},{12,13},{... | collective-permute-start | bytes 835592 | tf_op jit(solution)/shard_map/ppermute | solution.py:512
  24.9 0.8 slice_subtract_fusion
  25.7 0.7 unstack.18
  26.4 0.1 pad_add_fusion.refs_0_
  26.5 0.0 copy-start.1
  26.5 0.0 collective-permute-done.7.refs_10_
  26.5 0.0 collective-permute-done.4.refs_4_
  26.5 0.0 collective-permute-done.1.refs_2_
  26.5 18.2 %shard_map.55 = (f32[56,128]{1,0:T(8,128)S(1)}, f32[12,24,512]{2,1,0:T(8,128)S(1)}, f32[12,24,512]{2,1,0:T(8,128)S(1)}, f32[12,24,512]{2,1,0:T(8,128)S(1)}, f32[...) custom-call(s32[2]{0:T(128)S(1)} %pad_add_fusion.refs_0_, ...), custom_call_target="tpu_custom_call" | custom-call | tf_op jit(solution)/shard_map/pallas_call | solution.py:473
  44.7 1.2 collective-permute-start.10
  45.9 4.9 %collective-permute-start.9 = (f32[56,128]{1,0:T(8,128)S(1)}, f32[56,128]{1,0:T(8,128)S(1)}, u32[]{:S(2)}, u32[]{:S(2)}) collective-permute-start(f32[56,128]{1,0:T(8,128)S(1)} %get-tuple-element.30), channel_id=1, source_target_pairs={{0,2},{1,3},{2,0},{3,1},{4,6},{5,7},{6,4},{7,5},{8,10},{9,11},{10,... | collective-permute-start | bytes 86024 | tf_op jit(solution)/shard_map/ppermute | solution.py:516
  50.8 0.0 collective-permute-start.8
  50.8 2.0 %collective-permute-done.9 = f32[56,128]{1,0:T(8,128)S(1)} collective-permute-done((f32[56,128]{1,0:T(8,128)S(1)}, f32[56,128]{1,0:T(8,128)S(1)}, u32[]{:S(2)}, u32[]{:S(2)}) %collective-permute-start.9) | collective-permute-done | bytes 28704 | tf_op jit(solution)/shard_map/ppermute | solution.py:516
  52.9 0.0 collective-permute-done.8
  52.9 2.5 %collective-permute-start.11 = (f32[1,4,24,128]{3,2,1,0:T(8,128)S(1)}, f32[1,4,24,128]{3,2,1,0:T(8,128)S(1)}, u32[]{:S(2)}, u32[]{:S(2)}) collective-permute-start(f32[1,4,24,128]{3,2,1,0:T(8,128)S(1)} %maximum_bitcast_fusion), channel_id=1, source_target_pairs={{0,4},{4,0},{8,12},{12,8},{16,20},{20,16},{24,28},{28,24},{1,5},{5... | collective-permute-start | bytes 147464 | tf_op jit(solution)/shard_map/ppermute | solution.py:516
  55.4 2.6 %collective-permute-done.11 = f32[1,4,24,128]{3,2,1,0:T(8,128)S(1)} collective-permute-done((f32[1,4,24,128]{3,2,1,0:T(8,128)S(1)}, f32[1,4,24,128]{3,2,1,0:T(8,128)S(1)}, u32[]{:S(2)}, u32[]{:S(2)}) %collective-permute-start.11) | collective-permute-done | bytes 49184 | tf_op jit(solution)/shard_map/ppermute | solution.py:516
  58.0 7.8 %collective-permute-start.14 = (f32[2,4,24,128]{3,2,1,0:T(8,128)S(1)}, f32[2,4,24,128]{3,2,1,0:T(8,128)S(1)}, u32[]{:S(2)}, u32[]{:S(2)}) collective-permute-start(f32[2,4,24,128]{3,2,1,0:T(8,128)S(1)} %pad_maximum_fusion.1.refs_1_), channel_id=1, source_target_pairs={{0,24},{4,28},{8,16},{12,20},{16,8},{20,12},{24,0},{28,4},{1,25},{... | collective-permute-start | bytes 294920 | tf_op jit(solution)/shard_map/ppermute | solution.py:516
  65.7 0.0 collective-permute-start.13
  65.7 0.6 collective-permute-start.12
  66.4 1.3 collective-permute-start.16
  67.7 4.5 %collective-permute-start.15 = (f32[4,32,128]{2,1,0:T(8,128)S(1)}, f32[4,32,128]{2,1,0:T(8,128)S(1)}, u32[]{:S(2)}, u32[]{:S(2)}) collective-permute-start(f32[4,32,128]{2,1,0:T(8,128)S(1)} %pad_maximum_fusion.3.refs_6_), channel_id=1, source_target_pairs={{0,4},{4,8},{8,12},{12,16},{16,20},{20,24},{24,28},{1,5},{5,9},{9,... | collective-permute-start | bytes 196616 | tf_op jit(solution)/shard_map/ppermute | solution.py:512
  72.2 0.3 collective-permute-done.16.refs_7_
  72.5 1.6 collective-permute-done.15.refs_5_
  74.1 0.0 collective-permute-done.14.refs_4_
  74.1 0.6 collective-permute-done.13.refs_3_
  74.7 9.1 %shard_map.56.refs_15_.refs_19_ = f32[8,8,512]{2,1,0:T(8,128)S(1)} custom-call(s32[2]{0:T(128)S(1)} %pad_add_fusion.refs_0_, f32[2,4,24,128]{3,2,1,0:T(8,128)S(1)} %pad_maximum_fusion.1.refs_1_, f32[2,4,24,128]{3,2,1,0:T(8,128)S(1)} %collective-permute-done.12.refs_2_, f32[2,4,24,128]{3,2,1,0:T(8,128)S(1)} %collective-permute-done.13.refs_3_, ...), custom_call_target="tpu_custom_call" | custom-call | tf_op jit(solution)/shard_map/pallas_call | solution.py:499
  83.8 1.3 collective-permute-start.20
  85.1 4.6 %collective-permute-start.17 = (f32[8,8,512]{2,1,0:T(8,128)S(1)}, f32[8,8,512]{2,1,0:T(8,128)S(1)}, u32[]{:S(2)}, u32[]{:S(2)}) collective-permute-start(f32[8,8,512]{2,1,0:T(8,128)S(1)} %shard_map.56.refs_15_.refs_19_), channel_id=1, source_target_pairs={{0,4},{4,8},{8,12},{12,16},{16,20},{20,24},{24,28},{1,5},{5,9},{9,... | collective-permute-start | bytes 393224 | tf_op jit(solution)/shard_map/ppermute | solution.py:512
  89.6 1.3 collective-permute-start.23
  90.9 3.0 %collective-permute-start.19 = (f32[8,8,512]{2,1,0:T(8,128)S(1)}, f32[8,8,512]{2,1,0:T(8,128)S(1)}, u32[]{:S(2)}, u32[]{:S(2)}) collective-permute-start(f32[8,8,512]{2,1,0:T(8,128)S(1)} %shard_map.56.refs_15_.refs_19_), channel_id=1, source_target_pairs={{0,1},{1,2},{2,3},{4,5},{5,6},{6,7},{8,9},{9,10},{10,11},{12,13},{... | collective-permute-start | bytes 393224 | tf_op jit(solution)/shard_map/ppermute | solution.py:512
  94.0 0.0 collective-permute-done.20.refs_16_
  94.0 1.3 collective-permute-start.24
  95.3 3.5 %collective-permute-start.21 = (f32[8,8,512]{2,1,0:T(8,128)S(1)}, f32[8,8,512]{2,1,0:T(8,128)S(1)}, u32[]{:S(2)}, u32[]{:S(2)}) collective-permute-start(f32[8,8,512]{2,1,0:T(8,128)S(1)} %collective-permute-done.20.refs_16_), channel_id=1, source_target_pairs={{0,1},{1,2},{2,3},{4,5},{5,6},{6,7},{8,9},{9,10},{10,11},{12,13},{... | collective-permute-start | bytes 393224 | tf_op jit(solution)/shard_map/ppermute | solution.py:512
  98.8 0.0 collective-permute-done.17.refs_14_
  98.8 1.3 collective-permute-start.22
  100.1 4.3 %collective-permute-start.18 = (f32[8,8,512]{2,1,0:T(8,128)S(1)}, f32[8,8,512]{2,1,0:T(8,128)S(1)}, u32[]{:S(2)}, u32[]{:S(2)}) collective-permute-start(f32[8,8,512]{2,1,0:T(8,128)S(1)} %collective-permute-done.17.refs_14_), channel_id=1, source_target_pairs={{0,1},{1,2},{2,3},{4,5},{5,6},{6,7},{8,9},{9,10},{10,11},{12,13},{... | collective-permute-start | bytes 393224 | tf_op jit(solution)/shard_map/ppermute | solution.py:512
  104.5 0.9 collective-permute-done.18.refs_11_
  105.4 18.9 %shard_map.57 = (f32[56,128]{1,0:T(8,128)S(1)}, f32[12,24,512]{2,1,0:T(8,128)S(1)}, f32[12,24,512]{2,1,0:T(8,128)S(1)}, f32[12,24,512]{2,1,0:T(8,128)S(1)}, f32[...) custom-call(s32[2]{0:T(128)S(1)} %pad_add_fusion.refs_0_, ...), custom_call_target="tpu_custom_call" | custom-call | tf_op jit(solution)/shard_map/pallas_call | solution.py:473
  124.3 1.7 %collective-permute-start.27 = (f32[56,128]{1,0:T(8,128)S(1)}, f32[56,128]{1,0:T(8,128)S(1)}, u32[]{:S(2)}, u32[]{:S(2)}) collective-permute-start(f32[56,128]{1,0:T(8,128)S(1)} %get-tuple-element.43), channel_id=1, source_target_pairs={{0,3},{1,2},{2,1},{3,0},{4,7},{5,6},{6,5},{7,4},{8,11},{9,10},{10,... | collective-permute-start | bytes 86024 | tf_op jit(solution)/shard_map/ppermute | solution.py:516
  126.0 3.5 %collective-permute-start.26 = (f32[56,128]{1,0:T(8,128)S(1)}, f32[56,128]{1,0:T(8,128)S(1)}, u32[]{:S(2)}, u32[]{:S(2)}) collective-permute-start(f32[56,128]{1,0:T(8,128)S(1)} %get-tuple-element.43), channel_id=1, source_target_pairs={{0,2},{1,3},{2,0},{3,1},{4,6},{5,7},{6,4},{7,5},{8,10},{9,11},{10,... | collective-permute-start | bytes 86024 | tf_op jit(solution)/shard_map/ppermute | solution.py:516
  129.5 0.0 collective-permute-start.25
  129.6 2.0 %collective-permute-done.26 = f32[56,128]{1,0:T(8,128)S(1)} collective-permute-done((f32[56,128]{1,0:T(8,128)S(1)}, f32[56,128]{1,0:T(8,128)S(1)}, u32[]{:S(2)}, u32[]{:S(2)}) %collective-permute-start.26) | collective-permute-done | bytes 28704 | tf_op jit(solution)/shard_map/ppermute | solution.py:516
  131.6 3.0 %collective-permute-start.28 = (f32[1,4,24,128]{3,2,1,0:T(8,128)S(1)}, f32[1,4,24,128]{3,2,1,0:T(8,128)S(1)}, u32[]{:S(2)}, u32[]{:S(2)}) collective-permute-start(f32[1,4,24,128]{3,2,1,0:T(8,128)S(1)} %maximum_bitcast_fusion.1), channel_id=1, source_target_pairs={{0,4},{4,0},{8,12},{12,8},{16,20},{20,16},{24,28},{28,24},{1,5},{5... | collective-permute-start | bytes 147464 | tf_op jit(solution)/shard_map/ppermute | solution.py:516
  134.6 2.6 %collective-permute-done.28 = f32[1,4,24,128]{3,2,1,0:T(8,128)S(1)} collective-permute-done((f32[1,4,24,128]{3,2,1,0:T(8,128)S(1)}, f32[1,4,24,128]{3,2,1,0:T(8,128)S(1)}, u32[]{:S(2)}, u32[]{:S(2)}) %collective-permute-start.28) | collective-permute-done | bytes 49184 | tf_op jit(solution)/shard_map/ppermute | solution.py:516
  137.2 3.5 %collective-permute-start.31 = (f32[2,4,24,128]{3,2,1,0:T(8,128)S(1)}, f32[2,4,24,128]{3,2,1,0:T(8,128)S(1)}, u32[]{:S(2)}, u32[]{:S(2)}) collective-permute-start(f32[2,4,24,128]{3,2,1,0:T(8,128)S(1)} %pad_maximum_fusion.2.refs_1_), channel_id=1, source_target_pairs={{0,24},{4,28},{8,16},{12,20},{16,8},{20,12},{24,0},{28,4},{1,25},{... | collective-permute-start | bytes 294920 | tf_op jit(solution)/shard_map/ppermute | solution.py:516
  140.7 0.9 collective-permute-start.29
  141.7 1.3 collective-permute-start.33
  142.9 4.5 %collective-permute-start.32 = (f32[4,32,128]{2,1,0:T(8,128)S(1)}, f32[4,32,128]{2,1,0:T(8,128)S(1)}, u32[]{:S(2)}, u32[]{:S(2)}) collective-permute-start(f32[4,32,128]{2,1,0:T(8,128)S(1)} %pad_maximum_fusion.4.refs_6_), channel_id=1, source_target_pairs={{0,4},{4,8},{8,12},{12,16},{16,20},{20,24},{24,28},{1,5},{5,9},{9,... | collective-permute-start | bytes 196616 | tf_op jit(solution)/shard_map/ppermute | solution.py:512
  147.5 0.3 collective-permute-done.33.refs_7_
  147.8 1.6 collective-permute-done.32.refs_5_
  149.4 0.5 collective-permute-done.30.refs_3_
  149.9 9.7 %shard_map.58 = f32[8,8,512]{2,1,0:T(8,128)} custom-call(s32[2]{0:T(128)S(1)} %pad_add_fusion.refs_0_, f32[2,4,24,128]{3,2,1,0:T(8,128)S(1)} %pad_maximum_fusion.2.refs_1_, f32[2,4,24,128]{3,2,1,0:T(8,128)S(1)} %collective-permute-done.29.refs_2_, f32[2,4,24,128]{3,2,1,0:T(8,128)S(1)} %collective-permute-done.30.refs_3_, ...), custom_call_target="tpu_custom_call" | custom-call | tf_op jit(solution)/shard_map/pallas_call | solution.py:499
  (41 shorter events, 0.1 us)
Async XLA Ops:
  2.7 11.5 %collective-permute-start.3 = (f32[17,8,512]{2,1,0:T(8,128)S(1)}, f32[17,8,512]{2,1,0:T(8,128)S(1)}, u32[]{:S(2)}, u32[]{:S(2)}) collective-permute-start(f32[17,8,512]{2,1,0:T(8,128)S(1)} %pad_maximum_fusion.refs_6_), channel_id=1, source_target_pairs={{4,0},{8,4},{12,8},{16,12},{20,16},{24,20},{28,24},{5,1},{9,5},{13... | collective-permute-start | bytes 835592 | tf_op jit(solution)/shard_map/ppermute | solution.py:512
  4.0 16.3 %collective-permute-start = (f32[17,8,512]{2,1,0:T(8,128)S(1)}, f32[17,8,512]{2,1,0:T(8,128)S(1)}, u32[]{:S(2)}, u32[]{:S(2)}) collective-permute-start(f32[17,8,512]{2,1,0:T(8,128)S(1)} %pad_maximum_fusion.refs_6_), channel_id=1, source_target_pairs={{0,4},{4,8},{8,12},{12,16},{16,20},{20,24},{24,28},{1,5},{5,9},{9,... | collective-permute-start | bytes 835592 | tf_op jit(solution)/shard_map/ppermute | solution.py:512
  9.5 12.1 %collective-permute-start.6 = (f32[17,8,512]{2,1,0:T(8,128)S(1)}, f32[17,8,512]{2,1,0:T(8,128)S(1)}, u32[]{:S(2)}, u32[]{:S(2)}) collective-permute-start(f32[17,8,512]{2,1,0:T(8,128)S(1)} %pad_maximum_fusion.refs_6_), channel_id=1, source_target_pairs={{1,0},{2,1},{3,2},{5,4},{6,5},{7,6},{9,8},{10,9},{11,10},{13,12},{... | collective-permute-start | bytes 835592 | tf_op jit(solution)/shard_map/ppermute | solution.py:512
  10.8 15.7 %collective-permute-start.2 = (f32[17,8,512]{2,1,0:T(8,128)S(1)}, f32[17,8,512]{2,1,0:T(8,128)S(1)}, u32[]{:S(2)}, u32[]{:S(2)}) collective-permute-start(f32[17,8,512]{2,1,0:T(8,128)S(1)} %pad_maximum_fusion.refs_6_), channel_id=1, source_target_pairs={{0,1},{1,2},{2,3},{4,5},{5,6},{6,7},{8,9},{9,10},{10,11},{12,13},{... | collective-permute-start | bytes 835592 | tf_op jit(solution)/shard_map/ppermute | solution.py:512
  14.2 12.3 %collective-permute-start.7 = (f32[17,8,512]{2,1,0:T(8,128)S(1)}, f32[17,8,512]{2,1,0:T(8,128)S(1)}, u32[]{:S(2)}, u32[]{:S(2)}) collective-permute-start(f32[17,8,512]{2,1,0:T(8,128)S(1)} %collective-permute-done.3.refs_7_), channel_id=1, source_target_pairs={{1,0},{2,1},{3,2},{5,4},{6,5},{7,6},{9,8},{10,9},{11,10},{13,12},{... | collective-permute-start | bytes 835592 | tf_op jit(solution)/shard_map/ppermute | solution.py:512
  15.5 11.0 %collective-permute-start.4 = (f32[17,8,512]{2,1,0:T(8,128)S(1)}, f32[17,8,512]{2,1,0:T(8,128)S(1)}, u32[]{:S(2)}, u32[]{:S(2)}) collective-permute-start(f32[17,8,512]{2,1,0:T(8,128)S(1)} %collective-permute-done.3.refs_7_), channel_id=1, source_target_pairs={{0,1},{1,2},{2,3},{4,5},{5,6},{6,7},{8,9},{9,10},{10,11},{12,13},{... | collective-permute-start | bytes 835592 | tf_op jit(solution)/shard_map/ppermute | solution.py:512
  20.3 6.2 %collective-permute-start.5 = (f32[17,8,512]{2,1,0:T(8,128)S(1)}, f32[17,8,512]{2,1,0:T(8,128)S(1)}, u32[]{:S(2)}, u32[]{:S(2)}) collective-permute-start(f32[17,8,512]{2,1,0:T(8,128)S(1)} %collective-permute-done.refs_5_), channel_id=1, source_target_pairs={{1,0},{2,1},{3,2},{5,4},{6,5},{7,6},{9,8},{10,9},{11,10},{13,12},{... | collective-permute-start | bytes 835592 | tf_op jit(solution)/shard_map/ppermute | solution.py:512
  21.6 4.9 %collective-permute-start.1 = (f32[17,8,512]{2,1,0:T(8,128)S(1)}, f32[17,8,512]{2,1,0:T(8,128)S(1)}, u32[]{:S(2)}, u32[]{:S(2)}) collective-permute-start(f32[17,8,512]{2,1,0:T(8,128)S(1)} %collective-permute-done.refs_5_), channel_id=1, source_target_pairs={{0,1},{1,2},{2,3},{4,5},{5,6},{6,7},{8,9},{9,10},{10,11},{12,13},{... | collective-permute-start | bytes 835592 | tf_op jit(solution)/shard_map/ppermute | solution.py:512
  26.5 48.2 %copy-start.1 = (f32[8,8,512]{2,1,0:T(8,128)S(1)}, f32[8,8,512]{2,1,0:T(8,128)}, u32[]{:S(2)}) copy-start(f32[8,8,512]{2,1,0:T(8,128)} %refs_19_.1) | copy-start | bytes 393220
  44.7 39.1 %copy-start = (f32[24,24,512]{2,1,0:T(8,128)}, f32[24,24,512]{2,1,0:T(8,128)S(1)}, u32[]{:S(2)}) copy-start(f32[24,24,512]{2,1,0:T(8,128)S(1)} %get-tuple-element.42.refs_20_) | copy-start | bytes 3538948
  44.7 6.1 %collective-permute-start.10 = (f32[56,128]{1,0:T(8,128)S(1)}, f32[56,128]{1,0:T(8,128)S(1)}, u32[]{:S(2)}, u32[]{:S(2)}) collective-permute-start(f32[56,128]{1,0:T(8,128)S(1)} %get-tuple-element.30), channel_id=1, source_target_pairs={{0,3},{1,2},{2,1},{3,0},{4,7},{5,6},{6,5},{7,4},{8,11},{9,10},{10,... | collective-permute-start | bytes 86024 | tf_op jit(solution)/shard_map/ppermute | solution.py:516
  45.9 7.0 %collective-permute-start.9 = (f32[56,128]{1,0:T(8,128)S(1)}, f32[56,128]{1,0:T(8,128)S(1)}, u32[]{:S(2)}, u32[]{:S(2)}) collective-permute-start(f32[56,128]{1,0:T(8,128)S(1)} %get-tuple-element.30), channel_id=1, source_target_pairs={{0,2},{1,3},{2,0},{3,1},{4,6},{5,7},{6,4},{7,5},{8,10},{9,11},{10,... | collective-permute-start | bytes 86024 | tf_op jit(solution)/shard_map/ppermute | solution.py:516
  50.8 2.1 %collective-permute-start.8 = (f32[56,128]{1,0:T(8,128)S(1)}, f32[56,128]{1,0:T(8,128)S(1)}, u32[]{:S(2)}, u32[]{:S(2)}) collective-permute-start(f32[56,128]{1,0:T(8,128)S(1)} %get-tuple-element.30), channel_id=1, source_target_pairs={{0,1},{1,0},{2,3},{3,2},{4,5},{5,4},{6,7},{7,6},{8,9},{9,8},{10,11... | collective-permute-start | bytes 86024 | tf_op jit(solution)/shard_map/ppermute | solution.py:516
  52.9 5.1 %collective-permute-start.11 = (f32[1,4,24,128]{3,2,1,0:T(8,128)S(1)}, f32[1,4,24,128]{3,2,1,0:T(8,128)S(1)}, u32[]{:S(2)}, u32[]{:S(2)}) collective-permute-start(f32[1,4,24,128]{3,2,1,0:T(8,128)S(1)} %maximum_bitcast_fusion), channel_id=1, source_target_pairs={{0,4},{4,0},{8,12},{12,8},{16,20},{20,16},{24,28},{28,24},{1,5},{5... | collective-permute-start | bytes 147464 | tf_op jit(solution)/shard_map/ppermute | solution.py:516
  58.0 16.2 %collective-permute-start.14 = (f32[2,4,24,128]{3,2,1,0:T(8,128)S(1)}, f32[2,4,24,128]{3,2,1,0:T(8,128)S(1)}, u32[]{:S(2)}, u32[]{:S(2)}) collective-permute-start(f32[2,4,24,128]{3,2,1,0:T(8,128)S(1)} %pad_maximum_fusion.1.refs_1_), channel_id=1, source_target_pairs={{0,24},{4,28},{8,16},{12,20},{16,8},{20,12},{24,0},{28,4},{1,25},{... | collective-permute-start | bytes 294920 | tf_op jit(solution)/shard_map/ppermute | solution.py:516
  65.7 9.0 %collective-permute-start.13 = (f32[2,4,24,128]{3,2,1,0:T(8,128)S(1)}, f32[2,4,24,128]{3,2,1,0:T(8,128)S(1)}, u32[]{:S(2)}, u32[]{:S(2)}) collective-permute-start(f32[2,4,24,128]{3,2,1,0:T(8,128)S(1)} %pad_maximum_fusion.1.refs_1_), channel_id=1, source_target_pairs={{0,16},{4,20},{8,24},{12,28},{16,0},{20,4},{24,8},{28,12},{1,17},{... | collective-permute-start | bytes 294920 | tf_op jit(solution)/shard_map/ppermute | solution.py:516
  65.7 9.0 %collective-permute-start.12 = (f32[2,4,24,128]{3,2,1,0:T(8,128)S(1)}, f32[2,4,24,128]{3,2,1,0:T(8,128)S(1)}, u32[]{:S(2)}, u32[]{:S(2)}) collective-permute-start(f32[2,4,24,128]{3,2,1,0:T(8,128)S(1)} %pad_maximum_fusion.1.refs_1_), channel_id=1, source_target_pairs={{0,8},{4,12},{8,0},{12,4},{16,24},{20,28},{24,16},{28,20},{1,9},{5... | collective-permute-start | bytes 294920 | tf_op jit(solution)/shard_map/ppermute | solution.py:516
  66.4 6.1 %collective-permute-start.16 = (f32[4,32,128]{2,1,0:T(8,128)S(1)}, f32[4,32,128]{2,1,0:T(8,128)S(1)}, u32[]{:S(2)}, u32[]{:S(2)}) collective-permute-start(f32[4,32,128]{2,1,0:T(8,128)S(1)} %pad_maximum_fusion.3.refs_6_), channel_id=1, source_target_pairs={{4,0},{8,4},{12,8},{16,12},{20,16},{24,20},{28,24},{5,1},{9,5},{13... | collective-permute-start | bytes 196616 | tf_op jit(solution)/shard_map/ppermute | solution.py:512
  67.7 6.4 %collective-permute-start.15 = (f32[4,32,128]{2,1,0:T(8,128)S(1)}, f32[4,32,128]{2,1,0:T(8,128)S(1)}, u32[]{:S(2)}, u32[]{:S(2)}) collective-permute-start(f32[4,32,128]{2,1,0:T(8,128)S(1)} %pad_maximum_fusion.3.refs_6_), channel_id=1, source_target_pairs={{0,4},{4,8},{8,12},{12,16},{16,20},{20,24},{24,28},{1,5},{5,9},{9,... | collective-permute-start | bytes 196616 | tf_op jit(solution)/shard_map/ppermute | solution.py:512
  83.8 10.2 %collective-permute-start.20 = (f32[8,8,512]{2,1,0:T(8,128)S(1)}, f32[8,8,512]{2,1,0:T(8,128)S(1)}, u32[]{:S(2)}, u32[]{:S(2)}) collective-permute-start(f32[8,8,512]{2,1,0:T(8,128)S(1)} %shard_map.56.refs_15_.refs_19_), channel_id=1, source_target_pairs={{4,0},{8,4},{12,8},{16,12},{20,16},{24,20},{28,24},{5,1},{9,5},{13... | collective-permute-start | bytes 393224 | tf_op jit(solution)/shard_map/ppermute | solution.py:512
  85.1 13.7 %collective-permute-start.17 = (f32[8,8,512]{2,1,0:T(8,128)S(1)}, f32[8,8,512]{2,1,0:T(8,128)S(1)}, u32[]{:S(2)}, u32[]{:S(2)}) collective-permute-start(f32[8,8,512]{2,1,0:T(8,128)S(1)} %shard_map.56.refs_15_.refs_19_), channel_id=1, source_target_pairs={{0,4},{4,8},{8,12},{12,16},{16,20},{20,24},{24,28},{1,5},{5,9},{9,... | collective-permute-start | bytes 393224 | tf_op jit(solution)/shard_map/ppermute | solution.py:512
  89.6 10.5 %collective-permute-start.23 = (f32[8,8,512]{2,1,0:T(8,128)S(1)}, f32[8,8,512]{2,1,0:T(8,128)S(1)}, u32[]{:S(2)}, u32[]{:S(2)}) collective-permute-start(f32[8,8,512]{2,1,0:T(8,128)S(1)} %shard_map.56.refs_15_.refs_19_), channel_id=1, source_target_pairs={{1,0},{2,1},{3,2},{5,4},{6,5},{7,6},{9,8},{10,9},{11,10},{13,12},{... | collective-permute-start | bytes 393224 | tf_op jit(solution)/shard_map/ppermute | solution.py:512
  90.9 13.5 %collective-permute-start.19 = (f32[8,8,512]{2,1,0:T(8,128)S(1)}, f32[8,8,512]{2,1,0:T(8,128)S(1)}, u32[]{:S(2)}, u32[]{:S(2)}) collective-permute-start(f32[8,8,512]{2,1,0:T(8,128)S(1)} %shard_map.56.refs_15_.refs_19_), channel_id=1, source_target_pairs={{0,1},{1,2},{2,3},{4,5},{5,6},{6,7},{8,9},{9,10},{10,11},{12,13},{... | collective-permute-start | bytes 393224 | tf_op jit(solution)/shard_map/ppermute | solution.py:512
  94.0 10.4 %collective-permute-start.24 = (f32[8,8,512]{2,1,0:T(8,128)S(1)}, f32[8,8,512]{2,1,0:T(8,128)S(1)}, u32[]{:S(2)}, u32[]{:S(2)}) collective-permute-start(f32[8,8,512]{2,1,0:T(8,128)S(1)} %collective-permute-done.20.refs_16_), channel_id=1, source_target_pairs={{1,0},{2,1},{3,2},{5,4},{6,5},{7,6},{9,8},{10,9},{11,10},{13,12},{... | collective-permute-start | bytes 393224 | tf_op jit(solution)/shard_map/ppermute | solution.py:512
  95.3 9.1 %collective-permute-start.21 = (f32[8,8,512]{2,1,0:T(8,128)S(1)}, f32[8,8,512]{2,1,0:T(8,128)S(1)}, u32[]{:S(2)}, u32[]{:S(2)}) collective-permute-start(f32[8,8,512]{2,1,0:T(8,128)S(1)} %collective-permute-done.20.refs_16_), channel_id=1, source_target_pairs={{0,1},{1,2},{2,3},{4,5},{5,6},{6,7},{8,9},{9,10},{10,11},{12,13},{... | collective-permute-start | bytes 393224 | tf_op jit(solution)/shard_map/ppermute | solution.py:512
  98.8 5.6 %collective-permute-start.22 = (f32[8,8,512]{2,1,0:T(8,128)S(1)}, f32[8,8,512]{2,1,0:T(8,128)S(1)}, u32[]{:S(2)}, u32[]{:S(2)}) collective-permute-start(f32[8,8,512]{2,1,0:T(8,128)S(1)} %collective-permute-done.17.refs_14_), channel_id=1, source_target_pairs={{1,0},{2,1},{3,2},{5,4},{6,5},{7,6},{9,8},{10,9},{11,10},{13,12},{... | collective-permute-start | bytes 393224 | tf_op jit(solution)/shard_map/ppermute | solution.py:512
  100.1 5.2 %collective-permute-start.18 = (f32[8,8,512]{2,1,0:T(8,128)S(1)}, f32[8,8,512]{2,1,0:T(8,128)S(1)}, u32[]{:S(2)}, u32[]{:S(2)}) collective-permute-start(f32[8,8,512]{2,1,0:T(8,128)S(1)} %collective-permute-done.17.refs_14_), channel_id=1, source_target_pairs={{0,1},{1,2},{2,3},{4,5},{5,6},{6,7},{8,9},{9,10},{10,11},{12,13},{... | collective-permute-start | bytes 393224 | tf_op jit(solution)/shard_map/ppermute | solution.py:512
  124.3 5.2 %collective-permute-start.27 = (f32[56,128]{1,0:T(8,128)S(1)}, f32[56,128]{1,0:T(8,128)S(1)}, u32[]{:S(2)}, u32[]{:S(2)}) collective-permute-start(f32[56,128]{1,0:T(8,128)S(1)} %get-tuple-element.43), channel_id=1, source_target_pairs={{0,3},{1,2},{2,1},{3,0},{4,7},{5,6},{6,5},{7,4},{8,11},{9,10},{10,... | collective-permute-start | bytes 86024 | tf_op jit(solution)/shard_map/ppermute | solution.py:516
  126.0 5.6 %collective-permute-start.26 = (f32[56,128]{1,0:T(8,128)S(1)}, f32[56,128]{1,0:T(8,128)S(1)}, u32[]{:S(2)}, u32[]{:S(2)}) collective-permute-start(f32[56,128]{1,0:T(8,128)S(1)} %get-tuple-element.43), channel_id=1, source_target_pairs={{0,2},{1,3},{2,0},{3,1},{4,6},{5,7},{6,4},{7,5},{8,10},{9,11},{10,... | collective-permute-start | bytes 86024 | tf_op jit(solution)/shard_map/ppermute | solution.py:516
  129.5 2.1 %collective-permute-start.25 = (f32[56,128]{1,0:T(8,128)S(1)}, f32[56,128]{1,0:T(8,128)S(1)}, u32[]{:S(2)}, u32[]{:S(2)}) collective-permute-start(f32[56,128]{1,0:T(8,128)S(1)} %get-tuple-element.43), channel_id=1, source_target_pairs={{0,1},{1,0},{2,3},{3,2},{4,5},{5,4},{6,7},{7,6},{8,9},{9,8},{10,11... | collective-permute-start | bytes 86024 | tf_op jit(solution)/shard_map/ppermute | solution.py:516
  131.6 5.6 %collective-permute-start.28 = (f32[1,4,24,128]{3,2,1,0:T(8,128)S(1)}, f32[1,4,24,128]{3,2,1,0:T(8,128)S(1)}, u32[]{:S(2)}, u32[]{:S(2)}) collective-permute-start(f32[1,4,24,128]{3,2,1,0:T(8,128)S(1)} %maximum_bitcast_fusion.1), channel_id=1, source_target_pairs={{0,4},{4,0},{8,12},{12,8},{16,20},{20,16},{24,28},{28,24},{1,5},{5... | collective-permute-start | bytes 147464 | tf_op jit(solution)/shard_map/ppermute | solution.py:516
  137.2 12.2 %collective-permute-start.31 = (f32[2,4,24,128]{3,2,1,0:T(8,128)S(1)}, f32[2,4,24,128]{3,2,1,0:T(8,128)S(1)}, u32[]{:S(2)}, u32[]{:S(2)}) collective-permute-start(f32[2,4,24,128]{3,2,1,0:T(8,128)S(1)} %pad_maximum_fusion.2.refs_1_), channel_id=1, source_target_pairs={{0,24},{4,28},{8,16},{12,20},{16,8},{20,12},{24,0},{28,4},{1,25},{... | collective-permute-start | bytes 294920 | tf_op jit(solution)/shard_map/ppermute | solution.py:516
  140.7 9.1 %collective-permute-start.30 = (f32[2,4,24,128]{3,2,1,0:T(8,128)S(1)}, f32[2,4,24,128]{3,2,1,0:T(8,128)S(1)}, u32[]{:S(2)}, u32[]{:S(2)}) collective-permute-start(f32[2,4,24,128]{3,2,1,0:T(8,128)S(1)} %pad_maximum_fusion.2.refs_1_), channel_id=1, source_target_pairs={{0,16},{4,20},{8,24},{12,28},{16,0},{20,4},{24,8},{28,12},{1,17},{... | collective-permute-start | bytes 294920 | tf_op jit(solution)/shard_map/ppermute | solution.py:516
  140.7 9.1 %collective-permute-start.29 = (f32[2,4,24,128]{3,2,1,0:T(8,128)S(1)}, f32[2,4,24,128]{3,2,1,0:T(8,128)S(1)}, u32[]{:S(2)}, u32[]{:S(2)}) collective-permute-start(f32[2,4,24,128]{3,2,1,0:T(8,128)S(1)} %pad_maximum_fusion.2.refs_1_), channel_id=1, source_target_pairs={{0,8},{4,12},{8,0},{12,4},{16,24},{20,28},{24,16},{28,20},{1,9},{5... | collective-permute-start | bytes 294920 | tf_op jit(solution)/shard_map/ppermute | solution.py:516
  141.7 6.1 %collective-permute-start.33 = (f32[4,32,128]{2,1,0:T(8,128)S(1)}, f32[4,32,128]{2,1,0:T(8,128)S(1)}, u32[]{:S(2)}, u32[]{:S(2)}) collective-permute-start(f32[4,32,128]{2,1,0:T(8,128)S(1)} %pad_maximum_fusion.4.refs_6_), channel_id=1, source_target_pairs={{4,0},{8,4},{12,8},{16,12},{20,16},{24,20},{28,24},{5,1},{9,5},{13... | collective-permute-start | bytes 196616 | tf_op jit(solution)/shard_map/ppermute | solution.py:512
  142.9 6.4 %collective-permute-start.32 = (f32[4,32,128]{2,1,0:T(8,128)S(1)}, f32[4,32,128]{2,1,0:T(8,128)S(1)}, u32[]{:S(2)}, u32[]{:S(2)}) collective-permute-start(f32[4,32,128]{2,1,0:T(8,128)S(1)} %pad_maximum_fusion.4.refs_6_), channel_id=1, source_target_pairs={{0,4},{4,8},{8,12},{12,16},{16,20},{20,24},{24,28},{1,5},{5,9},{9,... | collective-permute-start | bytes 196616 | tf_op jit(solution)/shard_map/ppermute | solution.py:512

commit v2 on v1

--- a/solution.py
+++ b/solution.py
@@ -17,6 +17,13 @@
 
 def roll(value, shift, axis):
     return pltpu.roll(value, shift % value.shape[axis], axis)
+
+
+def place(which, index):
+    if which == 0:
+        return 1
+    odd = index & 1
+    return 2 - 2 * odd if which == 1 else 2 * odd
 
 
 def spread_pairs(value, low, step, axis):
@@ -47,23 +54,25 @@
     state_refs, refs = refs[:9], refs[9:]
     if first:
         head_refs = state_refs
-        sat_old_ref = None
     else:
         head_refs, refs = refs[:9], refs[9:]
         sat_old_ref, refs = refs[0], refs[1:]
     payload_ref, refs = refs[0], refs[1:]
     outs0, refs = refs[:6], refs[6:]
     outs1, refs = refs[:5], refs[5:]
-    head_out = None
     if first:
-        head_out, refs = refs[0], refs[1:]
+        sat_out, refs = refs[0], refs[1:]
     head, cond, stor, grow, fx, fy, fz, src, inv, err = refs[:10]
     src1, stor1, fx1, fy1, fz1, inv1, err1, rows2 = refs[10:]
 
     strip, slab = where_ref[0], where_ref[1]
     zw, xw = 3 * zl, 3 * xl
-    ny = head.shape[2]
+    ny = head.shape[3]
     shape = (xw, ny)
+
+    def slab_of(ref, z):
+        return ref[z].reshape(shape)
+
     xi = lax.broadcasted_iota(jnp.int32, shape, 0)
     yi = lax.broadcasted_iota(jnp.int32, shape, 1)
     parity0 = (xi + yi) & 1
@@ -81,16 +90,15 @@
             jnp.logical_and(z == 2 * width, slab == slabs - 1),
         )
 
-    forcing = jnp.concatenate([r[2 * zl] for r in state_refs[3:6]], axis=0)
     table = table_ref[...]
-
-    for zb in range(3):
-
-        def soil_step(i, carry, zb=zb):
-            z = zb * zl + i
-            soil = jnp.concatenate([r[zl + i] for r in state_refs[3 * zb : 3 * zb + 3]], axis=0)
-            p = jnp.concatenate([r[i] for r in head_refs[3 * zb : 3 * zb + 3]], axis=0)
-            soil = soil.astype(jnp.int32)
+    for block in range(9):
+        z_at, x_at = place(block // 3, slab), place(block % 3, strip)
+
+        def soil_step(i, carry, block=block, z_at=z_at, x_at=x_at):
+            z = z_at * zl + i
+            soil = state_refs[block][zl + i].astype(jnp.int32)
+            p = head_refs[block][i]
+            forcing = state_refs[block % 3][2 * zl]
             dtheta, alpha, shape_n, k_sat, expon_m = (look_up(table, k, soil) for k in range(5))
             layer = (slab * zl - zl + z).astype(jnp.float32)
             depth = jnp.full((1, ny), layer, jnp.float32)
@@ -101,39 +109,40 @@
             root = jnp.exp(-0.5 * expon_m * log_b)
             sat = root * root
             slope = expon_m * shape_n * alpha * sat * jnp.exp((shape_n - 1.0) * log_s - log_b)
-            cond[z] = k_sat * root * jnp.square(1.0 - jnp.exp(expon_m * (log_p - log_b)))
-            stor[z] = slope * (dtheta / DT + sink)
+            cond[z, x_at] = k_sat * root * jnp.square(1.0 - jnp.exp(expon_m * (log_p - log_b)))
+            stor[z, x_at] = slope * (dtheta / DT + sink)
             g = sink * sat
             if first:
-                head_out[z] = sat
+                sat_out[z, x_at] = sat
             else:
-                g = g + dtheta * (sat - sat_old_ref[z]) / DT
-            grow[z] = g
-            head[z] = p
+                g = g + dtheta * (sat - sat_old_ref[z, x_at]) / DT
+            grow[z, x_at] = g
+            head[z, x_at] = p
             return carry
 
         lax.fori_loop(0, zl, soil_step, 0)
 
     def face_z(z):
-        both = 0.5 * (cond[jnp.maximum(z - 1, 0)] + cond[jnp.minimum(z, zw - 1)])
+        both = 0.5 * (slab_of(cond, jnp.maximum(z - 1, 0)) + slab_of(cond, jnp.minimum(z, zw - 1)))
         closed = jnp.logical_or(edge_z(z, zl), jnp.logical_or(z == 0, z == zw))
         return both * jnp.where(closed, 0.0, 1.0)
 
     fz[0] = jnp.zeros(shape, jnp.float32)
 
     def face_step(z, carry):
-        c, p = cond[z], head[z]
+        c, p = slab_of(cond, z), slab_of(head, z)
         across = jnp.where(edge_x, 0.0, 0.5 * (c + roll(c, 1, 0)))
         along = jnp.where(edge_y, 0.0, 0.5 * (c + roll(c, 1, 1)))
         low, high = fz[z], face_z(z + 1)
         flux_x = across * (roll(p, 1, 0) - p)
         flux_y = along * (roll(p, 1, 1) - p)
-        p_low, p_high = head[jnp.maximum(z - 1, 0)], head[jnp.minimum(z + 1, zw - 1)]
+        p_low = slab_of(head, jnp.maximum(z - 1, 0))
+        p_high = slab_of(head, jnp.minimum(z + 1, zw - 1))
         flux_low = low * (p_low - p + GRAVITY)
         flux_high = high * (p - p_high + GRAVITY)
         source = (flux_x - roll(flux_x, -1, 0)) + (flux_y - roll(flux_y, -1, 1))
-        source = source + (flux_low - flux_high) - grow[z]
-        diagonal = stor[z] + (across + roll(across, -1, 0)) + (along + roll(along, -1, 1))
+        source = source + (flux_low - flux_high) - slab_of(grow, z)
+        diagonal = slab_of(stor, z) + (across + roll(across, -1, 0)) + (along + roll(along, -1, 1))
         inverse = 1.0 / (diagonal + (low + high))
         fx[z], fy[z], fz[z + 1] = across, along, high
         src[z], inv[z] = source, inverse
@@ -165,7 +174,9 @@
         za, zb = 2 * k, 2 * k + 1
         resid = jnp.where(parity0 == 0, sum0(za), sum0(zb))
         src1[k] = spread_pairs(spread_pairs(resid, x_low, 1, 0), y_low, 1, 1)
-        stor1[k] = spread_pairs(spread_pairs(stor[za] + stor[zb], x_low, 1, 0), y_low, 1, 1)
+        stor1[k] = spread_pairs(
+            spread_pairs(slab_of(stor, za) + slab_of(stor, zb), x_low, 1, 0), y_low, 1, 1
+        )
         across = spread_pairs(fx[za] + fx[zb], y_low, 1, 1)
         fx1[k] = jnp.where(x_low, across, roll(across, 1, 0))
         along = spread_pairs(fy[za] + fy[zb], x_low, 1, 0)
@@ -386,8 +397,9 @@
         inside = jnp.logical_and(g >= 0, g < slabs)
         m = jnp.bitwise_xor(slab, jnp.clip(g, 0, slabs - 1))
         keep = jnp.where(inside, 1.0, 0.0)
-        for xb in range(3):
-            tile = near[xb][m]
+        for which in range(3):
+            xb = place(which, strip)
+            tile = near[which][m]
             plane = jnp.concatenate(
                 [tile[8 * c : 8 * c + 8, :] for c in range(ny // 128)], axis=1
             )
@@ -397,12 +409,17 @@
                 v = jnp.where(jnp.logical_and(xo == (xk == 0), yo == (yk == 0)), plane, 0.0)
                 v = v + roll(v, 1 if xk == 0 else -1, 0)
                 v = v + roll(v, 1 if yk == 0 else -1, 1)
-                for h in range(xl // 4):
-                    row = ((zb * zl1 + k) // 2) * 3 * x2 + xb * x2 + h
-                    e1[zb * zl1 + k, xb * xl + 4 * h : xb * xl + 4 * h + 4, :] = (
-                        v[4 * h : 4 * h + 4, :] + wide[row : row + 1, :]
-                    )
+                e1[zb * zl1 + k, xb] = v
     window = (3 * xl, ny)
+    for k in range(3 * zl1):
+        rows = [wide[k // 2 * 3 * x2 + x : k // 2 * 3 * x2 + x + 1, :] for x in range(3 * x2)]
+        rows = [jnp.broadcast_to(row, (4, ny)) for row in rows]
+        rows = [jnp.concatenate(rows[x2 * b : x2 * b + x2], axis=0)[None] for b in range(3)]
+        e1[k] = e1[k] + jnp.concatenate(rows, axis=0)
+
+    def at1(k):
+        return e1[k].reshape(window)
+
     xi = lax.broadcasted_iota(jnp.int32, window, 0)
     yi = lax.broadcasted_iota(jnp.int32, window, 1)
     parity0 = (xi + yi) & 1
@@ -411,10 +428,10 @@
     def level1(k, colour):
         i = k - (zl1 - 2)
         total = neighbour_sum(
-            e1[k], e1[k - 1], e1[k + 1], fx1[i], fy1[i], fz1[i], fz1[i + 1], 2
+            at1(k), at1(k - 1), at1(k + 1), fx1[i], fy1[i], fz1[i], fz1[i + 1], 2
         )
         updated = (src1[i] + total) * inv1[i]
-        e1[k] = jnp.where(parity1 == ((k + colour) & 1), updated, e1[k])
+        e1[k] = jnp.where(parity1 == ((k + colour) & 1), updated, at1(k)).reshape(3, xl, ny)
 
     def up1(colour, reach):
         def step(k, carry):
@@ -427,7 +444,7 @@
     up1(1, 1)
 
     def join(i, carry):
-        e0[i] = e0_in[i] + e1[(zl - 2 + i) // 2]
+        e0[i] = e0_in[i] + at1((zl - 2 + i) // 2)
         return carry
 
     lax.fori_loop(0, zl + 4, join, 0)
@@ -465,9 +482,10 @@
     out_shape += [f32(zl + 4, xw, ny)] * 6 + [f32(zl // 2 + 5, xw, ny)] * 5
     operands = [where, table, *state]
     if first:
-        out_shape.append(f32(zw, xw, ny))
+        out_shape.append(f32(zw, 3, xl, ny))
     else:
         operands += [*head, sat_old]
+    split = pltpu.VMEM((zw, 3, xl, ny), jnp.float32)
     full, half = pltpu.VMEM((zw, xw, ny), jnp.float32), pltpu.VMEM((zw // 2, xw, ny), jnp.float32)
     tall = pltpu.VMEM((zw + 1, xw, ny), jnp.float32)
     return pl.pallas_call(
@@ -475,7 +493,7 @@
         out_shape=out_shape,
         in_specs=[SMEM] + [VMEM] * (len(operands) - 1),
         out_specs=[VMEM] * len(out_shape),
-        scratch_shapes=[full] * 6 + [tall] + [full] * 3 + [half] * 7
+        scratch_shapes=[split] * 4 + [full] * 2 + [tall] + [full] * 3 + [half] * 7
         + [pltpu.VMEM((rows2, ny), jnp.float32)],
         compiler_params=pltpu.CompilerParams(vmem_limit_bytes=44 * 1024 * 1024),
     )(*operands)
@@ -493,7 +511,7 @@
         pltpu.VMEM(((strips + 2) * x2, 24, 128), jnp.float32),
         pltpu.VMEM((n, ny // 4), jnp.float32),
         pltpu.VMEM((n, ny), jnp.float32),
-        pltpu.VMEM((3 * zl // 2, 3 * xl, ny), jnp.float32),
+        pltpu.VMEM((3 * zl // 2, 3, xl, ny), jnp.float32),
         pltpu.VMEM((zl + 4, 3 * xl, ny), jnp.float32),
     ]
     return pl.pallas_call(
@@ -506,30 +524,27 @@
     )(*operands)
 
 
-def shifted(x, axis, step):
-    size = lax.axis_size(axis)
-    pairs = [(i, i + step) for i in range(size) if 0 <= i + step < size]
-    return lax.ppermute(x, axis, pairs)
-
-
 def swapped(x, axis, mask):
     return lax.ppermute(x, axis, [(i, i ^ mask) for i in range(lax.axis_size(axis))])
 
 
+def odd_pairs(x, axis):
+    size = lax.axis_size(axis)
+    pairs = [(i, i + 1) for i in range(1, size - 1, 2)]
+    return lax.ppermute(x, axis, pairs + [(j, i) for i, j in pairs])
+
+
 def neighbourhood(x):
-    row = [shifted(x, "xy", 1), x, shifted(x, "xy", -1)]
-    return (
-        [shifted(v, "gz", 1) for v in row] + row + [shifted(v, "gz", -1) for v in row]
-    )
-
-
-def gather_strips(x):
+    row = [x, swapped(x, "xy", 1), odd_pairs(x, "xy")]
+    return row + [swapped(v, "gz", 1) for v in row] + [odd_pairs(v, "gz") for v in row]
+
+
+def gather_strips(own, partner):
     size = lax.axis_size("xy")
-    x = x[None]
+    x = jnp.stack([own, partner])
     if size == 8:
-        pair = jnp.concatenate([x, swapped(x, "xy", 1)])
-        return [pair] + [swapped(pair, "xy", m) for m in (2, 4, 6)]
-    mask = 1
+        return [x] + [swapped(x, "xy", m) for m in (2, 4, 6)]
+    mask = 2
     while mask < size:
         x = jnp.concatenate([x, swapped(x, "xy", mask)])
         mask *= 2
@@ -552,10 +567,10 @@
 
     def finish(payload, kept, head):
         slab = [payload] + [swapped(payload, "gz", m) for m in range(1, slabs)]
-        equations = jnp.stack([p[:base] for p in slab])
-        corrections = jnp.stack([p[base:] for p in slab])
-        pieces = gather_strips(equations)
-        near = [shifted(corrections, "xy", 1), corrections, shifted(corrections, "xy", -1)]
+        full = jnp.stack(slab)
+        partner = swapped(full, "xy", 1)
+        pieces = gather_strips(full[:, :base], partner[:, :base])
+        near = [full[:, base:], partner[:, base:], odd_pairs(full[:, base:], "xy")]
         return up(*sizes, where, pieces, near, kept, head)
 
     payload, *kept, sat_old = down(True, *sizes, where, table, state)

time: 161 us -> 151 us (0.938)
  starting transfers between devices: 82.6 us -> 51.7 us
  waiting for transfers between devices: 16.4 us -> 32.4 us
  Pallas kernels: 55.9 us -> 62.1 us
    ppermute x20 -> x10, starting transfers between devices: 53 us -> 6.63 us  [odd_pairs(): return lax.ppermute(x, axis, pairs + [(j, i) for i, j in pairs])]
    ppermute x14 -> x22, waiting for transfers between devices: 10.3 us -> 32.3 us  [swapped(): lax.ppermute(x, axis, [(i, i ^ mask) for i in range(lax.axis_size(axis))])]
    ppermute x14 -> x22, starting transfers between devices: 29.6 us -> 45 us  [swapped(): lax.ppermute(x, axis, [(i, i ^ mask) for i in range(lax.axis_size(axis))])]
    pallas_call x2, Pallas kernels: 37.1 us -> 43.5 us  [down(): pl.pallas_call(functools.partial(down_kernel, first, slabs, strips, zl, x...]
    ppermute x20 -> x10, waiting for transfers between devices: 6.07 us -> 0.03 us  [odd_pairs(): return lax.ppermute(x, axis, pairs + [(j, i) for i, j in pairs])]
  transfers between devices with their start and end apart: 34 -> 32, of which waited for: 13 -> 10; matrix products, arithmetic and copies ran while one was open for 1% -> 1% of each run, Pallas kernels for 0% -> 0%
where the time goes in v2:
time: 151 us
  Pallas kernels  62.1 us (41%)
  starting transfers between devices  51.7 us (34%)
  waiting for transfers between devices  32.4 us (21%)
  other arithmetic  3.58 us (2%)
    ppermute x22, starting transfers between devices, swapped(): lax.ppermute(x, axis, [(i, i ^ mask) for i in range(lax.axis_size(axis))])  45 us
    pallas_call x2, Pallas kernels, down(): pl.pallas_call(functools.partial(down_kernel, first, slabs, strips, zl, x...  43.5 us
    ppermute x22, waiting for transfers between devices, swapped(): lax.ppermute(x, axis, [(i, i ^ mask) for i in range(lax.axis_size(axis))])  32.3 us
    pallas_call x2, Pallas kernels, up(): pl.pallas_call(functools.partial(up_kernel, slabs, strips, zl, xl, counts...  18.6 us
    ppermute x10, starting transfers between devices, odd_pairs(): return lax.ppermute(x, axis, pairs + [(j, i) for i, j in pairs])  6.63 us
  transfers between devices with their start and end apart: 32, of which 10 were waited for; matrix products, arithmetic and copies ran while one was open for 1% of the time, Pallas kernels for 0%

profile of v2, /device:TPU:0, one launch (start us, length us, event | category | flops | bytes accessed | tf_op | source)
XLA Modules:
  0.0 150.8 jit_solution(2955796987969011089)
XLA Ops:
  0.0 0.9 convert_element_type.11
  0.9 0.8 multiply_bitcast_fusion
  1.7 0.9 pad_maximum_fusion.refs_2_
  2.7 0.7 collective-permute-start.1
  3.3 5.8 %collective-permute-start = (f32[17,8,512]{2,1,0:T(8,128)S(1)}, f32[17,8,512]{2,1,0:T(8,128)S(1)}, u32[]{:S(2)}, u32[]{:S(2)}) collective-permute-start(f32[17,8,512]{2,1,0:T(8,128)S(1)} %pad_maximum_fusion.refs_2_), channel_id=1, source_target_pairs={{0,4},{4,0},{8,12},{12,8},{16,20},{20,16},{24,28},{28,24},{1,5},{5... | collective-permute-start | bytes 835592 | tf_op jit(solution)/shard_map/ppermute | solution.py:528
  9.1 0.7 collective-permute-start.5
  9.8 2.9 %collective-permute-start.2 = (f32[17,8,512]{2,1,0:T(8,128)S(1)}, f32[17,8,512]{2,1,0:T(8,128)S(1)}, u32[]{:S(2)}, u32[]{:S(2)}) collective-permute-start(f32[17,8,512]{2,1,0:T(8,128)S(1)} %pad_maximum_fusion.refs_2_), channel_id=1, source_target_pairs={{0,1},{1,0},{2,3},{3,2},{4,5},{5,4},{6,7},{7,6},{8,9},{9,8},{10,11... | collective-permute-start | bytes 835592 | tf_op jit(solution)/shard_map/ppermute | solution.py:528
  12.7 0.0 collective-permute-done.1.refs_4_
  12.7 0.7 collective-permute-start.7
  13.4 1.3 collective-permute-start.4
  14.7 5.6 %collective-permute-done.refs_3_ = f32[17,8,512]{2,1,0:T(8,128)S(1)} collective-permute-done((f32[17,8,512]{2,1,0:T(8,128)S(1)}, f32[17,8,512]{2,1,0:T(8,128)S(1)}, u32[]{:S(2)}, u32[]{:S(2)}) %collective-permute-start) | collective-permute-done | bytes 278560 | tf_op jit(solution)/shard_map/ppermute | solution.py:528
  20.3 0.7 collective-permute-start.6
  21.0 0.0 collective-permute-done.5.refs_8_
  21.0 2.9 %collective-permute-start.3 = (f32[17,8,512]{2,1,0:T(8,128)S(1)}, f32[17,8,512]{2,1,0:T(8,128)S(1)}, u32[]{:S(2)}, u32[]{:S(2)}) collective-permute-start(f32[17,8,512]{2,1,0:T(8,128)S(1)} %collective-permute-done.refs_3_), channel_id=1, source_target_pairs={{0,1},{1,0},{2,3},{3,2},{4,5},{5,4},{6,7},{7,6},{8,9},{9,8},{10,11... | collective-permute-start | bytes 835592 | tf_op jit(solution)/shard_map/ppermute | solution.py:528
  23.9 0.8 slice_subtract_fusion
  24.7 0.7 unstack.18
  25.4 0.1 pad_add_fusion.refs_0_
  25.5 0.0 copy-start.1
  25.5 0.0 collective-permute-done.2.refs_5_
  25.5 0.0 collective-permute-done.7.refs_10_
  25.5 0.0 collective-permute-done.4.refs_7_
  25.5 0.0 collective-permute-done.6.refs_9_
  25.5 21.4 %shard_map.55 = (f32[56,128]{1,0:T(8,128)S(1)}, f32[12,24,512]{2,1,0:T(8,128)S(1)}, f32[12,24,512]{2,1,0:T(8,128)S(1)}, f32[12,24,512]{2,1,0:T(8,128)S(1)}, f32[...) custom-call(s32[2]{0:T(128)S(1)} %pad_add_fusion.refs_0_, ...), custom_call_target="tpu_custom_call" | custom-call | tf_op jit(solution)/shard_map/pallas_call | solution.py:491
  46.9 0.2 collective-permute-start.10
  47.2 4.1 %collective-permute-start.9 = (f32[56,128]{1,0:T(8,128)S(1)}, f32[56,128]{1,0:T(8,128)S(1)}, u32[]{:S(2)}, u32[]{:S(2)}) collective-permute-start(f32[56,128]{1,0:T(8,128)S(1)} %get-tuple-element.30), channel_id=1, source_target_pairs={{0,2},{1,3},{2,0},{3,1},{4,6},{5,7},{6,4},{7,5},{8,10},{9,11},{10,... | collective-permute-start | bytes 86024 | tf_op jit(solution)/shard_map/ppermute | solution.py:528
  51.3 0.0 collective-permute-start.8
  51.3 0.0 collective-permute-done.10
  51.3 2.1 %collective-permute-done.9 = f32[56,128]{1,0:T(8,128)S(1)} collective-permute-done((f32[56,128]{1,0:T(8,128)S(1)}, f32[56,128]{1,0:T(8,128)S(1)}, u32[]{:S(2)}, u32[]{:S(2)}) %collective-permute-start.9) | collective-permute-done | bytes 28704 | tf_op jit(solution)/shard_map/ppermute | solution.py:528
  53.4 0.0 collective-permute-done.8
  53.4 2.5 %collective-permute-start.11 = (f32[4,56,128]{2,1,0:T(8,128)S(1)}, f32[4,56,128]{2,1,0:T(8,128)S(1)}, u32[]{:S(2)}, u32[]{:S(2)}) collective-permute-start(f32[4,56,128]{2,1,0:T(8,128)S(1)} %pad_maximum_fusion.1), channel_id=1, source_target_pairs={{0,4},{4,0},{8,12},{12,8},{16,20},{20,16},{24,28},{28,24},{1,5},{5... | collective-permute-start | bytes 344072 | tf_op jit(solution)/shard_map/ppermute | solution.py:528
  56.0 3.8 %collective-permute-done.11 = f32[4,56,128]{2,1,0:T(8,128)S(1)} collective-permute-done((f32[4,56,128]{2,1,0:T(8,128)S(1)}, f32[4,56,128]{2,1,0:T(8,128)S(1)}, u32[]{:S(2)}, u32[]{:S(2)}) %collective-permute-start.11) | collective-permute-done | bytes 114720 | tf_op jit(solution)/shard_map/ppermute | solution.py:528
  59.8 3.9 %collective-permute-start.14 = (f32[2,4,24,128]{3,2,1,0:T(8,128)S(1)}, f32[2,4,24,128]{3,2,1,0:T(8,128)S(1)}, u32[]{:S(2)}, u32[]{:S(2)}) collective-permute-start(f32[2,4,24,128]{3,2,1,0:T(8,128)S(1)} %pad_maximum_fusion.3.refs_1_), channel_id=1, source_target_pairs={{0,24},{4,28},{8,16},{12,20},{16,8},{20,12},{24,0},{28,4},{1,25},{... | collective-permute-start | bytes 294920 | tf_op jit(solution)/shard_map/ppermute | solution.py:528
  63.7 0.6 collective-permute-start.12
  64.4 0.7 collective-permute-start.15
  65.0 0.0 collective-permute-done.15.refs_7_
  65.1 2.3 %collective-permute-done.14.refs_4_ = f32[2,4,24,128]{3,2,1,0:T(8,128)S(1)} collective-permute-done((f32[2,4,24,128]{3,2,1,0:T(8,128)S(1)}, f32[2,4,24,128]{3,2,1,0:T(8,128)S(1)}, u32[]{:S(2)}, u32[]{:S(2)}) %collective-permute-start.14) | collective-permute-done | bytes 98336 | tf_op jit(solution)/shard_map/ppermute | solution.py:528
  67.3 5.3 %collective-permute-done.13.refs_3_ = f32[2,4,24,128]{3,2,1,0:T(8,128)S(1)} collective-permute-done((f32[2,4,24,128]{3,2,1,0:T(8,128)S(1)}, f32[2,4,24,128]{3,2,1,0:T(8,128)S(1)}, u32[]{:S(2)}, u32[]{:S(2)}) %collective-permute-start.13) | collective-permute-done | bytes 98336 | tf_op jit(solution)/shard_map/ppermute | solution.py:528
  72.6 9.0 %shard_map.56.refs_11_.refs_19_ = f32[8,8,512]{2,1,0:T(8,128)S(1)} custom-call(s32[2]{0:T(128)S(1)} %pad_add_fusion.refs_0_, f32[2,4,24,128]{3,2,1,0:T(8,128)S(1)} %pad_maximum_fusion.3.refs_1_, f32[2,4,24,128]{3,2,1,0:T(8,128)S(1)} %collective-permute-done.12.refs_2_, f32[2,4,24,128]{3,2,1,0:T(8,128)S(1)} %collective-permute-done.13.refs_3_, ...), custom_call_target="tpu_custom_call" | custom-call | tf_op jit(solution)/shard_map/pallas_call | solution.py:517
  81.6 0.7 collective-permute-start.17
  82.3 3.9 %collective-permute-start.16 = (f32[8,8,512]{2,1,0:T(8,128)S(1)}, f32[8,8,512]{2,1,0:T(8,128)S(1)}, u32[]{:S(2)}, u32[]{:S(2)}) collective-permute-start(f32[8,8,512]{2,1,0:T(8,128)S(1)} %shard_map.56.refs_11_.refs_19_), channel_id=1, source_target_pairs={{0,4},{4,0},{8,12},{12,8},{16,20},{20,16},{24,28},{28,24},{1,5},{5... | collective-permute-start | bytes 393224 | tf_op jit(solution)/shard_map/ppermute | solution.py:528
  86.2 0.7 collective-permute-start.21
  86.9 1.4 collective-permute-start.18
  88.3 0.7 collective-permute-start.23
  89.0 1.3 collective-permute-start.20
  90.3 0.7 collective-permute-start.22
  91.0 3.1 %collective-permute-start.19 = (f32[8,8,512]{2,1,0:T(8,128)S(1)}, f32[8,8,512]{2,1,0:T(8,128)S(1)}, u32[]{:S(2)}, u32[]{:S(2)}) collective-permute-start(f32[8,8,512]{2,1,0:T(8,128)S(1)} %collective-permute-done.16.refs_12_), channel_id=1, source_target_pairs={{0,1},{1,0},{2,3},{3,2},{4,5},{5,4},{6,7},{7,6},{8,9},{9,8},{10,11... | collective-permute-start | bytes 393224 | tf_op jit(solution)/shard_map/ppermute | solution.py:528
  94.1 0.0 collective-permute-done.23.refs_19_
  94.1 0.0 collective-permute-done.20.refs_16_
  94.1 1.0 collective-permute-done.19.refs_15_
  95.0 22.1 %shard_map.57 = (f32[56,128]{1,0:T(8,128)S(1)}, f32[12,24,512]{2,1,0:T(8,128)S(1)}, f32[12,24,512]{2,1,0:T(8,128)S(1)}, f32[12,24,512]{2,1,0:T(8,128)S(1)}, f32[...) custom-call(s32[2]{0:T(128)S(1)} %pad_add_fusion.refs_0_, ...), custom_call_target="tpu_custom_call" | custom-call | tf_op jit(solution)/shard_map/pallas_call | solution.py:491
  117.2 0.1 collective-permute-start.26
  117.3 3.3 %collective-permute-start.25 = (f32[56,128]{1,0:T(8,128)S(1)}, f32[56,128]{1,0:T(8,128)S(1)}, u32[]{:S(2)}, u32[]{:S(2)}) collective-permute-start(f32[56,128]{1,0:T(8,128)S(1)} %get-tuple-element.43), channel_id=1, source_target_pairs={{0,2},{1,3},{2,0},{3,1},{4,6},{5,7},{6,4},{7,5},{8,10},{9,11},{10,... | collective-permute-start | bytes 86024 | tf_op jit(solution)/shard_map/ppermute | solution.py:528
  120.5 0.0 collective-permute-start.24
  120.6 0.0 collective-permute-done.26
  120.6 2.0 %collective-permute-done.25 = f32[56,128]{1,0:T(8,128)S(1)} collective-permute-done((f32[56,128]{1,0:T(8,128)S(1)}, f32[56,128]{1,0:T(8,128)S(1)}, u32[]{:S(2)}, u32[]{:S(2)}) %collective-permute-start.25) | collective-permute-done | bytes 28704 | tf_op jit(solution)/shard_map/ppermute | solution.py:528
  122.6 3.0 %collective-permute-start.27 = (f32[4,56,128]{2,1,0:T(8,128)S(1)}, f32[4,56,128]{2,1,0:T(8,128)S(1)}, u32[]{:S(2)}, u32[]{:S(2)}) collective-permute-start(f32[4,56,128]{2,1,0:T(8,128)S(1)} %pad_maximum_fusion.2), channel_id=1, source_target_pairs={{0,4},{4,0},{8,12},{12,8},{16,20},{20,16},{24,28},{28,24},{1,5},{5... | collective-permute-start | bytes 344072 | tf_op jit(solution)/shard_map/ppermute | solution.py:528
  125.7 2.8 %collective-permute-done.27 = f32[4,56,128]{2,1,0:T(8,128)S(1)} collective-permute-done((f32[4,56,128]{2,1,0:T(8,128)S(1)}, f32[4,56,128]{2,1,0:T(8,128)S(1)}, u32[]{:S(2)}, u32[]{:S(2)}) %collective-permute-start.27) | collective-permute-done | bytes 114720 | tf_op jit(solution)/shard_map/ppermute | solution.py:528
  128.5 3.9 %collective-permute-start.30 = (f32[2,4,24,128]{3,2,1,0:T(8,128)S(1)}, f32[2,4,24,128]{3,2,1,0:T(8,128)S(1)}, u32[]{:S(2)}, u32[]{:S(2)}) collective-permute-start(f32[2,4,24,128]{3,2,1,0:T(8,128)S(1)} %pad_maximum_fusion.4.refs_1_), channel_id=1, source_target_pairs={{0,24},{4,28},{8,16},{12,20},{16,8},{20,12},{24,0},{28,4},{1,25},{... | collective-permute-start | bytes 294920 | tf_op jit(solution)/shard_map/ppermute | solution.py:528
  132.4 0.6 collective-permute-start.28
  133.1 0.7 collective-permute-start.31
  133.8 1.9 %collective-permute-done.30.refs_4_ = f32[2,4,24,128]{3,2,1,0:T(8,128)S(1)} collective-permute-done((f32[2,4,24,128]{3,2,1,0:T(8,128)S(1)}, f32[2,4,24,128]{3,2,1,0:T(8,128)S(1)}, u32[]{:S(2)}, u32[]{:S(2)}) %collective-permute-start.30) | collective-permute-done | bytes 98336 | tf_op jit(solution)/shard_map/ppermute | solution.py:528
  135.7 5.4 %collective-permute-done.29.refs_3_ = f32[2,4,24,128]{3,2,1,0:T(8,128)S(1)} collective-permute-done((f32[2,4,24,128]{3,2,1,0:T(8,128)S(1)}, f32[2,4,24,128]{3,2,1,0:T(8,128)S(1)}, u32[]{:S(2)}, u32[]{:S(2)}) %collective-permute-start.29) | collective-permute-done | bytes 98336 | tf_op jit(solution)/shard_map/ppermute | solution.py:528
  141.1 0.0 collective-permute-done.28.refs_2_
  141.1 9.6 %shard_map.58 = f32[8,8,512]{2,1,0:T(8,128)} custom-call(s32[2]{0:T(128)S(1)} %pad_add_fusion.refs_0_, f32[2,4,24,128]{3,2,1,0:T(8,128)S(1)} %pad_maximum_fusion.4.refs_1_, f32[2,4,24,128]{3,2,1,0:T(8,128)S(1)} %collective-permute-done.28.refs_2_, f32[2,4,24,128]{3,2,1,0:T(8,128)S(1)} %collective-permute-done.29.refs_3_, ...), custom_call_target="tpu_custom_call" | custom-call | tf_op jit(solution)/shard_map/pallas_call | solution.py:517
  (27 shorter events, 0.1 us)
Async XLA Ops:
  2.7 10.0 %collective-permute-start.1 = (f32[17,8,512]{2,1,0:T(8,128)S(1)}, f32[17,8,512]{2,1,0:T(8,128)S(1)}, u32[]{:S(2)}, u32[]{:S(2)}) collective-permute-start(f32[17,8,512]{2,1,0:T(8,128)S(1)} %pad_maximum_fusion.refs_2_), channel_id=1, source_target_pairs={{4,8},{12,16},{20,24},{8,4},{16,12},{24,20},{5,9},{13,17},{21,25},... | collective-permute-start | bytes 835592 | tf_op jit(solution)/shard_map/ppermute | solution.py:534
  3.3 17.0 %collective-permute-start = (f32[17,8,512]{2,1,0:T(8,128)S(1)}, f32[17,8,512]{2,1,0:T(8,128)S(1)}, u32[]{:S(2)}, u32[]{:S(2)}) collective-permute-start(f32[17,8,512]{2,1,0:T(8,128)S(1)} %pad_maximum_fusion.refs_2_), channel_id=1, source_target_pairs={{0,4},{4,0},{8,12},{12,8},{16,20},{20,16},{24,28},{28,24},{1,5},{5... | collective-permute-start | bytes 835592 | tf_op jit(solution)/shard_map/ppermute | solution.py:528
  9.1 11.9 %collective-permute-start.5 = (f32[17,8,512]{2,1,0:T(8,128)S(1)}, f32[17,8,512]{2,1,0:T(8,128)S(1)}, u32[]{:S(2)}, u32[]{:S(2)}) collective-permute-start(f32[17,8,512]{2,1,0:T(8,128)S(1)} %pad_maximum_fusion.refs_2_), channel_id=1, source_target_pairs={{1,2},{2,1},{5,6},{6,5},{9,10},{10,9},{13,14},{14,13},{17,18},{18,... | collective-permute-start | bytes 835592 | tf_op jit(solution)/shard_map/ppermute | solution.py:534
  9.8 15.7 %collective-permute-start.2 = (f32[17,8,512]{2,1,0:T(8,128)S(1)}, f32[17,8,512]{2,1,0:T(8,128)S(1)}, u32[]{:S(2)}, u32[]{:S(2)}) collective-permute-start(f32[17,8,512]{2,1,0:T(8,128)S(1)} %pad_maximum_fusion.refs_2_), channel_id=1, source_target_pairs={{0,1},{1,0},{2,3},{3,2},{4,5},{5,4},{6,7},{7,6},{8,9},{9,8},{10,11... | collective-permute-start | bytes 835592 | tf_op jit(solution)/shard_map/ppermute | solution.py:528
  12.7 12.8 %collective-permute-start.7 = (f32[17,8,512]{2,1,0:T(8,128)S(1)}, f32[17,8,512]{2,1,0:T(8,128)S(1)}, u32[]{:S(2)}, u32[]{:S(2)}) collective-permute-start(f32[17,8,512]{2,1,0:T(8,128)S(1)} %collective-permute-done.1.refs_4_), channel_id=1, source_target_pairs={{1,2},{2,1},{5,6},{6,5},{9,10},{10,9},{13,14},{14,13},{17,18},{18,... | collective-permute-start | bytes 835592 | tf_op jit(solution)/shard_map/ppermute | solution.py:534
  13.4 12.1 %collective-permute-start.4 = (f32[17,8,512]{2,1,0:T(8,128)S(1)}, f32[17,8,512]{2,1,0:T(8,128)S(1)}, u32[]{:S(2)}, u32[]{:S(2)}) collective-permute-start(f32[17,8,512]{2,1,0:T(8,128)S(1)} %collective-permute-done.1.refs_4_), channel_id=1, source_target_pairs={{0,1},{1,0},{2,3},{3,2},{4,5},{5,4},{6,7},{7,6},{8,9},{9,8},{10,11... | collective-permute-start | bytes 835592 | tf_op jit(solution)/shard_map/ppermute | solution.py:528
  20.3 5.2 %collective-permute-start.6 = (f32[17,8,512]{2,1,0:T(8,128)S(1)}, f32[17,8,512]{2,1,0:T(8,128)S(1)}, u32[]{:S(2)}, u32[]{:S(2)}) collective-permute-start(f32[17,8,512]{2,1,0:T(8,128)S(1)} %collective-permute-done.refs_3_), channel_id=1, source_target_pairs={{1,2},{2,1},{5,6},{6,5},{9,10},{10,9},{13,14},{14,13},{17,18},{18,... | collective-permute-start | bytes 835592 | tf_op jit(solution)/shard_map/ppermute | solution.py:534
  21.0 4.5 %collective-permute-start.3 = (f32[17,8,512]{2,1,0:T(8,128)S(1)}, f32[17,8,512]{2,1,0:T(8,128)S(1)}, u32[]{:S(2)}, u32[]{:S(2)}) collective-permute-start(f32[17,8,512]{2,1,0:T(8,128)S(1)} %collective-permute-done.refs_3_), channel_id=1, source_target_pairs={{0,1},{1,0},{2,3},{3,2},{4,5},{5,4},{6,7},{7,6},{8,9},{9,8},{10,11... | collective-permute-start | bytes 835592 | tf_op jit(solution)/shard_map/ppermute | solution.py:528
  25.5 47.1 %copy-start.1 = (f32[8,8,512]{2,1,0:T(8,128)S(1)}, f32[8,8,512]{2,1,0:T(8,128)}, u32[]{:S(2)}) copy-start(f32[8,8,512]{2,1,0:T(8,128)} %refs_19_.1) | copy-start | bytes 393220
  46.9 34.7 %copy-start = (f32[24,3,8,512]{3,2,1,0:T(8,128)}, f32[24,3,8,512]{3,2,1,0:T(8,128)S(1)}, u32[]{:S(2)}) copy-start(f32[24,3,8,512]{3,2,1,0:T(8,128)S(1)} %get-tuple-element.42.refs_20_) | copy-start | bytes 3538948
  46.9 4.3 %collective-permute-start.10 = (f32[56,128]{1,0:T(8,128)S(1)}, f32[56,128]{1,0:T(8,128)S(1)}, u32[]{:S(2)}, u32[]{:S(2)}) collective-permute-start(f32[56,128]{1,0:T(8,128)S(1)} %get-tuple-element.30), channel_id=1, source_target_pairs={{0,3},{1,2},{2,1},{3,0},{4,7},{5,6},{6,5},{7,4},{8,11},{9,10},{10,... | collective-permute-start | bytes 86024 | tf_op jit(solution)/shard_map/ppermute | solution.py:528
  47.2 6.3 %collective-permute-start.9 = (f32[56,128]{1,0:T(8,128)S(1)}, f32[56,128]{1,0:T(8,128)S(1)}, u32[]{:S(2)}, u32[]{:S(2)}) collective-permute-start(f32[56,128]{1,0:T(8,128)S(1)} %get-tuple-element.30), channel_id=1, source_target_pairs={{0,2},{1,3},{2,0},{3,1},{4,6},{5,7},{6,4},{7,5},{8,10},{9,11},{10,... | collective-permute-start | bytes 86024 | tf_op jit(solution)/shard_map/ppermute | solution.py:528
  51.3 2.2 %collective-permute-start.8 = (f32[56,128]{1,0:T(8,128)S(1)}, f32[56,128]{1,0:T(8,128)S(1)}, u32[]{:S(2)}, u32[]{:S(2)}) collective-permute-start(f32[56,128]{1,0:T(8,128)S(1)} %get-tuple-element.30), channel_id=1, source_target_pairs={{0,1},{1,0},{2,3},{3,2},{4,5},{5,4},{6,7},{7,6},{8,9},{9,8},{10,11... | collective-permute-start | bytes 86024 | tf_op jit(solution)/shard_map/ppermute | solution.py:528
  53.4 6.4 %collective-permute-start.11 = (f32[4,56,128]{2,1,0:T(8,128)S(1)}, f32[4,56,128]{2,1,0:T(8,128)S(1)}, u32[]{:S(2)}, u32[]{:S(2)}) collective-permute-start(f32[4,56,128]{2,1,0:T(8,128)S(1)} %pad_maximum_fusion.1), channel_id=1, source_target_pairs={{0,4},{4,0},{8,12},{12,8},{16,20},{20,16},{24,28},{28,24},{1,5},{5... | collective-permute-start | bytes 344072 | tf_op jit(solution)/shard_map/ppermute | solution.py:528
  59.8 7.5 %collective-permute-start.14 = (f32[2,4,24,128]{3,2,1,0:T(8,128)S(1)}, f32[2,4,24,128]{3,2,1,0:T(8,128)S(1)}, u32[]{:S(2)}, u32[]{:S(2)}) collective-permute-start(f32[2,4,24,128]{3,2,1,0:T(8,128)S(1)} %pad_maximum_fusion.3.refs_1_), channel_id=1, source_target_pairs={{0,24},{4,28},{8,16},{12,20},{16,8},{20,12},{24,0},{28,4},{1,25},{... | collective-permute-start | bytes 294920 | tf_op jit(solution)/shard_map/ppermute | solution.py:528
  63.7 8.9 %collective-permute-start.13 = (f32[2,4,24,128]{3,2,1,0:T(8,128)S(1)}, f32[2,4,24,128]{3,2,1,0:T(8,128)S(1)}, u32[]{:S(2)}, u32[]{:S(2)}) collective-permute-start(f32[2,4,24,128]{3,2,1,0:T(8,128)S(1)} %pad_maximum_fusion.3.refs_1_), channel_id=1, source_target_pairs={{0,16},{4,20},{8,24},{12,28},{16,0},{20,4},{24,8},{28,12},{1,17},{... | collective-permute-start | bytes 294920 | tf_op jit(solution)/shard_map/ppermute | solution.py:528
  63.7 8.9 %collective-permute-start.12 = (f32[2,4,24,128]{3,2,1,0:T(8,128)S(1)}, f32[2,4,24,128]{3,2,1,0:T(8,128)S(1)}, u32[]{:S(2)}, u32[]{:S(2)}) collective-permute-start(f32[2,4,24,128]{3,2,1,0:T(8,128)S(1)} %pad_maximum_fusion.3.refs_1_), channel_id=1, source_target_pairs={{0,8},{4,12},{8,0},{12,4},{16,24},{20,28},{24,16},{28,20},{1,9},{5... | collective-permute-start | bytes 294920 | tf_op jit(solution)/shard_map/ppermute | solution.py:528
  64.4 0.7 collective-permute-start.15
  81.6 6.7 %collective-permute-start.17 = (f32[8,8,512]{2,1,0:T(8,128)S(1)}, f32[8,8,512]{2,1,0:T(8,128)S(1)}, u32[]{:S(2)}, u32[]{:S(2)}) collective-permute-start(f32[8,8,512]{2,1,0:T(8,128)S(1)} %shard_map.56.refs_11_.refs_19_), channel_id=1, source_target_pairs={{4,8},{12,16},{20,24},{8,4},{16,12},{24,20},{5,9},{13,17},{21,25},... | collective-permute-start | bytes 393224 | tf_op jit(solution)/shard_map/ppermute | solution.py:534
  82.3 8.0 %collective-permute-start.16 = (f32[8,8,512]{2,1,0:T(8,128)S(1)}, f32[8,8,512]{2,1,0:T(8,128)S(1)}, u32[]{:S(2)}, u32[]{:S(2)}) collective-permute-start(f32[8,8,512]{2,1,0:T(8,128)S(1)} %shard_map.56.refs_11_.refs_19_), channel_id=1, source_target_pairs={{0,4},{4,0},{8,12},{12,8},{16,20},{20,16},{24,28},{28,24},{1,5},{5... | collective-permute-start | bytes 393224 | tf_op jit(solution)/shard_map/ppermute | solution.py:528
  86.2 4.8 %collective-permute-start.21 = (f32[8,8,512]{2,1,0:T(8,128)S(1)}, f32[8,8,512]{2,1,0:T(8,128)S(1)}, u32[]{:S(2)}, u32[]{:S(2)}) collective-permute-start(f32[8,8,512]{2,1,0:T(8,128)S(1)} %shard_map.56.refs_11_.refs_19_), channel_id=1, source_target_pairs={{1,2},{2,1},{5,6},{6,5},{9,10},{10,9},{13,14},{14,13},{17,18},{18,... | collective-permute-start | bytes 393224 | tf_op jit(solution)/shard_map/ppermute | solution.py:534
  86.9 7.2 %collective-permute-start.18 = (f32[8,8,512]{2,1,0:T(8,128)S(1)}, f32[8,8,512]{2,1,0:T(8,128)S(1)}, u32[]{:S(2)}, u32[]{:S(2)}) collective-permute-start(f32[8,8,512]{2,1,0:T(8,128)S(1)} %shard_map.56.refs_11_.refs_19_), channel_id=1, source_target_pairs={{0,1},{1,0},{2,3},{3,2},{4,5},{5,4},{6,7},{7,6},{8,9},{9,8},{10,11... | collective-permute-start | bytes 393224 | tf_op jit(solution)/shard_map/ppermute | solution.py:528
  88.3 5.8 %collective-permute-start.23 = (f32[8,8,512]{2,1,0:T(8,128)S(1)}, f32[8,8,512]{2,1,0:T(8,128)S(1)}, u32[]{:S(2)}, u32[]{:S(2)}) collective-permute-start(f32[8,8,512]{2,1,0:T(8,128)S(1)} %collective-permute-done.17.refs_13_), channel_id=1, source_target_pairs={{1,2},{2,1},{5,6},{6,5},{9,10},{10,9},{13,14},{14,13},{17,18},{18,... | collective-permute-start | bytes 393224 | tf_op jit(solution)/shard_map/ppermute | solution.py:534
  89.0 5.1 %collective-permute-start.20 = (f32[8,8,512]{2,1,0:T(8,128)S(1)}, f32[8,8,512]{2,1,0:T(8,128)S(1)}, u32[]{:S(2)}, u32[]{:S(2)}) collective-permute-start(f32[8,8,512]{2,1,0:T(8,128)S(1)} %collective-permute-done.17.refs_13_), channel_id=1, source_target_pairs={{0,1},{1,0},{2,3},{3,2},{4,5},{5,4},{6,7},{7,6},{8,9},{9,8},{10,11... | collective-permute-start | bytes 393224 | tf_op jit(solution)/shard_map/ppermute | solution.py:528
  90.3 3.8 %collective-permute-start.22 = (f32[8,8,512]{2,1,0:T(8,128)S(1)}, f32[8,8,512]{2,1,0:T(8,128)S(1)}, u32[]{:S(2)}, u32[]{:S(2)}) collective-permute-start(f32[8,8,512]{2,1,0:T(8,128)S(1)} %collective-permute-done.16.refs_12_), channel_id=1, source_target_pairs={{1,2},{2,1},{5,6},{6,5},{9,10},{10,9},{13,14},{14,13},{17,18},{18,... | collective-permute-start | bytes 393224 | tf_op jit(solution)/shard_map/ppermute | solution.py:534
  91.0 4.1 %collective-permute-start.19 = (f32[8,8,512]{2,1,0:T(8,128)S(1)}, f32[8,8,512]{2,1,0:T(8,128)S(1)}, u32[]{:S(2)}, u32[]{:S(2)}) collective-permute-start(f32[8,8,512]{2,1,0:T(8,128)S(1)} %collective-permute-done.16.refs_12_), channel_id=1, source_target_pairs={{0,1},{1,0},{2,3},{3,2},{4,5},{5,4},{6,7},{7,6},{8,9},{9,8},{10,11... | collective-permute-start | bytes 393224 | tf_op jit(solution)/shard_map/ppermute | solution.py:528
  117.2 3.4 %collective-permute-start.26 = (f32[56,128]{1,0:T(8,128)S(1)}, f32[56,128]{1,0:T(8,128)S(1)}, u32[]{:S(2)}, u32[]{:S(2)}) collective-permute-start(f32[56,128]{1,0:T(8,128)S(1)} %get-tuple-element.43), channel_id=1, source_target_pairs={{0,3},{1,2},{2,1},{3,0},{4,7},{5,6},{6,5},{7,4},{8,11},{9,10},{10,... | collective-permute-start | bytes 86024 | tf_op jit(solution)/shard_map/ppermute | solution.py:528
  117.3 5.3 %collective-permute-start.25 = (f32[56,128]{1,0:T(8,128)S(1)}, f32[56,128]{1,0:T(8,128)S(1)}, u32[]{:S(2)}, u32[]{:S(2)}) collective-permute-start(f32[56,128]{1,0:T(8,128)S(1)} %get-tuple-element.43), channel_id=1, source_target_pairs={{0,2},{1,3},{2,0},{3,1},{4,6},{5,7},{6,4},{7,5},{8,10},{9,11},{10,... | collective-permute-start | bytes 86024 | tf_op jit(solution)/shard_map/ppermute | solution.py:528
  120.5 2.1 %collective-permute-start.24 = (f32[56,128]{1,0:T(8,128)S(1)}, f32[56,128]{1,0:T(8,128)S(1)}, u32[]{:S(2)}, u32[]{:S(2)}) collective-permute-start(f32[56,128]{1,0:T(8,128)S(1)} %get-tuple-element.43), channel_id=1, source_target_pairs={{0,1},{1,0},{2,3},{3,2},{4,5},{5,4},{6,7},{7,6},{8,9},{9,8},{10,11... | collective-permute-start | bytes 86024 | tf_op jit(solution)/shard_map/ppermute | solution.py:528
  122.6 5.9 %collective-permute-start.27 = (f32[4,56,128]{2,1,0:T(8,128)S(1)}, f32[4,56,128]{2,1,0:T(8,128)S(1)}, u32[]{:S(2)}, u32[]{:S(2)}) collective-permute-start(f32[4,56,128]{2,1,0:T(8,128)S(1)} %pad_maximum_fusion.2), channel_id=1, source_target_pairs={{0,4},{4,0},{8,12},{12,8},{16,20},{20,16},{24,28},{28,24},{1,5},{5... | collective-permute-start | bytes 344072 | tf_op jit(solution)/shard_map/ppermute | solution.py:528
  128.5 7.2 %collective-permute-start.30 = (f32[2,4,24,128]{3,2,1,0:T(8,128)S(1)}, f32[2,4,24,128]{3,2,1,0:T(8,128)S(1)}, u32[]{:S(2)}, u32[]{:S(2)}) collective-permute-start(f32[2,4,24,128]{3,2,1,0:T(8,128)S(1)} %pad_maximum_fusion.4.refs_1_), channel_id=1, source_target_pairs={{0,24},{4,28},{8,16},{12,20},{16,8},{20,12},{24,0},{28,4},{1,25},{... | collective-permute-start | bytes 294920 | tf_op jit(solution)/shard_map/ppermute | solution.py:528
  132.4 8.7 %collective-permute-start.29 = (f32[2,4,24,128]{3,2,1,0:T(8,128)S(1)}, f32[2,4,24,128]{3,2,1,0:T(8,128)S(1)}, u32[]{:S(2)}, u32[]{:S(2)}) collective-permute-start(f32[2,4,24,128]{3,2,1,0:T(8,128)S(1)} %pad_maximum_fusion.4.refs_1_), channel_id=1, source_target_pairs={{0,16},{4,20},{8,24},{12,28},{16,0},{20,4},{24,8},{28,12},{1,17},{... | collective-permute-start | bytes 294920 | tf_op jit(solution)/shard_map/ppermute | solution.py:528
  132.4 8.7 %collective-permute-start.28 = (f32[2,4,24,128]{3,2,1,0:T(8,128)S(1)}, f32[2,4,24,128]{3,2,1,0:T(8,128)S(1)}, u32[]{:S(2)}, u32[]{:S(2)}) collective-permute-start(f32[2,4,24,128]{3,2,1,0:T(8,128)S(1)} %pad_maximum_fusion.4.refs_1_), channel_id=1, source_target_pairs={{0,8},{4,12},{8,0},{12,4},{16,24},{20,28},{24,16},{28,20},{1,9},{5... | collective-permute-start | bytes 294920 | tf_op jit(solution)/shard_map/ppermute | solution.py:528
  133.1 0.7 collective-permute-start.31

commit v3 on v2

--- a/solution.py
+++ b/solution.py
@@ -63,7 +63,7 @@
     if first:
         sat_out, refs = refs[0], refs[1:]
     head, cond, stor, grow, fx, fy, fz, src, inv, err = refs[:10]
-    src1, stor1, fx1, fy1, fz1, inv1, err1, rows2 = refs[10:]
+    src1, stor1, fx1, fy1, fz1, inv1, err1, rows2, table_rows = refs[10:]
 
     strip, slab = where_ref[0], where_ref[1]
     zw, xw = 3 * zl, 3 * xl
@@ -90,7 +90,13 @@
             jnp.logical_and(z == 2 * width, slab == slabs - 1),
         )
 
-    table = table_ref[...]
+    resid, high, alpha, shape_n, k_sat = (table_ref[k : k + 1, :] for k in range(5))
+    classes = table_ref.shape[1]
+    rows = (high - resid, alpha, shape_n, k_sat, 1.0 - 1.0 / shape_n)
+    table_rows[...] = jnp.ones(table_rows.shape, jnp.float32)
+    for k, row in enumerate(rows):
+        table_rows[k : k + 1, 0:classes] = row
+    table = table_rows[...]
     for block in range(9):
         z_at, x_at = place(block // 3, slab), place(block % 3, strip)
 
@@ -120,14 +126,15 @@
             head[z, x_at] = p
             return carry
 
-        lax.fori_loop(0, zl, soil_step, 0)
+        skip = 0 if block < 3 else 1
+        start = jnp.where(z_at == 0, skip, 0)
+        lax.fori_loop(0, zl - skip, lambda i, c: soil_step(start + i, c), 0, unroll=zl - skip)
 
     def face_z(z):
-        both = 0.5 * (slab_of(cond, jnp.maximum(z - 1, 0)) + slab_of(cond, jnp.minimum(z, zw - 1)))
-        closed = jnp.logical_or(edge_z(z, zl), jnp.logical_or(z == 0, z == zw))
-        return both * jnp.where(closed, 0.0, 1.0)
-
-    fz[0] = jnp.zeros(shape, jnp.float32)
+        both = 0.5 * (slab_of(cond, z - 1) + slab_of(cond, z))
+        return both * jnp.where(edge_z(z, zl), 0.0, 1.0)
+
+    fz[2] = face_z(2)
 
     def face_step(z, carry):
         c, p = slab_of(cond, z), slab_of(head, z)
@@ -136,8 +143,8 @@
         low, high = fz[z], face_z(z + 1)
         flux_x = across * (roll(p, 1, 0) - p)
         flux_y = along * (roll(p, 1, 1) - p)
-        p_low = slab_of(head, jnp.maximum(z - 1, 0))
-        p_high = slab_of(head, jnp.minimum(z + 1, zw - 1))
+        p_low = slab_of(head, z - 1)
+        p_high = slab_of(head, z + 1)
         flux_low = low * (p_low - p + GRAVITY)
         flux_high = high * (p - p_high + GRAVITY)
         source = (flux_x - roll(flux_x, -1, 0)) + (flux_y - roll(flux_y, -1, 1))
@@ -149,13 +156,13 @@
         err[z] = jnp.where(parity0 == (z & 1), source * inverse, 0.0)
         return carry
 
-    lax.fori_loop(0, zw, face_step, 0)
+    lax.fori_loop(2, zw - 2, face_step, 0, unroll=4)
 
     def sum0(z):
         return neighbour_sum(
             err[z],
-            err[jnp.maximum(z - 1, 0)],
-            err[jnp.minimum(z + 1, zw - 1)],
+            err[z - 1],
+            err[z + 1],
             fx[z],
             fy[z],
             fz[z],
@@ -168,7 +175,7 @@
         err[z] = jnp.where(parity0 == (z & 1), err[z], updated)
         return carry
 
-    lax.fori_loop(1, zw - 1, smooth_step, 0)
+    lax.fori_loop(3, zw - 3, smooth_step, 0, unroll=3)
 
     def coarse_step(k, carry):
         za, zb = 2 * k, 2 * k + 1
@@ -184,7 +191,7 @@
         fz1[k] = spread_pairs(spread_pairs(fz[za], x_low, 1, 0), y_low, 1, 1)
         return carry
 
-    lax.fori_loop(1, zw // 2 - 1, coarse_step, 0)
+    lax.fori_loop(2, zw // 2 - 1, coarse_step, 0, unroll=3)
 
     def first1(k, carry):
         across, along = fx1[k], fy1[k]
@@ -195,7 +202,7 @@
         return carry
 
     low1, high1 = zl // 2 - 2, zl + 2
-    lax.fori_loop(low1, high1, first1, 0)
+    lax.fori_loop(low1, high1, first1, 0, unroll=4)
 
     def sum1(k):
         return neighbour_sum(
@@ -207,7 +214,7 @@
         err1[k] = jnp.where(parity1 == (k & 1), err1[k], updated)
         return carry
 
-    lax.fori_loop(low1 + 1, high1 - 1, second1, 0)
+    lax.fori_loop(low1 + 1, high1 - 1, second1, 0, unroll=3)
 
     rows2[...] = jnp.zeros(rows2.shape, jnp.float32)
     own1 = zl // 2
@@ -246,14 +253,14 @@
             out[i] = ref[zl - 2 + i]
         return carry
 
-    lax.fori_loop(0, zl + 4, keep0, 0)
+    lax.fori_loop(0, zl + 4, keep0, 0, unroll=3)
 
     def keep1(i, carry):
         for out, ref in zip(outs1, (src1, inv1, fx1, fy1, fz1)):
             out[i] = ref[zl // 2 - 2 + i]
         return carry
 
-    lax.fori_loop(0, zl // 2 + 5, keep1, 0)
+    lax.fori_loop(0, zl // 2 + 5, keep1, 0, unroll=3)
 
 
 def solve_blocks(rhs, store, across, vertical, scratch, answer):
@@ -438,7 +445,7 @@
             level1(k, colour)
             return carry
 
-        lax.fori_loop(zl1 - reach, 2 * zl1 + reach, step, 0)
+        lax.fori_loop(zl1 - reach, 2 * zl1 + reach, step, 0, unroll=2)
 
     up1(0, 2)
     up1(1, 1)
@@ -447,7 +454,7 @@
         e0[i] = e0_in[i] + at1((zl - 2 + i) // 2)
         return carry
 
-    lax.fori_loop(0, zl + 4, join, 0)
+    lax.fori_loop(0, zl + 4, join, 0, unroll=3)
 
     def up0(colour, reach):
         def step(i, carry):
@@ -458,7 +465,7 @@
             e0[i] = jnp.where(parity0 == ((i + colour) & 1), updated, e0[i])
             return carry
 
-        lax.fori_loop(2 - reach, zl + 2 + reach, step, 0)
+        lax.fori_loop(2 - reach, zl + 2 + reach, step, 0, unroll=2)
 
     up0(0, 1)
     up0(1, 0)
@@ -494,7 +501,7 @@
         in_specs=[SMEM] + [VMEM] * (len(operands) - 1),
         out_specs=[VMEM] * len(out_shape),
         scratch_shapes=[split] * 4 + [full] * 2 + [tall] + [full] * 3 + [half] * 7
-        + [pltpu.VMEM((rows2, ny), jnp.float32)],
+        + [pltpu.VMEM((rows2, ny), jnp.float32), pltpu.VMEM((8, 128), jnp.float32)],
         compiler_params=pltpu.CompilerParams(vmem_limit_bytes=44 * 1024 * 1024),
     )(*operands)
 
@@ -555,9 +562,6 @@
     zl, xl, ny = head_old.shape
     strips, slabs = lax.axis_size("xy"), lax.axis_size("gz")
     where = jnp.stack([lax.axis_index("xy"), lax.axis_index("gz")]).astype(jnp.int32)
-    resid, sat, alpha, shape_n, k_sat = soil_table
-    table = jnp.stack([sat - resid, alpha, shape_n, k_sat, 1.0 - 1.0 / shape_n])
-    table = jnp.pad(table, ((0, 3), (0, 128 - table.shape[1])))
     sun_share = jnp.maximum(0.0, jnp.sin(math.pi * (sun_bin.astype(jnp.float32) - 6.0) / 12.0))
     forcing = ET_PEAK * sun_share * land_mask.astype(jnp.float32)
     own = jnp.concatenate([head_old, soil_type.astype(jnp.float32), forcing[None]])
@@ -573,9 +577,11 @@
         near = [full[:, base:], partner[:, base:], odd_pairs(full[:, base:], "xy")]
         return up(*sizes, where, pieces, near, kept, head)
 
-    payload, *kept, sat_old = down(True, *sizes, where, table, state)
+    payload, *kept, sat_old = down(True, *sizes, where, soil_table, state)
     head = finish(payload, kept, head_old)
-    payload, *kept = down(False, *sizes, where, table, state, neighbourhood(head), sat_old)
+    payload, *kept = down(
+        False, *sizes, where, soil_table, state, neighbourhood(head), sat_old
+    )
     return finish(payload, kept, head)
 
 

time: 151 us -> 129 us (0.85)
  Pallas kernels: 62.1 us -> 39.6 us
    pallas_call x2, Pallas kernels: 43.5 us -> 23.4 us  [down(): pl.pallas_call(functools.partial(down_kernel, first, slabs, strips, zl, x...]
    pallas_call x2, Pallas kernels: 18.6 us -> 16.2 us  [up(): pl.pallas_call(functools.partial(up_kernel, slabs, strips, zl, xl, counts...]
  transfers between devices with their start and end apart: 32 -> 32, of which waited for: 10 -> 12; matrix products, arithmetic and copies ran while one was open for 1% -> 0% of each run, Pallas kernels for 0% -> 0%
where the time goes in v3:
time: 129 us
  starting transfers between devices  52.1 us (40%)
  Pallas kernels  39.6 us (31%)
  waiting for transfers between devices  33.5 us (26%)
  other arithmetic  2.77 us (2%)
    ppermute x22, starting transfers between devices, swapped(): lax.ppermute(x, axis, [(i, i ^ mask) for i in range(lax.axis_size(axis))])  45.3 us
    ppermute x22, waiting for transfers between devices, swapped(): lax.ppermute(x, axis, [(i, i ^ mask) for i in range(lax.axis_size(axis))])  33.4 us
    pallas_call x2, Pallas kernels, down(): pl.pallas_call(functools.partial(down_kernel, first, slabs, strips, zl, x...  23.4 us
    pallas_call x2, Pallas kernels, up(): pl.pallas_call(functools.partial(up_kernel, slabs, strips, zl, xl, counts...  16.2 us
    ppermute x10, starting transfers between devices, odd_pairs(): return lax.ppermute(x, axis, pairs + [(j, i) for i, j in pairs])  6.81 us
  transfers between devices with their start and end apart: 32, of which 12 were waited for; matrix products, arithmetic and copies ran while one was open for 0% of the time, Pallas kernels for 0%

profile of v3, /device:TPU:0, one launch (start us, length us, event | category | flops | bytes accessed | tf_op | source)
XLA Modules:
  0.0 129.0 jit_solution(9331053324488249205)
XLA Ops:
  0.0 0.9 convert_element_type.9
  0.9 0.8 multiply_bitcast_fusion
  1.7 0.9 pad_maximum_fusion.refs_2_
  2.7 0.7 collective-permute-start.1
  3.3 5.8 %collective-permute-start = (f32[17,8,512]{2,1,0:T(8,128)S(1)}, f32[17,8,512]{2,1,0:T(8,128)S(1)}, u32[]{:S(2)}, u32[]{:S(2)}) collective-permute-start(f32[17,8,512]{2,1,0:T(8,128)S(1)} %pad_maximum_fusion.refs_2_), channel_id=1, source_target_pairs={{0,4},{4,0},{8,12},{12,8},{16,20},{20,16},{24,28},{28,24},{1,5},{5... | collective-permute-start | bytes 835592 | tf_op jit(solution)/shard_map/ppermute | solution.py:535
  9.1 0.7 collective-permute-start.5
  9.8 2.9 %collective-permute-start.2 = (f32[17,8,512]{2,1,0:T(8,128)S(1)}, f32[17,8,512]{2,1,0:T(8,128)S(1)}, u32[]{:S(2)}, u32[]{:S(2)}) collective-permute-start(f32[17,8,512]{2,1,0:T(8,128)S(1)} %pad_maximum_fusion.refs_2_), channel_id=1, source_target_pairs={{0,1},{1,0},{2,3},{3,2},{4,5},{5,4},{6,7},{7,6},{8,9},{9,8},{10,11... | collective-permute-start | bytes 835592 | tf_op jit(solution)/shard_map/ppermute | solution.py:535
  12.7 0.0 collective-permute-done.1.refs_4_
  12.7 0.7 collective-permute-start.7
  13.4 1.3 %collective-permute-start.4 = (f32[17,8,512]{2,1,0:T(8,128)S(1)}, f32[17,8,512]{2,1,0:T(8,128)S(1)}, u32[]{:S(2)}, u32[]{:S(2)}) collective-permute-start(f32[17,8,512]{2,1,0:T(8,128)S(1)} %collective-permute-done.1.refs_4_), channel_id=1, source_target_pairs={{0,1},{1,0},{2,3},{3,2},{4,5},{5,4},{6,7},{7,6},{8,9},{9,8},{10,11... | collective-permute-start | bytes 835592 | tf_op jit(solution)/shard_map/ppermute | solution.py:535
  14.7 5.6 %collective-permute-done.refs_3_ = f32[17,8,512]{2,1,0:T(8,128)S(1)} collective-permute-done((f32[17,8,512]{2,1,0:T(8,128)S(1)}, f32[17,8,512]{2,1,0:T(8,128)S(1)}, u32[]{:S(2)}, u32[]{:S(2)}) %collective-permute-start) | collective-permute-done | bytes 278560 | tf_op jit(solution)/shard_map/ppermute | solution.py:535
  20.3 0.7 collective-permute-start.6
  21.0 0.0 collective-permute-done.5.refs_8_
  21.0 2.9 %collective-permute-start.3 = (f32[17,8,512]{2,1,0:T(8,128)S(1)}, f32[17,8,512]{2,1,0:T(8,128)S(1)}, u32[]{:S(2)}, u32[]{:S(2)}) collective-permute-start(f32[17,8,512]{2,1,0:T(8,128)S(1)} %collective-permute-done.refs_3_), channel_id=1, source_target_pairs={{0,1},{1,0},{2,3},{3,2},{4,5},{5,4},{6,7},{7,6},{8,9},{9,8},{10,11... | collective-permute-start | bytes 835592 | tf_op jit(solution)/shard_map/ppermute | solution.py:535
  23.9 0.1 pad_add_fusion.refs_0_
  24.0 0.0 collective-permute-done.2.refs_5_
  24.0 0.0 collective-permute-done.7.refs_10_
  24.0 0.0 collective-permute-done.4.refs_7_
  24.0 1.1 collective-permute-done.3.refs_6_
  25.1 0.7 copy-done.2
  25.8 11.3 %shard_map.55 = (f32[56,128]{1,0:T(8,128)S(1)}, f32[12,24,512]{2,1,0:T(8,128)S(1)}, f32[12,24,512]{2,1,0:T(8,128)S(1)}, f32[12,24,512]{2,1,0:T(8,128)S(1)}, f32[...) custom-call(s32[2]{0:T(128)S(1)} %pad_add_fusion.refs_0_, ...), custom_call_target="tpu_custom_call" | custom-call | tf_op jit(solution)/shard_map/pallas_call | solution.py:498
  37.1 0.2 collective-permute-start.10
  37.3 4.6 %collective-permute-start.9 = (f32[56,128]{1,0:T(8,128)S(1)}, f32[56,128]{1,0:T(8,128)S(1)}, u32[]{:S(2)}, u32[]{:S(2)}) collective-permute-start(f32[56,128]{1,0:T(8,128)S(1)} %get-tuple-element.30), channel_id=1, source_target_pairs={{0,2},{1,3},{2,0},{3,1},{4,6},{5,7},{6,4},{7,5},{8,10},{9,11},{10,... | collective-permute-start | bytes 86024 | tf_op jit(solution)/shard_map/ppermute | solution.py:535
  41.9 0.0 collective-permute-start.8
  41.9 0.0 collective-permute-done.10
  41.9 2.1 %collective-permute-done.9 = f32[56,128]{1,0:T(8,128)S(1)} collective-permute-done((f32[56,128]{1,0:T(8,128)S(1)}, f32[56,128]{1,0:T(8,128)S(1)}, u32[]{:S(2)}, u32[]{:S(2)}) %collective-permute-start.9) | collective-permute-done | bytes 28704 | tf_op jit(solution)/shard_map/ppermute | solution.py:535
  44.1 0.0 collective-permute-done.8
  44.1 2.5 %collective-permute-start.11 = (f32[4,56,128]{2,1,0:T(8,128)S(1)}, f32[4,56,128]{2,1,0:T(8,128)S(1)}, u32[]{:S(2)}, u32[]{:S(2)}) collective-permute-start(f32[4,56,128]{2,1,0:T(8,128)S(1)} %pad_maximum_fusion.1), channel_id=1, source_target_pairs={{0,4},{4,0},{8,12},{12,8},{16,20},{20,16},{24,28},{28,24},{1,5},{5... | collective-permute-start | bytes 344072 | tf_op jit(solution)/shard_map/ppermute | solution.py:535
  46.6 3.8 %collective-permute-done.11 = f32[4,56,128]{2,1,0:T(8,128)S(1)} collective-permute-done((f32[4,56,128]{2,1,0:T(8,128)S(1)}, f32[4,56,128]{2,1,0:T(8,128)S(1)}, u32[]{:S(2)}, u32[]{:S(2)}) %collective-permute-start.11) | collective-permute-done | bytes 114720 | tf_op jit(solution)/shard_map/ppermute | solution.py:535
  50.5 3.9 %collective-permute-start.14 = (f32[2,4,24,128]{3,2,1,0:T(8,128)S(1)}, f32[2,4,24,128]{3,2,1,0:T(8,128)S(1)}, u32[]{:S(2)}, u32[]{:S(2)}) collective-permute-start(f32[2,4,24,128]{3,2,1,0:T(8,128)S(1)} %pad_maximum_fusion.3.refs_1_), channel_id=1, source_target_pairs={{0,24},{4,28},{8,16},{12,20},{16,8},{20,12},{24,0},{28,4},{1,25},{... | collective-permute-start | bytes 294920 | tf_op jit(solution)/shard_map/ppermute | solution.py:535
  54.4 0.0 collective-permute-start.13
  54.4 0.6 collective-permute-start.12
  55.0 0.7 collective-permute-start.15
  55.7 0.0 collective-permute-done.15.refs_7_
  55.7 2.3 %collective-permute-done.14.refs_4_ = f32[2,4,24,128]{3,2,1,0:T(8,128)S(1)} collective-permute-done((f32[2,4,24,128]{3,2,1,0:T(8,128)S(1)}, f32[2,4,24,128]{3,2,1,0:T(8,128)S(1)}, u32[]{:S(2)}, u32[]{:S(2)}) %collective-permute-start.14) | collective-permute-done | bytes 98336 | tf_op jit(solution)/shard_map/ppermute | solution.py:535
  58.0 5.3 %collective-permute-done.13.refs_3_ = f32[2,4,24,128]{3,2,1,0:T(8,128)S(1)} collective-permute-done((f32[2,4,24,128]{3,2,1,0:T(8,128)S(1)}, f32[2,4,24,128]{3,2,1,0:T(8,128)S(1)}, u32[]{:S(2)}, u32[]{:S(2)}) %collective-permute-start.13) | collective-permute-done | bytes 98336 | tf_op jit(solution)/shard_map/ppermute | solution.py:535
  63.3 7.8 %shard_map.56.refs_11_.refs_19_ = f32[8,8,512]{2,1,0:T(8,128)S(1)} custom-call(s32[2]{0:T(128)S(1)} %pad_add_fusion.refs_0_, f32[2,4,24,128]{3,2,1,0:T(8,128)S(1)} %pad_maximum_fusion.3.refs_1_, f32[2,4,24,128]{3,2,1,0:T(8,128)S(1)} %collective-permute-done.12.refs_2_, f32[2,4,24,128]{3,2,1,0:T(8,128)S(1)} %collective-permute-done.13.refs_3_, ...), custom_call_target="tpu_custom_call" | custom-call | tf_op jit(solution)/shard_map/pallas_call | solution.py:524
  71.1 0.7 collective-permute-start.17
  71.7 3.9 %collective-permute-start.16 = (f32[8,8,512]{2,1,0:T(8,128)S(1)}, f32[8,8,512]{2,1,0:T(8,128)S(1)}, u32[]{:S(2)}, u32[]{:S(2)}) collective-permute-start(f32[8,8,512]{2,1,0:T(8,128)S(1)} %shard_map.56.refs_11_.refs_19_), channel_id=1, source_target_pairs={{0,4},{4,0},{8,12},{12,8},{16,20},{20,16},{24,28},{28,24},{1,5},{5... | collective-permute-start | bytes 393224 | tf_op jit(solution)/shard_map/ppermute | solution.py:535
  75.7 0.7 collective-permute-start.21
  76.4 1.4 %collective-permute-start.18 = (f32[8,8,512]{2,1,0:T(8,128)S(1)}, f32[8,8,512]{2,1,0:T(8,128)S(1)}, u32[]{:S(2)}, u32[]{:S(2)}) collective-permute-start(f32[8,8,512]{2,1,0:T(8,128)S(1)} %shard_map.56.refs_11_.refs_19_), channel_id=1, source_target_pairs={{0,1},{1,0},{2,3},{3,2},{4,5},{5,4},{6,7},{7,6},{8,9},{9,8},{10,11... | collective-permute-start | bytes 393224 | tf_op jit(solution)/shard_map/ppermute | solution.py:535
  77.8 0.0 collective-permute-done.17.refs_13_
  77.8 0.7 collective-permute-start.23
  78.4 1.3 %collective-permute-start.20 = (f32[8,8,512]{2,1,0:T(8,128)S(1)}, f32[8,8,512]{2,1,0:T(8,128)S(1)}, u32[]{:S(2)}, u32[]{:S(2)}) collective-permute-start(f32[8,8,512]{2,1,0:T(8,128)S(1)} %collective-permute-done.17.refs_13_), channel_id=1, source_target_pairs={{0,1},{1,0},{2,3},{3,2},{4,5},{5,4},{6,7},{7,6},{8,9},{9,8},{10,11... | collective-permute-start | bytes 393224 | tf_op jit(solution)/shard_map/ppermute | solution.py:535
  79.8 0.0 collective-permute-done.16.refs_12_
  79.8 0.8 collective-permute-start.22
  80.6 3.1 %collective-permute-start.19 = (f32[8,8,512]{2,1,0:T(8,128)S(1)}, f32[8,8,512]{2,1,0:T(8,128)S(1)}, u32[]{:S(2)}, u32[]{:S(2)}) collective-permute-start(f32[8,8,512]{2,1,0:T(8,128)S(1)} %collective-permute-done.16.refs_12_), channel_id=1, source_target_pairs={{0,1},{1,0},{2,3},{3,2},{4,5},{5,4},{6,7},{7,6},{8,9},{9,8},{10,11... | collective-permute-start | bytes 393224 | tf_op jit(solution)/shard_map/ppermute | solution.py:535
  83.7 0.0 collective-permute-done.18.refs_14_
  83.7 0.0 collective-permute-done.23.refs_19_
  83.7 1.0 collective-permute-done.19.refs_15_
  84.7 12.1 %shard_map.57 = (f32[56,128]{1,0:T(8,128)S(1)}, f32[12,24,512]{2,1,0:T(8,128)S(1)}, f32[12,24,512]{2,1,0:T(8,128)S(1)}, f32[12,24,512]{2,1,0:T(8,128)S(1)}, f32[...) custom-call(s32[2]{0:T(128)S(1)} %pad_add_fusion.refs_0_, ...), custom_call_target="tpu_custom_call" | custom-call | tf_op jit(solution)/shard_map/pallas_call | solution.py:498
  96.8 0.1 collective-permute-start.26
  96.9 3.1 %collective-permute-start.25 = (f32[56,128]{1,0:T(8,128)S(1)}, f32[56,128]{1,0:T(8,128)S(1)}, u32[]{:S(2)}, u32[]{:S(2)}) collective-permute-start(f32[56,128]{1,0:T(8,128)S(1)} %get-tuple-element.43), channel_id=1, source_target_pairs={{0,2},{1,3},{2,0},{3,1},{4,6},{5,7},{6,4},{7,5},{8,10},{9,11},{10,... | collective-permute-start | bytes 86024 | tf_op jit(solution)/shard_map/ppermute | solution.py:535
  99.9 0.0 collective-permute-start.24
  100.0 0.2 collective-permute-done.26
  100.1 1.9 %collective-permute-done.25 = f32[56,128]{1,0:T(8,128)S(1)} collective-permute-done((f32[56,128]{1,0:T(8,128)S(1)}, f32[56,128]{1,0:T(8,128)S(1)}, u32[]{:S(2)}, u32[]{:S(2)}) %collective-permute-start.25) | collective-permute-done | bytes 28704 | tf_op jit(solution)/shard_map/ppermute | solution.py:535
  102.0 3.0 %collective-permute-start.27 = (f32[4,56,128]{2,1,0:T(8,128)S(1)}, f32[4,56,128]{2,1,0:T(8,128)S(1)}, u32[]{:S(2)}, u32[]{:S(2)}) collective-permute-start(f32[4,56,128]{2,1,0:T(8,128)S(1)} %pad_maximum_fusion.2), channel_id=1, source_target_pairs={{0,4},{4,0},{8,12},{12,8},{16,20},{20,16},{24,28},{28,24},{1,5},{5... | collective-permute-start | bytes 344072 | tf_op jit(solution)/shard_map/ppermute | solution.py:535
  105.1 2.8 %collective-permute-done.27 = f32[4,56,128]{2,1,0:T(8,128)S(1)} collective-permute-done((f32[4,56,128]{2,1,0:T(8,128)S(1)}, f32[4,56,128]{2,1,0:T(8,128)S(1)}, u32[]{:S(2)}, u32[]{:S(2)}) %collective-permute-start.27) | collective-permute-done | bytes 114720 | tf_op jit(solution)/shard_map/ppermute | solution.py:535
  107.9 3.9 %collective-permute-start.30 = (f32[2,4,24,128]{3,2,1,0:T(8,128)S(1)}, f32[2,4,24,128]{3,2,1,0:T(8,128)S(1)}, u32[]{:S(2)}, u32[]{:S(2)}) collective-permute-start(f32[2,4,24,128]{3,2,1,0:T(8,128)S(1)} %pad_maximum_fusion.4.refs_1_), channel_id=1, source_target_pairs={{0,24},{4,28},{8,16},{12,20},{16,8},{20,12},{24,0},{28,4},{1,25},{... | collective-permute-start | bytes 294920 | tf_op jit(solution)/shard_map/ppermute | solution.py:535
  111.8 0.6 collective-permute-start.28
  112.5 0.7 collective-permute-start.31
  113.2 1.9 %collective-permute-done.30.refs_4_ = f32[2,4,24,128]{3,2,1,0:T(8,128)S(1)} collective-permute-done((f32[2,4,24,128]{3,2,1,0:T(8,128)S(1)}, f32[2,4,24,128]{3,2,1,0:T(8,128)S(1)}, u32[]{:S(2)}, u32[]{:S(2)}) %collective-permute-start.30) | collective-permute-done | bytes 98336 | tf_op jit(solution)/shard_map/ppermute | solution.py:535
  115.1 5.4 %collective-permute-done.29.refs_3_ = f32[2,4,24,128]{3,2,1,0:T(8,128)S(1)} collective-permute-done((f32[2,4,24,128]{3,2,1,0:T(8,128)S(1)}, f32[2,4,24,128]{3,2,1,0:T(8,128)S(1)}, u32[]{:S(2)}, u32[]{:S(2)}) %collective-permute-start.29) | collective-permute-done | bytes 98336 | tf_op jit(solution)/shard_map/ppermute | solution.py:535
  120.5 8.4 %shard_map.58 = f32[8,8,512]{2,1,0:T(8,128)} custom-call(s32[2]{0:T(128)S(1)} %pad_add_fusion.refs_0_, f32[2,4,24,128]{3,2,1,0:T(8,128)S(1)} %pad_maximum_fusion.4.refs_1_, f32[2,4,24,128]{3,2,1,0:T(8,128)S(1)} %collective-permute-done.28.refs_2_, f32[2,4,24,128]{3,2,1,0:T(8,128)S(1)} %collective-permute-done.29.refs_3_, ...), custom_call_target="tpu_custom_call" | custom-call | tf_op jit(solution)/shard_map/pallas_call | solution.py:524
  (26 shorter events, 0.1 us)
Async XLA Ops:
  2.7 10.0 %collective-permute-start.1 = (f32[17,8,512]{2,1,0:T(8,128)S(1)}, f32[17,8,512]{2,1,0:T(8,128)S(1)}, u32[]{:S(2)}, u32[]{:S(2)}) collective-permute-start(f32[17,8,512]{2,1,0:T(8,128)S(1)} %pad_maximum_fusion.refs_2_), channel_id=1, source_target_pairs={{4,8},{12,16},{20,24},{8,4},{16,12},{24,20},{5,9},{13,17},{21,25},... | collective-permute-start | bytes 835592 | tf_op jit(solution)/shard_map/ppermute | solution.py:541
  3.3 17.0 %collective-permute-start = (f32[17,8,512]{2,1,0:T(8,128)S(1)}, f32[17,8,512]{2,1,0:T(8,128)S(1)}, u32[]{:S(2)}, u32[]{:S(2)}) collective-permute-start(f32[17,8,512]{2,1,0:T(8,128)S(1)} %pad_maximum_fusion.refs_2_), channel_id=1, source_target_pairs={{0,4},{4,0},{8,12},{12,8},{16,20},{20,16},{24,28},{28,24},{1,5},{5... | collective-permute-start | bytes 835592 | tf_op jit(solution)/shard_map/ppermute | solution.py:535
  9.1 11.9 %collective-permute-start.5 = (f32[17,8,512]{2,1,0:T(8,128)S(1)}, f32[17,8,512]{2,1,0:T(8,128)S(1)}, u32[]{:S(2)}, u32[]{:S(2)}) collective-permute-start(f32[17,8,512]{2,1,0:T(8,128)S(1)} %pad_maximum_fusion.refs_2_), channel_id=1, source_target_pairs={{1,2},{2,1},{5,6},{6,5},{9,10},{10,9},{13,14},{14,13},{17,18},{18,... | collective-permute-start | bytes 835592 | tf_op jit(solution)/shard_map/ppermute | solution.py:541
  9.8 14.2 %collective-permute-start.2 = (f32[17,8,512]{2,1,0:T(8,128)S(1)}, f32[17,8,512]{2,1,0:T(8,128)S(1)}, u32[]{:S(2)}, u32[]{:S(2)}) collective-permute-start(f32[17,8,512]{2,1,0:T(8,128)S(1)} %pad_maximum_fusion.refs_2_), channel_id=1, source_target_pairs={{0,1},{1,0},{2,3},{3,2},{4,5},{5,4},{6,7},{7,6},{8,9},{9,8},{10,11... | collective-permute-start | bytes 835592 | tf_op jit(solution)/shard_map/ppermute | solution.py:535
  12.7 11.3 %collective-permute-start.7 = (f32[17,8,512]{2,1,0:T(8,128)S(1)}, f32[17,8,512]{2,1,0:T(8,128)S(1)}, u32[]{:S(2)}, u32[]{:S(2)}) collective-permute-start(f32[17,8,512]{2,1,0:T(8,128)S(1)} %collective-permute-done.1.refs_4_), channel_id=1, source_target_pairs={{1,2},{2,1},{5,6},{6,5},{9,10},{10,9},{13,14},{14,13},{17,18},{18,... | collective-permute-start | bytes 835592 | tf_op jit(solution)/shard_map/ppermute | solution.py:541
  13.4 10.6 %collective-permute-start.4 = (f32[17,8,512]{2,1,0:T(8,128)S(1)}, f32[17,8,512]{2,1,0:T(8,128)S(1)}, u32[]{:S(2)}, u32[]{:S(2)}) collective-permute-start(f32[17,8,512]{2,1,0:T(8,128)S(1)} %collective-permute-done.1.refs_4_), channel_id=1, source_target_pairs={{0,1},{1,0},{2,3},{3,2},{4,5},{5,4},{6,7},{7,6},{8,9},{9,8},{10,11... | collective-permute-start | bytes 835592 | tf_op jit(solution)/shard_map/ppermute | solution.py:535
  20.3 3.7 %collective-permute-start.6 = (f32[17,8,512]{2,1,0:T(8,128)S(1)}, f32[17,8,512]{2,1,0:T(8,128)S(1)}, u32[]{:S(2)}, u32[]{:S(2)}) collective-permute-start(f32[17,8,512]{2,1,0:T(8,128)S(1)} %collective-permute-done.refs_3_), channel_id=1, source_target_pairs={{1,2},{2,1},{5,6},{6,5},{9,10},{10,9},{13,14},{14,13},{17,18},{18,... | collective-permute-start | bytes 835592 | tf_op jit(solution)/shard_map/ppermute | solution.py:541
  21.0 4.1 %collective-permute-start.3 = (f32[17,8,512]{2,1,0:T(8,128)S(1)}, f32[17,8,512]{2,1,0:T(8,128)S(1)}, u32[]{:S(2)}, u32[]{:S(2)}) collective-permute-start(f32[17,8,512]{2,1,0:T(8,128)S(1)} %collective-permute-done.refs_3_), channel_id=1, source_target_pairs={{0,1},{1,0},{2,3},{3,2},{4,5},{5,4},{6,7},{7,6},{8,9},{9,8},{10,11... | collective-permute-start | bytes 835592 | tf_op jit(solution)/shard_map/ppermute | solution.py:535
  24.0 39.3 %copy-start.1 = (f32[8,8,512]{2,1,0:T(8,128)S(1)}, f32[8,8,512]{2,1,0:T(8,128)}, u32[]{:S(2)}) copy-start(f32[8,8,512]{2,1,0:T(8,128)} %refs_19_.1) | copy-start | bytes 393220
  25.1 0.7 copy-start.2
  37.1 34.0 %copy-start = (f32[24,3,8,512]{3,2,1,0:T(8,128)}, f32[24,3,8,512]{3,2,1,0:T(8,128)S(1)}, u32[]{:S(2)}) copy-start(f32[24,3,8,512]{3,2,1,0:T(8,128)S(1)} %get-tuple-element.42.refs_20_) | copy-start | bytes 3538948
  37.1 4.8 %collective-permute-start.10 = (f32[56,128]{1,0:T(8,128)S(1)}, f32[56,128]{1,0:T(8,128)S(1)}, u32[]{:S(2)}, u32[]{:S(2)}) collective-permute-start(f32[56,128]{1,0:T(8,128)S(1)} %get-tuple-element.30), channel_id=1, source_target_pairs={{0,3},{1,2},{2,1},{3,0},{4,7},{5,6},{6,5},{7,4},{8,11},{9,10},{10,... | collective-permute-start | bytes 86024 | tf_op jit(solution)/shard_map/ppermute | solution.py:535
  37.3 6.7 %collective-permute-start.9 = (f32[56,128]{1,0:T(8,128)S(1)}, f32[56,128]{1,0:T(8,128)S(1)}, u32[]{:S(2)}, u32[]{:S(2)}) collective-permute-start(f32[56,128]{1,0:T(8,128)S(1)} %get-tuple-element.30), channel_id=1, source_target_pairs={{0,2},{1,3},{2,0},{3,1},{4,6},{5,7},{6,4},{7,5},{8,10},{9,11},{10,... | collective-permute-start | bytes 86024 | tf_op jit(solution)/shard_map/ppermute | solution.py:535
  41.9 2.2 %collective-permute-start.8 = (f32[56,128]{1,0:T(8,128)S(1)}, f32[56,128]{1,0:T(8,128)S(1)}, u32[]{:S(2)}, u32[]{:S(2)}) collective-permute-start(f32[56,128]{1,0:T(8,128)S(1)} %get-tuple-element.30), channel_id=1, source_target_pairs={{0,1},{1,0},{2,3},{3,2},{4,5},{5,4},{6,7},{7,6},{8,9},{9,8},{10,11... | collective-permute-start | bytes 86024 | tf_op jit(solution)/shard_map/ppermute | solution.py:535
  44.1 6.4 %collective-permute-start.11 = (f32[4,56,128]{2,1,0:T(8,128)S(1)}, f32[4,56,128]{2,1,0:T(8,128)S(1)}, u32[]{:S(2)}, u32[]{:S(2)}) collective-permute-start(f32[4,56,128]{2,1,0:T(8,128)S(1)} %pad_maximum_fusion.1), channel_id=1, source_target_pairs={{0,4},{4,0},{8,12},{12,8},{16,20},{20,16},{24,28},{28,24},{1,5},{5... | collective-permute-start | bytes 344072 | tf_op jit(solution)/shard_map/ppermute | solution.py:535
  50.5 7.5 %collective-permute-start.14 = (f32[2,4,24,128]{3,2,1,0:T(8,128)S(1)}, f32[2,4,24,128]{3,2,1,0:T(8,128)S(1)}, u32[]{:S(2)}, u32[]{:S(2)}) collective-permute-start(f32[2,4,24,128]{3,2,1,0:T(8,128)S(1)} %pad_maximum_fusion.3.refs_1_), channel_id=1, source_target_pairs={{0,24},{4,28},{8,16},{12,20},{16,8},{20,12},{24,0},{28,4},{1,25},{... | collective-permute-start | bytes 294920 | tf_op jit(solution)/shard_map/ppermute | solution.py:535
  54.4 8.9 %collective-permute-start.13 = (f32[2,4,24,128]{3,2,1,0:T(8,128)S(1)}, f32[2,4,24,128]{3,2,1,0:T(8,128)S(1)}, u32[]{:S(2)}, u32[]{:S(2)}) collective-permute-start(f32[2,4,24,128]{3,2,1,0:T(8,128)S(1)} %pad_maximum_fusion.3.refs_1_), channel_id=1, source_target_pairs={{0,16},{4,20},{8,24},{12,28},{16,0},{20,4},{24,8},{28,12},{1,17},{... | collective-permute-start | bytes 294920 | tf_op jit(solution)/shard_map/ppermute | solution.py:535
  54.4 8.9 %collective-permute-start.12 = (f32[2,4,24,128]{3,2,1,0:T(8,128)S(1)}, f32[2,4,24,128]{3,2,1,0:T(8,128)S(1)}, u32[]{:S(2)}, u32[]{:S(2)}) collective-permute-start(f32[2,4,24,128]{3,2,1,0:T(8,128)S(1)} %pad_maximum_fusion.3.refs_1_), channel_id=1, source_target_pairs={{0,8},{4,12},{8,0},{12,4},{16,24},{20,28},{24,16},{28,20},{1,9},{5... | collective-permute-start | bytes 294920 | tf_op jit(solution)/shard_map/ppermute | solution.py:535
  55.0 0.7 collective-permute-start.15
  71.1 6.7 %collective-permute-start.17 = (f32[8,8,512]{2,1,0:T(8,128)S(1)}, f32[8,8,512]{2,1,0:T(8,128)S(1)}, u32[]{:S(2)}, u32[]{:S(2)}) collective-permute-start(f32[8,8,512]{2,1,0:T(8,128)S(1)} %shard_map.56.refs_11_.refs_19_), channel_id=1, source_target_pairs={{4,8},{12,16},{20,24},{8,4},{16,12},{24,20},{5,9},{13,17},{21,25},... | collective-permute-start | bytes 393224 | tf_op jit(solution)/shard_map/ppermute | solution.py:541
  71.7 8.0 %collective-permute-start.16 = (f32[8,8,512]{2,1,0:T(8,128)S(1)}, f32[8,8,512]{2,1,0:T(8,128)S(1)}, u32[]{:S(2)}, u32[]{:S(2)}) collective-permute-start(f32[8,8,512]{2,1,0:T(8,128)S(1)} %shard_map.56.refs_11_.refs_19_), channel_id=1, source_target_pairs={{0,4},{4,0},{8,12},{12,8},{16,20},{20,16},{24,28},{28,24},{1,5},{5... | collective-permute-start | bytes 393224 | tf_op jit(solution)/shard_map/ppermute | solution.py:535
  75.7 4.9 %collective-permute-start.21 = (f32[8,8,512]{2,1,0:T(8,128)S(1)}, f32[8,8,512]{2,1,0:T(8,128)S(1)}, u32[]{:S(2)}, u32[]{:S(2)}) collective-permute-start(f32[8,8,512]{2,1,0:T(8,128)S(1)} %shard_map.56.refs_11_.refs_19_), channel_id=1, source_target_pairs={{1,2},{2,1},{5,6},{6,5},{9,10},{10,9},{13,14},{14,13},{17,18},{18,... | collective-permute-start | bytes 393224 | tf_op jit(solution)/shard_map/ppermute | solution.py:541
  76.4 7.3 %collective-permute-start.18 = (f32[8,8,512]{2,1,0:T(8,128)S(1)}, f32[8,8,512]{2,1,0:T(8,128)S(1)}, u32[]{:S(2)}, u32[]{:S(2)}) collective-permute-start(f32[8,8,512]{2,1,0:T(8,128)S(1)} %shard_map.56.refs_11_.refs_19_), channel_id=1, source_target_pairs={{0,1},{1,0},{2,3},{3,2},{4,5},{5,4},{6,7},{7,6},{8,9},{9,8},{10,11... | collective-permute-start | bytes 393224 | tf_op jit(solution)/shard_map/ppermute | solution.py:535
  77.8 6.0 %collective-permute-start.23 = (f32[8,8,512]{2,1,0:T(8,128)S(1)}, f32[8,8,512]{2,1,0:T(8,128)S(1)}, u32[]{:S(2)}, u32[]{:S(2)}) collective-permute-start(f32[8,8,512]{2,1,0:T(8,128)S(1)} %collective-permute-done.17.refs_13_), channel_id=1, source_target_pairs={{1,2},{2,1},{5,6},{6,5},{9,10},{10,9},{13,14},{14,13},{17,18},{18,... | collective-permute-start | bytes 393224 | tf_op jit(solution)/shard_map/ppermute | solution.py:541
  78.4 5.3 %collective-permute-start.20 = (f32[8,8,512]{2,1,0:T(8,128)S(1)}, f32[8,8,512]{2,1,0:T(8,128)S(1)}, u32[]{:S(2)}, u32[]{:S(2)}) collective-permute-start(f32[8,8,512]{2,1,0:T(8,128)S(1)} %collective-permute-done.17.refs_13_), channel_id=1, source_target_pairs={{0,1},{1,0},{2,3},{3,2},{4,5},{5,4},{6,7},{7,6},{8,9},{9,8},{10,11... | collective-permute-start | bytes 393224 | tf_op jit(solution)/shard_map/ppermute | solution.py:535
  79.8 3.9 %collective-permute-start.22 = (f32[8,8,512]{2,1,0:T(8,128)S(1)}, f32[8,8,512]{2,1,0:T(8,128)S(1)}, u32[]{:S(2)}, u32[]{:S(2)}) collective-permute-start(f32[8,8,512]{2,1,0:T(8,128)S(1)} %collective-permute-done.16.refs_12_), channel_id=1, source_target_pairs={{1,2},{2,1},{5,6},{6,5},{9,10},{10,9},{13,14},{14,13},{17,18},{18,... | collective-permute-start | bytes 393224 | tf_op jit(solution)/shard_map/ppermute | solution.py:541
  80.6 4.1 %collective-permute-start.19 = (f32[8,8,512]{2,1,0:T(8,128)S(1)}, f32[8,8,512]{2,1,0:T(8,128)S(1)}, u32[]{:S(2)}, u32[]{:S(2)}) collective-permute-start(f32[8,8,512]{2,1,0:T(8,128)S(1)} %collective-permute-done.16.refs_12_), channel_id=1, source_target_pairs={{0,1},{1,0},{2,3},{3,2},{4,5},{5,4},{6,7},{7,6},{8,9},{9,8},{10,11... | collective-permute-start | bytes 393224 | tf_op jit(solution)/shard_map/ppermute | solution.py:535
  96.8 3.4 %collective-permute-start.26 = (f32[56,128]{1,0:T(8,128)S(1)}, f32[56,128]{1,0:T(8,128)S(1)}, u32[]{:S(2)}, u32[]{:S(2)}) collective-permute-start(f32[56,128]{1,0:T(8,128)S(1)} %get-tuple-element.43), channel_id=1, source_target_pairs={{0,3},{1,2},{2,1},{3,0},{4,7},{5,6},{6,5},{7,4},{8,11},{9,10},{10,... | collective-permute-start | bytes 86024 | tf_op jit(solution)/shard_map/ppermute | solution.py:535
  96.9 5.2 %collective-permute-start.25 = (f32[56,128]{1,0:T(8,128)S(1)}, f32[56,128]{1,0:T(8,128)S(1)}, u32[]{:S(2)}, u32[]{:S(2)}) collective-permute-start(f32[56,128]{1,0:T(8,128)S(1)} %get-tuple-element.43), channel_id=1, source_target_pairs={{0,2},{1,3},{2,0},{3,1},{4,6},{5,7},{6,4},{7,5},{8,10},{9,11},{10,... | collective-permute-start | bytes 86024 | tf_op jit(solution)/shard_map/ppermute | solution.py:535
  99.9 2.1 %collective-permute-start.24 = (f32[56,128]{1,0:T(8,128)S(1)}, f32[56,128]{1,0:T(8,128)S(1)}, u32[]{:S(2)}, u32[]{:S(2)}) collective-permute-start(f32[56,128]{1,0:T(8,128)S(1)} %get-tuple-element.43), channel_id=1, source_target_pairs={{0,1},{1,0},{2,3},{3,2},{4,5},{5,4},{6,7},{7,6},{8,9},{9,8},{10,11... | collective-permute-start | bytes 86024 | tf_op jit(solution)/shard_map/ppermute | solution.py:535
  102.0 5.9 %collective-permute-start.27 = (f32[4,56,128]{2,1,0:T(8,128)S(1)}, f32[4,56,128]{2,1,0:T(8,128)S(1)}, u32[]{:S(2)}, u32[]{:S(2)}) collective-permute-start(f32[4,56,128]{2,1,0:T(8,128)S(1)} %pad_maximum_fusion.2), channel_id=1, source_target_pairs={{0,4},{4,0},{8,12},{12,8},{16,20},{20,16},{24,28},{28,24},{1,5},{5... | collective-permute-start | bytes 344072 | tf_op jit(solution)/shard_map/ppermute | solution.py:535
  107.9 7.2 %collective-permute-start.30 = (f32[2,4,24,128]{3,2,1,0:T(8,128)S(1)}, f32[2,4,24,128]{3,2,1,0:T(8,128)S(1)}, u32[]{:S(2)}, u32[]{:S(2)}) collective-permute-start(f32[2,4,24,128]{3,2,1,0:T(8,128)S(1)} %pad_maximum_fusion.4.refs_1_), channel_id=1, source_target_pairs={{0,24},{4,28},{8,16},{12,20},{16,8},{20,12},{24,0},{28,4},{1,25},{... | collective-permute-start | bytes 294920 | tf_op jit(solution)/shard_map/ppermute | solution.py:535
  111.8 8.7 %collective-permute-start.29 = (f32[2,4,24,128]{3,2,1,0:T(8,128)S(1)}, f32[2,4,24,128]{3,2,1,0:T(8,128)S(1)}, u32[]{:S(2)}, u32[]{:S(2)}) collective-permute-start(f32[2,4,24,128]{3,2,1,0:T(8,128)S(1)} %pad_maximum_fusion.4.refs_1_), channel_id=1, source_target_pairs={{0,16},{4,20},{8,24},{12,28},{16,0},{20,4},{24,8},{28,12},{1,17},{... | collective-permute-start | bytes 294920 | tf_op jit(solution)/shard_map/ppermute | solution.py:535
  111.8 8.7 %collective-permute-start.28 = (f32[2,4,24,128]{3,2,1,0:T(8,128)S(1)}, f32[2,4,24,128]{3,2,1,0:T(8,128)S(1)}, u32[]{:S(2)}, u32[]{:S(2)}) collective-permute-start(f32[2,4,24,128]{3,2,1,0:T(8,128)S(1)} %pad_maximum_fusion.4.refs_1_), channel_id=1, source_target_pairs={{0,8},{4,12},{8,0},{12,4},{16,24},{20,28},{24,16},{28,20},{1,9},{5... | collective-permute-start | bytes 294920 | tf_op jit(solution)/shard_map/ppermute | solution.py:535
  112.5 0.7 collective-permute-start.31

commit v4 on v3

--- a/solution.py
+++ b/solution.py
@@ -263,45 +263,57 @@
     lax.fori_loop(0, zl // 2 + 5, keep1, 0, unroll=3)
 
 
-def solve_blocks(rhs, store, across, vertical, scratch, answer):
-    count = rhs.shape[0]
-    sub = lax.broadcasted_iota(jnp.int32, (8, 128), 0)
-    lane = lax.broadcasted_iota(jnp.int32, (8, 128), 1)
-    real = (sub & 1) == 0
-    same = lane == sub
-
-    def forward(b, before):
-        here_x = jnp.where(real, across[b], 0.0)
-        next_x = jnp.where(real, across[b + 1], 0.0)
-        low = jnp.where(real, vertical[b], 0.0)
-        high = roll(low, -2, 0)
-        diagonal = jnp.where(real, store[b] + here_x + next_x + low + high, 1.0)
-        m = jnp.where(same, diagonal, 0.0)
-        m = m - jnp.where(lane == sub - 2, low, 0.0) - jnp.where(lane == sub + 2, high, 0.0)
-        m = m - jnp.where(lane == sub + 8, next_x, 0.0)
-        m = m + jnp.where(jnp.logical_and(lane == 16, real), rhs[b], 0.0)
-        carried = jnp.where(lane < 8, roll(before, -8, 1), jnp.where(lane == 16, before, 0.0))
-        m = m + here_x * carried
-        for z in range(0, 8, 2):
-            row = m[z : z + 1, :]
-            row = row / row[:, z : z + 1]
-            m = jnp.where(sub == z, row, m - m[:, z : z + 1] * row)
-        scratch[b] = m
-        return m
-
-    lax.fori_loop(0, count, forward, jnp.zeros((8, 128), jnp.float32))
-
-    def backward(i, above):
-        b = count - 1 - i
-        m = scratch[b]
-        row = jnp.sum(jnp.where(lane == sub + 8, above, 0.0), axis=0, keepdims=True)
-        mask = jnp.logical_and(lane >= 8, lane < 16)
-        taken = jnp.where(lane == 16, m, 0.0) - jnp.where(mask, m * row, 0.0)
-        value = jnp.broadcast_to(jnp.sum(taken, axis=1, keepdims=True), (8, 128))
-        answer[b] = jnp.where(real, value, roll(value, 1, 0))
-        return value
-
-    lax.fori_loop(0, count, backward, jnp.zeros((8, 128), jnp.float32))
+def solve_blocks(block, factors, answer, strips, slabs):
+    zero = jnp.zeros((1, 128), jnp.float32)
+
+    def entry(kind, b, z):
+        return block[kind, b, 2 * z : 2 * z + 1, :]
+
+    pairs = [(i, j) for i in range(slabs) for j in range(i, slabs)]
+
+    def forward(b, carry):
+        a = dict(zip(pairs, carry[: len(pairs)]))
+        r = list(carry[len(pairs) :]) + [zero] * slabs
+        for z in range(slabs):
+            here, after = entry(2, b, z), entry(2, b + 1, z)
+            low = entry(3, b, z)
+            high = entry(3, b, z + 1) if z + 1 < slabs else zero
+            a[z, z] = a[z, z] + (entry(1, b, z) + here + after + low + high)
+            if z + 1 < slabs:
+                a[z, z + 1] = a[z, z + 1] - high
+            a[z, slabs + z] = -after
+            r[z] = r[z] + entry(0, b, z)
+        for i in range(slabs):
+            inverse = 1.0 / a[i, i]
+            others = list(range(i + 1, slabs + i + 1))
+            scaled = [a[i, j] * inverse if (i, j) in a else None for j in others]
+            for n, j in enumerate(others):
+                if scaled[n] is None:
+                    continue
+                for k in others[n:]:
+                    if (i, k) in a:
+                        a[j, k] = a.get((j, k), zero) - scaled[n] * a[i, k]
+                r[j] = r[j] - scaled[n] * r[i]
+                factors[b, i * (slabs + 1) + n] = scaled[n]
+            factors[b, i * (slabs + 1) + slabs] = r[i] * inverse
+        nexts = [a.get((slabs + i, slabs + j), zero) for i, j in pairs]
+        return tuple(nexts + r[slabs:])
+
+    unroll = strips if strips <= 8 else 1
+    lax.fori_loop(0, strips, forward, (zero,) * (len(pairs) + slabs), unroll=unroll)
+
+    def backward(n, above):
+        b = strips - 1 - n
+        x = [None] * slabs + list(above)
+        for i in reversed(range(slabs)):
+            value = factors[b, i * (slabs + 1) + slabs]
+            for n, j in enumerate(range(i + 1, slabs + i + 1)):
+                value = value - factors[b, i * (slabs + 1) + n] * x[j]
+            x[i] = value
+            answer[b, 2 * i : 2 * i + 2, :] = jnp.broadcast_to(value, (2, 128))
+        return tuple(x[:slabs])
+
+    lax.fori_loop(0, strips, backward, (zero,) * slabs, unroll=unroll)
 
 
 def up_kernel(slabs, strips, zl, xl, counts, *refs):
@@ -311,7 +323,7 @@
     e0_in, src0, inv0, fx0, fy0, fz0 = refs[:6]
     src1, inv1, fx1, fy1, fz1 = refs[6:11]
     head_ref, out_ref = refs[11], refs[12]
-    a2, block, answer, e2, picked, wide, e1, e0 = refs[13:]
+    a2, block, factors, answer, e2, picked, wide, e1, e0 = refs[13:]
     strip, slab = where_ref[0], where_ref[1]
     x2, z2 = xl // 4, zl // 4
     rows2 = strips * x2
@@ -370,9 +382,7 @@
     block[2, 0:strips] = blocks(fx, False, True)
     block[2, strips] = jnp.zeros((8, 128), jnp.float32)
     block[3, 0:strips] = blocks(fz, True, False)
-    solve_blocks(
-        block.at[0, 0:strips], block.at[1], block.at[2], block.at[3], block.at[4], answer
-    )
+    solve_blocks(block, factors, answer, strips, slabs)
     add = jnp.broadcast_to(answer[...][:, None], (strips, x2, 8, 128)).reshape(shape)
     e = e + add
     e = jnp.where(even, (source + sum2(e)) * inverse, e)
@@ -473,6 +483,15 @@
         out_ref[z] = head_ref[z] + e0[z + 2][xl : 2 * xl]
 
 
+def lay_kernel(head_ref, soil_ref, land_ref, sun_ref, out_ref):
+    zl = head_ref.shape[0]
+    out_ref[0:zl] = head_ref[...]
+    out_ref[zl : 2 * zl] = soil_ref[...].astype(jnp.float32)
+    hour = sun_ref[...].astype(jnp.float32)
+    sun_share = jnp.maximum(0.0, jnp.sin(math.pi * (hour - 6.0) / 12.0))
+    out_ref[2 * zl] = ET_PEAK * sun_share * land_ref[...].astype(jnp.float32)
+
+
 VMEM = pl.BlockSpec(memory_space=pltpu.VMEM)
 SMEM = pl.BlockSpec(memory_space=pltpu.SMEM)
 
@@ -513,7 +532,8 @@
     n = -(-9 * x2 * z2 // 8) * 8
     scratch = [
         pltpu.VMEM((5, strips * x2, 8, 128), jnp.float32),
-        pltpu.VMEM((5, strips + 1, 8, 128), jnp.float32),
+        pltpu.VMEM((4, strips + 1, 8, 128), jnp.float32),
+        pltpu.VMEM((strips, slabs * (slabs + 1), 1, 128), jnp.float32),
         pltpu.VMEM((strips, 8, 128), jnp.float32),
         pltpu.VMEM(((strips + 2) * x2, 24, 128), jnp.float32),
         pltpu.VMEM((n, ny // 4), jnp.float32),
@@ -562,9 +582,12 @@
     zl, xl, ny = head_old.shape
     strips, slabs = lax.axis_size("xy"), lax.axis_size("gz")
     where = jnp.stack([lax.axis_index("xy"), lax.axis_index("gz")]).astype(jnp.int32)
-    sun_share = jnp.maximum(0.0, jnp.sin(math.pi * (sun_bin.astype(jnp.float32) - 6.0) / 12.0))
-    forcing = ET_PEAK * sun_share * land_mask.astype(jnp.float32)
-    own = jnp.concatenate([head_old, soil_type.astype(jnp.float32), forcing[None]])
+    own = pl.pallas_call(
+        lay_kernel,
+        out_shape=f32(2 * zl + 1, xl, ny),
+        in_specs=[VMEM] * 4,
+        out_specs=VMEM,
+    )(head_old, soil_type, land_mask, sun_bin)
     state = neighbourhood(own)
     sizes = (slabs, strips, zl, xl, ny)
     base = -(-5 * (xl // 4) * (zl // 4) // 8) * 8

time: 129 us -> 124 us (0.961)
  Pallas kernels: 39.6 us -> 34.3 us
  other arithmetic: 2.77 us -> 0.12 us
  local copies, waits for them, and re-layouts: 0.73 us -> 2.73 us
    pallas_call x2, Pallas kernels: 16.2 us -> 9.09 us  [up(): pl.pallas_call(functools.partial(up_kernel, slabs, strips, zl, xl, counts...]
    unnamed x6 -> x10, local copies, waits for them, and re-layouts: 0.69 us -> 2.69 us
    pallas_call x0 -> x1, Pallas kernels: none -> 1.78 us  [per_device(): pl.pallas_call(lay_kernel, out_shape=f32(2 * zl + 1, xl, ny), in_specs=[V...]
where the time goes in v4:
time: 124 us; the launch traced here: 123 us
  starting transfers between devices  52 us (42%)
  Pallas kernels  34.3 us (28%)
  waiting for transfers between devices  33.8 us (27%)
  local copies, waits for them, and re-layouts  2.73 us (2%)
    ppermute x22, starting transfers between devices, swapped(): lax.ppermute(x, axis, [(i, i ^ mask) for i in range(lax.axis_size(axis))])  45.2 us
    ppermute x22, waiting for transfers between devices, swapped(): lax.ppermute(x, axis, [(i, i ^ mask) for i in range(lax.axis_size(axis))])  33.7 us
    pallas_call x2, Pallas kernels, down(): pl.pallas_call(functools.partial(down_kernel, first, slabs, strips, zl, x...  23.4 us
    pallas_call x2, Pallas kernels, up(): pl.pallas_call(functools.partial(up_kernel, slabs, strips, zl, xl, counts...  9.09 us
    ppermute x10, starting transfers between devices, odd_pairs(): return lax.ppermute(x, axis, pairs + [(j, i) for i, j in pairs])  6.79 us
    unnamed x10, local copies, waits for them, and re-layouts  2.69 us
  transfers between devices with their start and end apart: 32, of which 12 were waited for; matrix products, arithmetic and copies ran while one was open for 0% of the time, Pallas kernels for 0%

profile of v4, /device:TPU:0, one launch (start us, length us, event | category | flops | bytes accessed | tf_op | source)
XLA Modules:
  0.0 123.1 jit_solution(10236166072734544655)
XLA Ops:
  0.0 1.8 %shard_map.55.refs_2_ = f32[17,8,512]{2,1,0:T(8,128)} custom-call(f32[8,8,512]{2,1,0:T(8,128)} %refs_19_.1, s32[8,8,512]{2,1,0:T(8,128)} %soil_ref.1, s32[8,512]{1,0:T(8,128)} %land_ref.1, s32[8,512]{1,0:T(8,128)} %sun_ref.1), custom_call_target="tpu_custom_call" | custom-call | tf_op jit(solution)/shard_map/pallas_call | solution.py:585
  1.8 0.7 collective-permute-start.1
  2.5 5.8 %collective-permute-start = (f32[17,8,512]{2,1,0:T(8,128)}, f32[17,8,512]{2,1,0:T(8,128)S(1)}, u32[]{:S(2)}, u32[]{:S(2)}) collective-permute-start(f32[17,8,512]{2,1,0:T(8,128)} %shard_map.55.refs_2_), channel_id=1, source_target_pairs={{0,4},{4,0},{8,12},{12,8},{16,20},{20,16},{24,28},{28,24},{1,5},{5... | collective-permute-start | bytes 835592 | tf_op jit(solution)/shard_map/ppermute | solution.py:555
  8.2 0.7 collective-permute-start.5
  8.9 2.9 %collective-permute-start.2 = (f32[17,8,512]{2,1,0:T(8,128)}, f32[17,8,512]{2,1,0:T(8,128)S(1)}, u32[]{:S(2)}, u32[]{:S(2)}) collective-permute-start(f32[17,8,512]{2,1,0:T(8,128)} %shard_map.55.refs_2_), channel_id=1, source_target_pairs={{0,1},{1,0},{2,3},{3,2},{4,5},{5,4},{6,7},{7,6},{8,9},{9,8},{10,11... | collective-permute-start | bytes 835592 | tf_op jit(solution)/shard_map/ppermute | solution.py:555
  11.8 0.0 collective-permute-done.1.refs_4_
  11.8 0.7 collective-permute-start.7
  12.5 1.3 %collective-permute-start.4 = (f32[17,8,512]{2,1,0:T(8,128)S(1)}, f32[17,8,512]{2,1,0:T(8,128)S(1)}, u32[]{:S(2)}, u32[]{:S(2)}) collective-permute-start(f32[17,8,512]{2,1,0:T(8,128)S(1)} %collective-permute-done.1.refs_4_), channel_id=1, source_target_pairs={{0,1},{1,0},{2,3},{3,2},{4,5},{5,4},{6,7},{7,6},{8,9},{9,8},{10,11... | collective-permute-start | bytes 835592 | tf_op jit(solution)/shard_map/ppermute | solution.py:555
  13.8 5.9 %collective-permute-done.refs_3_ = f32[17,8,512]{2,1,0:T(8,128)S(1)} collective-permute-done((f32[17,8,512]{2,1,0:T(8,128)}, f32[17,8,512]{2,1,0:T(8,128)S(1)}, u32[]{:S(2)}, u32[]{:S(2)}) %collective-permute-start) | collective-permute-done | bytes 278560 | tf_op jit(solution)/shard_map/ppermute | solution.py:555
  19.7 0.7 collective-permute-start.6
  20.4 0.0 collective-permute-done.5.refs_8_
  20.4 2.9 %collective-permute-start.3 = (f32[17,8,512]{2,1,0:T(8,128)S(1)}, f32[17,8,512]{2,1,0:T(8,128)S(1)}, u32[]{:S(2)}, u32[]{:S(2)}) collective-permute-start(f32[17,8,512]{2,1,0:T(8,128)S(1)} %collective-permute-done.refs_3_), channel_id=1, source_target_pairs={{0,1},{1,0},{2,3},{3,2},{4,5},{5,4},{6,7},{7,6},{8,9},{9,8},{10,11... | collective-permute-start | bytes 835592 | tf_op jit(solution)/shard_map/ppermute | solution.py:555
  23.3 0.1 pad_add_fusion.refs_0_
  23.4 0.0 collective-permute-done.2.refs_5_
  23.4 0.0 collective-permute-done.7.refs_10_
  23.4 0.0 collective-permute-done.4.refs_7_
  23.4 0.0 collective-permute-done.6.refs_9_
  23.4 1.1 collective-permute-done.3.refs_6_
  24.5 1.0 copy-done
  25.5 0.7 copy-done.4
  26.2 11.3 %shard_map.56 = (f32[56,128]{1,0:T(8,128)S(1)}, f32[12,24,512]{2,1,0:T(8,128)S(1)}, f32[12,24,512]{2,1,0:T(8,128)S(1)}, f32[12,24,512]{2,1,0:T(8,128)S(1)}, f32[...) custom-call(s32[2]{0:T(128)S(1)} %pad_add_fusion.refs_0_, ...), custom_call_target="tpu_custom_call" | custom-call | tf_op jit(solution)/shard_map/pallas_call | solution.py:517
  37.5 1.0 copy-done.2
  38.5 0.2 collective-permute-start.10
  38.7 4.6 %collective-permute-start.9 = (f32[56,128]{1,0:T(8,128)S(1)}, f32[56,128]{1,0:T(8,128)S(1)}, u32[]{:S(2)}, u32[]{:S(2)}) collective-permute-start(f32[56,128]{1,0:T(8,128)S(1)} %get-tuple-element.30), channel_id=1, source_target_pairs={{0,2},{1,3},{2,0},{3,1},{4,6},{5,7},{6,4},{7,5},{8,10},{9,11},{10,... | collective-permute-start | bytes 86024 | tf_op jit(solution)/shard_map/ppermute | solution.py:555
  43.3 0.0 collective-permute-start.8
  43.3 2.1 %collective-permute-done.9 = f32[56,128]{1,0:T(8,128)S(1)} collective-permute-done((f32[56,128]{1,0:T(8,128)S(1)}, f32[56,128]{1,0:T(8,128)S(1)}, u32[]{:S(2)}, u32[]{:S(2)}) %collective-permute-start.9) | collective-permute-done | bytes 28704 | tf_op jit(solution)/shard_map/ppermute | solution.py:555
  45.4 0.0 collective-permute-done.8
  45.4 2.4 %collective-permute-start.11 = (f32[4,56,128]{2,1,0:T(8,128)S(1)}, f32[4,56,128]{2,1,0:T(8,128)S(1)}, u32[]{:S(2)}, u32[]{:S(2)}) collective-permute-start(f32[4,56,128]{2,1,0:T(8,128)S(1)} %pad_maximum_fusion), channel_id=1, source_target_pairs={{0,4},{4,0},{8,12},{12,8},{16,20},{20,16},{24,28},{28,24},{1,5},{5... | collective-permute-start | bytes 344072 | tf_op jit(solution)/shard_map/ppermute | solution.py:555
  47.9 3.8 %collective-permute-done.11 = f32[4,56,128]{2,1,0:T(8,128)S(1)} collective-permute-done((f32[4,56,128]{2,1,0:T(8,128)S(1)}, f32[4,56,128]{2,1,0:T(8,128)S(1)}, u32[]{:S(2)}, u32[]{:S(2)}) %collective-permute-start.11) | collective-permute-done | bytes 114720 | tf_op jit(solution)/shard_map/ppermute | solution.py:555
  51.7 3.9 %collective-permute-start.14 = (f32[2,4,24,128]{3,2,1,0:T(8,128)S(1)}, f32[2,4,24,128]{3,2,1,0:T(8,128)S(1)}, u32[]{:S(2)}, u32[]{:S(2)}) collective-permute-start(f32[2,4,24,128]{3,2,1,0:T(8,128)S(1)} %pad_maximum_fusion.2.refs_1_), channel_id=1, source_target_pairs={{0,24},{4,28},{8,16},{12,20},{16,8},{20,12},{24,0},{28,4},{1,25},{... | collective-permute-start | bytes 294920 | tf_op jit(solution)/shard_map/ppermute | solution.py:555
  55.6 0.6 collective-permute-start.12
  56.3 0.7 collective-permute-start.15
  57.0 2.3 %collective-permute-done.14.refs_4_ = f32[2,4,24,128]{3,2,1,0:T(8,128)S(1)} collective-permute-done((f32[2,4,24,128]{3,2,1,0:T(8,128)S(1)}, f32[2,4,24,128]{3,2,1,0:T(8,128)S(1)}, u32[]{:S(2)}, u32[]{:S(2)}) %collective-permute-start.14) | collective-permute-done | bytes 98336 | tf_op jit(solution)/shard_map/ppermute | solution.py:555
  59.3 5.3 %collective-permute-done.13.refs_3_ = f32[2,4,24,128]{3,2,1,0:T(8,128)S(1)} collective-permute-done((f32[2,4,24,128]{3,2,1,0:T(8,128)S(1)}, f32[2,4,24,128]{3,2,1,0:T(8,128)S(1)}, u32[]{:S(2)}, u32[]{:S(2)}) %collective-permute-start.13) | collective-permute-done | bytes 98336 | tf_op jit(solution)/shard_map/ppermute | solution.py:555
  64.5 0.0 collective-permute-done.12.refs_2_
  64.5 4.2 %shard_map.57.refs_11_.refs_19_ = f32[8,8,512]{2,1,0:T(8,128)S(1)} custom-call(s32[2]{0:T(128)S(1)} %pad_add_fusion.refs_0_, f32[2,4,24,128]{3,2,1,0:T(8,128)S(1)} %pad_maximum_fusion.2.refs_1_, f32[2,4,24,128]{3,2,1,0:T(8,128)S(1)} %collective-permute-done.12.refs_2_, f32[2,4,24,128]{3,2,1,0:T(8,128)S(1)} %collective-permute-done.13.refs_3_, ...), custom_call_target="tpu_custom_call" | custom-call | tf_op jit(solution)/shard_map/pallas_call | solution.py:544
  68.8 0.7 collective-permute-start.17
  69.4 3.9 %collective-permute-start.16 = (f32[8,8,512]{2,1,0:T(8,128)S(1)}, f32[8,8,512]{2,1,0:T(8,128)S(1)}, u32[]{:S(2)}, u32[]{:S(2)}) collective-permute-start(f32[8,8,512]{2,1,0:T(8,128)S(1)} %shard_map.57.refs_11_.refs_19_), channel_id=1, source_target_pairs={{0,4},{4,0},{8,12},{12,8},{16,20},{20,16},{24,28},{28,24},{1,5},{5... | collective-permute-start | bytes 393224 | tf_op jit(solution)/shard_map/ppermute | solution.py:555
  73.4 0.7 collective-permute-start.21
  74.0 1.4 %collective-permute-start.18 = (f32[8,8,512]{2,1,0:T(8,128)S(1)}, f32[8,8,512]{2,1,0:T(8,128)S(1)}, u32[]{:S(2)}, u32[]{:S(2)}) collective-permute-start(f32[8,8,512]{2,1,0:T(8,128)S(1)} %shard_map.57.refs_11_.refs_19_), channel_id=1, source_target_pairs={{0,1},{1,0},{2,3},{3,2},{4,5},{5,4},{6,7},{7,6},{8,9},{9,8},{10,11... | collective-permute-start | bytes 393224 | tf_op jit(solution)/shard_map/ppermute | solution.py:555
  75.4 0.0 collective-permute-done.17.refs_13_
  75.4 0.7 collective-permute-start.23
  76.1 1.3 %collective-permute-start.20 = (f32[8,8,512]{2,1,0:T(8,128)S(1)}, f32[8,8,512]{2,1,0:T(8,128)S(1)}, u32[]{:S(2)}, u32[]{:S(2)}) collective-permute-start(f32[8,8,512]{2,1,0:T(8,128)S(1)} %collective-permute-done.17.refs_13_), channel_id=1, source_target_pairs={{0,1},{1,0},{2,3},{3,2},{4,5},{5,4},{6,7},{7,6},{8,9},{9,8},{10,11... | collective-permute-start | bytes 393224 | tf_op jit(solution)/shard_map/ppermute | solution.py:555
  77.5 0.0 collective-permute-done.16.refs_12_
  77.5 0.8 collective-permute-start.22
  78.3 3.1 %collective-permute-start.19 = (f32[8,8,512]{2,1,0:T(8,128)S(1)}, f32[8,8,512]{2,1,0:T(8,128)S(1)}, u32[]{:S(2)}, u32[]{:S(2)}) collective-permute-start(f32[8,8,512]{2,1,0:T(8,128)S(1)} %collective-permute-done.16.refs_12_), channel_id=1, source_target_pairs={{0,1},{1,0},{2,3},{3,2},{4,5},{5,4},{6,7},{7,6},{8,9},{9,8},{10,11... | collective-permute-start | bytes 393224 | tf_op jit(solution)/shard_map/ppermute | solution.py:555
  81.4 0.0 collective-permute-done.18.refs_14_
  81.4 0.0 collective-permute-done.23.refs_19_
  81.4 0.0 collective-permute-done.20.refs_16_
  81.4 1.0 collective-permute-done.19.refs_15_
  82.4 12.1 %shard_map.58 = (f32[56,128]{1,0:T(8,128)S(1)}, f32[12,24,512]{2,1,0:T(8,128)S(1)}, f32[12,24,512]{2,1,0:T(8,128)S(1)}, f32[12,24,512]{2,1,0:T(8,128)S(1)}, f32[...) custom-call(s32[2]{0:T(128)S(1)} %pad_add_fusion.refs_0_, ...), custom_call_target="tpu_custom_call" | custom-call | tf_op jit(solution)/shard_map/pallas_call | solution.py:517
  94.5 0.1 collective-permute-start.26
  94.5 3.1 %collective-permute-start.25 = (f32[56,128]{1,0:T(8,128)S(1)}, f32[56,128]{1,0:T(8,128)S(1)}, u32[]{:S(2)}, u32[]{:S(2)}) collective-permute-start(f32[56,128]{1,0:T(8,128)S(1)} %get-tuple-element.43), channel_id=1, source_target_pairs={{0,2},{1,3},{2,0},{3,1},{4,6},{5,7},{6,4},{7,5},{8,10},{9,11},{10,... | collective-permute-start | bytes 86024 | tf_op jit(solution)/shard_map/ppermute | solution.py:555
  97.6 0.0 collective-permute-start.24
  97.7 0.2 collective-permute-done.26
  97.8 1.9 %collective-permute-done.25 = f32[56,128]{1,0:T(8,128)S(1)} collective-permute-done((f32[56,128]{1,0:T(8,128)S(1)}, f32[56,128]{1,0:T(8,128)S(1)}, u32[]{:S(2)}, u32[]{:S(2)}) %collective-permute-start.25) | collective-permute-done | bytes 28704 | tf_op jit(solution)/shard_map/ppermute | solution.py:555
  99.7 3.0 %collective-permute-start.27 = (f32[4,56,128]{2,1,0:T(8,128)S(1)}, f32[4,56,128]{2,1,0:T(8,128)S(1)}, u32[]{:S(2)}, u32[]{:S(2)}) collective-permute-start(f32[4,56,128]{2,1,0:T(8,128)S(1)} %pad_maximum_fusion.1), channel_id=1, source_target_pairs={{0,4},{4,0},{8,12},{12,8},{16,20},{20,16},{24,28},{28,24},{1,5},{5... | collective-permute-start | bytes 344072 | tf_op jit(solution)/shard_map/ppermute | solution.py:555
  102.8 2.8 %collective-permute-done.27 = f32[4,56,128]{2,1,0:T(8,128)S(1)} collective-permute-done((f32[4,56,128]{2,1,0:T(8,128)S(1)}, f32[4,56,128]{2,1,0:T(8,128)S(1)}, u32[]{:S(2)}, u32[]{:S(2)}) %collective-permute-start.27) | collective-permute-done | bytes 114720 | tf_op jit(solution)/shard_map/ppermute | solution.py:555
  105.6 3.9 %collective-permute-start.30 = (f32[2,4,24,128]{3,2,1,0:T(8,128)S(1)}, f32[2,4,24,128]{3,2,1,0:T(8,128)S(1)}, u32[]{:S(2)}, u32[]{:S(2)}) collective-permute-start(f32[2,4,24,128]{3,2,1,0:T(8,128)S(1)} %pad_maximum_fusion.3.refs_1_), channel_id=1, source_target_pairs={{0,24},{4,28},{8,16},{12,20},{16,8},{20,12},{24,0},{28,4},{1,25},{... | collective-permute-start | bytes 294920 | tf_op jit(solution)/shard_map/ppermute | solution.py:555
  109.5 0.6 collective-permute-start.28
  110.2 0.7 collective-permute-start.31
  110.8 1.9 %collective-permute-done.30.refs_4_ = f32[2,4,24,128]{3,2,1,0:T(8,128)S(1)} collective-permute-done((f32[2,4,24,128]{3,2,1,0:T(8,128)S(1)}, f32[2,4,24,128]{3,2,1,0:T(8,128)S(1)}, u32[]{:S(2)}, u32[]{:S(2)}) %collective-permute-start.30) | collective-permute-done | bytes 98336 | tf_op jit(solution)/shard_map/ppermute | solution.py:555
  112.8 5.4 %collective-permute-done.29.refs_3_ = f32[2,4,24,128]{3,2,1,0:T(8,128)S(1)} collective-permute-done((f32[2,4,24,128]{3,2,1,0:T(8,128)S(1)}, f32[2,4,24,128]{3,2,1,0:T(8,128)S(1)}, u32[]{:S(2)}, u32[]{:S(2)}) %collective-permute-start.29) | collective-permute-done | bytes 98336 | tf_op jit(solution)/shard_map/ppermute | solution.py:555
  118.2 4.9 %shard_map.59 = f32[8,8,512]{2,1,0:T(8,128)} custom-call(s32[2]{0:T(128)S(1)} %pad_add_fusion.refs_0_, f32[2,4,24,128]{3,2,1,0:T(8,128)S(1)} %pad_maximum_fusion.3.refs_1_, f32[2,4,24,128]{3,2,1,0:T(8,128)S(1)} %collective-permute-done.28.refs_2_, f32[2,4,24,128]{3,2,1,0:T(8,128)S(1)} %collective-permute-done.29.refs_3_, ...), custom_call_target="tpu_custom_call" | custom-call | tf_op jit(solution)/shard_map/pallas_call | solution.py:544
  (28 shorter events, 0.1 us)
Async XLA Ops:
  1.8 10.0 %collective-permute-start.1 = (f32[17,8,512]{2,1,0:T(8,128)}, f32[17,8,512]{2,1,0:T(8,128)S(1)}, u32[]{:S(2)}, u32[]{:S(2)}) collective-permute-start(f32[17,8,512]{2,1,0:T(8,128)} %shard_map.55.refs_2_), channel_id=1, source_target_pairs={{4,8},{12,16},{20,24},{8,4},{16,12},{24,20},{5,9},{13,17},{21,25},... | collective-permute-start | bytes 835592 | tf_op jit(solution)/shard_map/ppermute | solution.py:561
  2.5 17.3 %collective-permute-start = (f32[17,8,512]{2,1,0:T(8,128)}, f32[17,8,512]{2,1,0:T(8,128)S(1)}, u32[]{:S(2)}, u32[]{:S(2)}) collective-permute-start(f32[17,8,512]{2,1,0:T(8,128)} %shard_map.55.refs_2_), channel_id=1, source_target_pairs={{0,4},{4,0},{8,12},{12,8},{16,20},{20,16},{24,28},{28,24},{1,5},{5... | collective-permute-start | bytes 835592 | tf_op jit(solution)/shard_map/ppermute | solution.py:555
  8.2 12.2 %collective-permute-start.5 = (f32[17,8,512]{2,1,0:T(8,128)}, f32[17,8,512]{2,1,0:T(8,128)S(1)}, u32[]{:S(2)}, u32[]{:S(2)}) collective-permute-start(f32[17,8,512]{2,1,0:T(8,128)} %shard_map.55.refs_2_), channel_id=1, source_target_pairs={{1,2},{2,1},{5,6},{6,5},{9,10},{10,9},{13,14},{14,13},{17,18},{18,... | collective-permute-start | bytes 835592 | tf_op jit(solution)/shard_map/ppermute | solution.py:561
  8.9 14.5 %collective-permute-start.2 = (f32[17,8,512]{2,1,0:T(8,128)}, f32[17,8,512]{2,1,0:T(8,128)S(1)}, u32[]{:S(2)}, u32[]{:S(2)}) collective-permute-start(f32[17,8,512]{2,1,0:T(8,128)} %shard_map.55.refs_2_), channel_id=1, source_target_pairs={{0,1},{1,0},{2,3},{3,2},{4,5},{5,4},{6,7},{7,6},{8,9},{9,8},{10,11... | collective-permute-start | bytes 835592 | tf_op jit(solution)/shard_map/ppermute | solution.py:555
  11.8 11.6 %collective-permute-start.7 = (f32[17,8,512]{2,1,0:T(8,128)S(1)}, f32[17,8,512]{2,1,0:T(8,128)S(1)}, u32[]{:S(2)}, u32[]{:S(2)}) collective-permute-start(f32[17,8,512]{2,1,0:T(8,128)S(1)} %collective-permute-done.1.refs_4_), channel_id=1, source_target_pairs={{1,2},{2,1},{5,6},{6,5},{9,10},{10,9},{13,14},{14,13},{17,18},{18,... | collective-permute-start | bytes 835592 | tf_op jit(solution)/shard_map/ppermute | solution.py:561
  12.5 10.9 %collective-permute-start.4 = (f32[17,8,512]{2,1,0:T(8,128)S(1)}, f32[17,8,512]{2,1,0:T(8,128)S(1)}, u32[]{:S(2)}, u32[]{:S(2)}) collective-permute-start(f32[17,8,512]{2,1,0:T(8,128)S(1)} %collective-permute-done.1.refs_4_), channel_id=1, source_target_pairs={{0,1},{1,0},{2,3},{3,2},{4,5},{5,4},{6,7},{7,6},{8,9},{9,8},{10,11... | collective-permute-start | bytes 835592 | tf_op jit(solution)/shard_map/ppermute | solution.py:555
  19.7 3.7 %collective-permute-start.6 = (f32[17,8,512]{2,1,0:T(8,128)S(1)}, f32[17,8,512]{2,1,0:T(8,128)S(1)}, u32[]{:S(2)}, u32[]{:S(2)}) collective-permute-start(f32[17,8,512]{2,1,0:T(8,128)S(1)} %collective-permute-done.refs_3_), channel_id=1, source_target_pairs={{1,2},{2,1},{5,6},{6,5},{9,10},{10,9},{13,14},{14,13},{17,18},{18,... | collective-permute-start | bytes 835592 | tf_op jit(solution)/shard_map/ppermute | solution.py:561
  20.4 4.1 %collective-permute-start.3 = (f32[17,8,512]{2,1,0:T(8,128)S(1)}, f32[17,8,512]{2,1,0:T(8,128)S(1)}, u32[]{:S(2)}, u32[]{:S(2)}) collective-permute-start(f32[17,8,512]{2,1,0:T(8,128)S(1)} %collective-permute-done.refs_3_), channel_id=1, source_target_pairs={{0,1},{1,0},{2,3},{3,2},{4,5},{5,4},{6,7},{7,6},{8,9},{9,8},{10,11... | collective-permute-start | bytes 835592 | tf_op jit(solution)/shard_map/ppermute | solution.py:555
  24.5 1.0 copy-start
  25.5 0.7 copy-start.4
  26.1 38.4 %copy-start.3 = (f32[8,8,512]{2,1,0:T(8,128)S(1)}, f32[8,8,512]{2,1,0:T(8,128)}, u32[]{:S(2)}) copy-start(f32[8,8,512]{2,1,0:T(8,128)} %refs_19_.1) | copy-start | bytes 393220
  37.5 1.1 copy-start.2
  38.5 4.7 %collective-permute-start.10 = (f32[56,128]{1,0:T(8,128)S(1)}, f32[56,128]{1,0:T(8,128)S(1)}, u32[]{:S(2)}, u32[]{:S(2)}) collective-permute-start(f32[56,128]{1,0:T(8,128)S(1)} %get-tuple-element.30), channel_id=1, source_target_pairs={{0,3},{1,2},{2,1},{3,0},{4,7},{5,6},{6,5},{7,4},{8,11},{9,10},{10,... | collective-permute-start | bytes 86024 | tf_op jit(solution)/shard_map/ppermute | solution.py:555
  38.7 6.7 %collective-permute-start.9 = (f32[56,128]{1,0:T(8,128)S(1)}, f32[56,128]{1,0:T(8,128)S(1)}, u32[]{:S(2)}, u32[]{:S(2)}) collective-permute-start(f32[56,128]{1,0:T(8,128)S(1)} %get-tuple-element.30), channel_id=1, source_target_pairs={{0,2},{1,3},{2,0},{3,1},{4,6},{5,7},{6,4},{7,5},{8,10},{9,11},{10,... | collective-permute-start | bytes 86024 | tf_op jit(solution)/shard_map/ppermute | solution.py:555
  43.3 2.2 %collective-permute-start.8 = (f32[56,128]{1,0:T(8,128)S(1)}, f32[56,128]{1,0:T(8,128)S(1)}, u32[]{:S(2)}, u32[]{:S(2)}) collective-permute-start(f32[56,128]{1,0:T(8,128)S(1)} %get-tuple-element.30), channel_id=1, source_target_pairs={{0,1},{1,0},{2,3},{3,2},{4,5},{5,4},{6,7},{7,6},{8,9},{9,8},{10,11... | collective-permute-start | bytes 86024 | tf_op jit(solution)/shard_map/ppermute | solution.py:555
  45.4 6.3 %collective-permute-start.11 = (f32[4,56,128]{2,1,0:T(8,128)S(1)}, f32[4,56,128]{2,1,0:T(8,128)S(1)}, u32[]{:S(2)}, u32[]{:S(2)}) collective-permute-start(f32[4,56,128]{2,1,0:T(8,128)S(1)} %pad_maximum_fusion), channel_id=1, source_target_pairs={{0,4},{4,0},{8,12},{12,8},{16,20},{20,16},{24,28},{28,24},{1,5},{5... | collective-permute-start | bytes 344072 | tf_op jit(solution)/shard_map/ppermute | solution.py:555
  51.7 7.5 %collective-permute-start.14 = (f32[2,4,24,128]{3,2,1,0:T(8,128)S(1)}, f32[2,4,24,128]{3,2,1,0:T(8,128)S(1)}, u32[]{:S(2)}, u32[]{:S(2)}) collective-permute-start(f32[2,4,24,128]{3,2,1,0:T(8,128)S(1)} %pad_maximum_fusion.2.refs_1_), channel_id=1, source_target_pairs={{0,24},{4,28},{8,16},{12,20},{16,8},{20,12},{24,0},{28,4},{1,25},{... | collective-permute-start | bytes 294920 | tf_op jit(solution)/shard_map/ppermute | solution.py:555
  55.6 8.9 %collective-permute-start.13 = (f32[2,4,24,128]{3,2,1,0:T(8,128)S(1)}, f32[2,4,24,128]{3,2,1,0:T(8,128)S(1)}, u32[]{:S(2)}, u32[]{:S(2)}) collective-permute-start(f32[2,4,24,128]{3,2,1,0:T(8,128)S(1)} %pad_maximum_fusion.2.refs_1_), channel_id=1, source_target_pairs={{0,16},{4,20},{8,24},{12,28},{16,0},{20,4},{24,8},{28,12},{1,17},{... | collective-permute-start | bytes 294920 | tf_op jit(solution)/shard_map/ppermute | solution.py:555
  55.6 8.9 %collective-permute-start.12 = (f32[2,4,24,128]{3,2,1,0:T(8,128)S(1)}, f32[2,4,24,128]{3,2,1,0:T(8,128)S(1)}, u32[]{:S(2)}, u32[]{:S(2)}) collective-permute-start(f32[2,4,24,128]{3,2,1,0:T(8,128)S(1)} %pad_maximum_fusion.2.refs_1_), channel_id=1, source_target_pairs={{0,8},{4,12},{8,0},{12,4},{16,24},{20,28},{24,16},{28,20},{1,9},{5... | collective-permute-start | bytes 294920 | tf_op jit(solution)/shard_map/ppermute | solution.py:555
  56.3 0.7 collective-permute-start.15
  64.5 17.9 %copy-start.1 = (f32[17,8,512]{2,1,0:T(8,128)S(1)}, f32[17,8,512]{2,1,0:T(8,128)}, u32[]{:S(2)}) copy-start(f32[17,8,512]{2,1,0:T(8,128)} %shard_map.55.refs_2_) | copy-start | bytes 835588
  68.8 6.7 %collective-permute-start.17 = (f32[8,8,512]{2,1,0:T(8,128)S(1)}, f32[8,8,512]{2,1,0:T(8,128)S(1)}, u32[]{:S(2)}, u32[]{:S(2)}) collective-permute-start(f32[8,8,512]{2,1,0:T(8,128)S(1)} %shard_map.57.refs_11_.refs_19_), channel_id=1, source_target_pairs={{4,8},{12,16},{20,24},{8,4},{16,12},{24,20},{5,9},{13,17},{21,25},... | collective-permute-start | bytes 393224 | tf_op jit(solution)/shard_map/ppermute | solution.py:561
  69.4 8.0 %collective-permute-start.16 = (f32[8,8,512]{2,1,0:T(8,128)S(1)}, f32[8,8,512]{2,1,0:T(8,128)S(1)}, u32[]{:S(2)}, u32[]{:S(2)}) collective-permute-start(f32[8,8,512]{2,1,0:T(8,128)S(1)} %shard_map.57.refs_11_.refs_19_), channel_id=1, source_target_pairs={{0,4},{4,0},{8,12},{12,8},{16,20},{20,16},{24,28},{28,24},{1,5},{5... | collective-permute-start | bytes 393224 | tf_op jit(solution)/shard_map/ppermute | solution.py:555
  73.4 4.9 %collective-permute-start.21 = (f32[8,8,512]{2,1,0:T(8,128)S(1)}, f32[8,8,512]{2,1,0:T(8,128)S(1)}, u32[]{:S(2)}, u32[]{:S(2)}) collective-permute-start(f32[8,8,512]{2,1,0:T(8,128)S(1)} %shard_map.57.refs_11_.refs_19_), channel_id=1, source_target_pairs={{1,2},{2,1},{5,6},{6,5},{9,10},{10,9},{13,14},{14,13},{17,18},{18,... | collective-permute-start | bytes 393224 | tf_op jit(solution)/shard_map/ppermute | solution.py:561
  74.0 7.3 %collective-permute-start.18 = (f32[8,8,512]{2,1,0:T(8,128)S(1)}, f32[8,8,512]{2,1,0:T(8,128)S(1)}, u32[]{:S(2)}, u32[]{:S(2)}) collective-permute-start(f32[8,8,512]{2,1,0:T(8,128)S(1)} %shard_map.57.refs_11_.refs_19_), channel_id=1, source_target_pairs={{0,1},{1,0},{2,3},{3,2},{4,5},{5,4},{6,7},{7,6},{8,9},{9,8},{10,11... | collective-permute-start | bytes 393224 | tf_op jit(solution)/shard_map/ppermute | solution.py:555
  75.4 6.0 %collective-permute-start.23 = (f32[8,8,512]{2,1,0:T(8,128)S(1)}, f32[8,8,512]{2,1,0:T(8,128)S(1)}, u32[]{:S(2)}, u32[]{:S(2)}) collective-permute-start(f32[8,8,512]{2,1,0:T(8,128)S(1)} %collective-permute-done.17.refs_13_), channel_id=1, source_target_pairs={{1,2},{2,1},{5,6},{6,5},{9,10},{10,9},{13,14},{14,13},{17,18},{18,... | collective-permute-start | bytes 393224 | tf_op jit(solution)/shard_map/ppermute | solution.py:561
  76.1 5.3 %collective-permute-start.20 = (f32[8,8,512]{2,1,0:T(8,128)S(1)}, f32[8,8,512]{2,1,0:T(8,128)S(1)}, u32[]{:S(2)}, u32[]{:S(2)}) collective-permute-start(f32[8,8,512]{2,1,0:T(8,128)S(1)} %collective-permute-done.17.refs_13_), channel_id=1, source_target_pairs={{0,1},{1,0},{2,3},{3,2},{4,5},{5,4},{6,7},{7,6},{8,9},{9,8},{10,11... | collective-permute-start | bytes 393224 | tf_op jit(solution)/shard_map/ppermute | solution.py:555
  77.5 3.9 %collective-permute-start.22 = (f32[8,8,512]{2,1,0:T(8,128)S(1)}, f32[8,8,512]{2,1,0:T(8,128)S(1)}, u32[]{:S(2)}, u32[]{:S(2)}) collective-permute-start(f32[8,8,512]{2,1,0:T(8,128)S(1)} %collective-permute-done.16.refs_12_), channel_id=1, source_target_pairs={{1,2},{2,1},{5,6},{6,5},{9,10},{10,9},{13,14},{14,13},{17,18},{18,... | collective-permute-start | bytes 393224 | tf_op jit(solution)/shard_map/ppermute | solution.py:561
  78.3 4.1 %collective-permute-start.19 = (f32[8,8,512]{2,1,0:T(8,128)S(1)}, f32[8,8,512]{2,1,0:T(8,128)S(1)}, u32[]{:S(2)}, u32[]{:S(2)}) collective-permute-start(f32[8,8,512]{2,1,0:T(8,128)S(1)} %collective-permute-done.16.refs_12_), channel_id=1, source_target_pairs={{0,1},{1,0},{2,3},{3,2},{4,5},{5,4},{6,7},{7,6},{8,9},{9,8},{10,11... | collective-permute-start | bytes 393224 | tf_op jit(solution)/shard_map/ppermute | solution.py:555
  94.5 3.4 %collective-permute-start.26 = (f32[56,128]{1,0:T(8,128)S(1)}, f32[56,128]{1,0:T(8,128)S(1)}, u32[]{:S(2)}, u32[]{:S(2)}) collective-permute-start(f32[56,128]{1,0:T(8,128)S(1)} %get-tuple-element.43), channel_id=1, source_target_pairs={{0,3},{1,2},{2,1},{3,0},{4,7},{5,6},{6,5},{7,4},{8,11},{9,10},{10,... | collective-permute-start | bytes 86024 | tf_op jit(solution)/shard_map/ppermute | solution.py:555
  94.5 5.2 %collective-permute-start.25 = (f32[56,128]{1,0:T(8,128)S(1)}, f32[56,128]{1,0:T(8,128)S(1)}, u32[]{:S(2)}, u32[]{:S(2)}) collective-permute-start(f32[56,128]{1,0:T(8,128)S(1)} %get-tuple-element.43), channel_id=1, source_target_pairs={{0,2},{1,3},{2,0},{3,1},{4,6},{5,7},{6,4},{7,5},{8,10},{9,11},{10,... | collective-permute-start | bytes 86024 | tf_op jit(solution)/shard_map/ppermute | solution.py:555
  97.6 2.1 %collective-permute-start.24 = (f32[56,128]{1,0:T(8,128)S(1)}, f32[56,128]{1,0:T(8,128)S(1)}, u32[]{:S(2)}, u32[]{:S(2)}) collective-permute-start(f32[56,128]{1,0:T(8,128)S(1)} %get-tuple-element.43), channel_id=1, source_target_pairs={{0,1},{1,0},{2,3},{3,2},{4,5},{5,4},{6,7},{7,6},{8,9},{9,8},{10,11... | collective-permute-start | bytes 86024 | tf_op jit(solution)/shard_map/ppermute | solution.py:555
  99.7 5.9 %collective-permute-start.27 = (f32[4,56,128]{2,1,0:T(8,128)S(1)}, f32[4,56,128]{2,1,0:T(8,128)S(1)}, u32[]{:S(2)}, u32[]{:S(2)}) collective-permute-start(f32[4,56,128]{2,1,0:T(8,128)S(1)} %pad_maximum_fusion.1), channel_id=1, source_target_pairs={{0,4},{4,0},{8,12},{12,8},{16,20},{20,16},{24,28},{28,24},{1,5},{5... | collective-permute-start | bytes 344072 | tf_op jit(solution)/shard_map/ppermute | solution.py:555
  105.6 7.2 %collective-permute-start.30 = (f32[2,4,24,128]{3,2,1,0:T(8,128)S(1)}, f32[2,4,24,128]{3,2,1,0:T(8,128)S(1)}, u32[]{:S(2)}, u32[]{:S(2)}) collective-permute-start(f32[2,4,24,128]{3,2,1,0:T(8,128)S(1)} %pad_maximum_fusion.3.refs_1_), channel_id=1, source_target_pairs={{0,24},{4,28},{8,16},{12,20},{16,8},{20,12},{24,0},{28,4},{1,25},{... | collective-permute-start | bytes 294920 | tf_op jit(solution)/shard_map/ppermute | solution.py:555
  109.5 8.7 %collective-permute-start.29 = (f32[2,4,24,128]{3,2,1,0:T(8,128)S(1)}, f32[2,4,24,128]{3,2,1,0:T(8,128)S(1)}, u32[]{:S(2)}, u32[]{:S(2)}) collective-permute-start(f32[2,4,24,128]{3,2,1,0:T(8,128)S(1)} %pad_maximum_fusion.3.refs_1_), channel_id=1, source_target_pairs={{0,16},{4,20},{8,24},{12,28},{16,0},{20,4},{24,8},{28,12},{1,17},{... | collective-permute-start | bytes 294920 | tf_op jit(solution)/shard_map/ppermute | solution.py:555
  109.5 8.7 %collective-permute-start.28 = (f32[2,4,24,128]{3,2,1,0:T(8,128)S(1)}, f32[2,4,24,128]{3,2,1,0:T(8,128)S(1)}, u32[]{:S(2)}, u32[]{:S(2)}) collective-permute-start(f32[2,4,24,128]{3,2,1,0:T(8,128)S(1)} %pad_maximum_fusion.3.refs_1_), channel_id=1, source_target_pairs={{0,8},{4,12},{8,0},{12,4},{16,24},{20,28},{24,16},{28,20},{1,9},{5... | collective-permute-start | bytes 294920 | tf_op jit(solution)/shard_map/ppermute | solution.py:555
  110.2 0.7 collective-permute-start.31

commit v5 on v4

--- a/solution.py
+++ b/solution.py
@@ -58,12 +58,12 @@
         head_refs, refs = refs[:9], refs[9:]
         sat_old_ref, refs = refs[0], refs[1:]
     payload_ref, refs = refs[0], refs[1:]
-    outs0, refs = refs[:6], refs[6:]
-    outs1, refs = refs[:5], refs[5:]
+    err, src, inv, fx, fy, fz = refs[:6]
+    src1, inv1, fx1, fy1, fz1 = refs[6:11]
+    refs = refs[11:]
     if first:
         sat_out, refs = refs[0], refs[1:]
-    head, cond, stor, grow, fx, fy, fz, src, inv, err = refs[:10]
-    src1, stor1, fx1, fy1, fz1, inv1, err1, rows2, table_rows = refs[10:]
+    head, cond, stor, grow, stor1, err1, rows2 = refs
 
     strip, slab = where_ref[0], where_ref[1]
     zw, xw = 3 * zl, 3 * xl
@@ -90,13 +90,7 @@
             jnp.logical_and(z == 2 * width, slab == slabs - 1),
         )
 
-    resid, high, alpha, shape_n, k_sat = (table_ref[k : k + 1, :] for k in range(5))
-    classes = table_ref.shape[1]
-    rows = (high - resid, alpha, shape_n, k_sat, 1.0 - 1.0 / shape_n)
-    table_rows[...] = jnp.ones(table_rows.shape, jnp.float32)
-    for k, row in enumerate(rows):
-        table_rows[k : k + 1, 0:classes] = row
-    table = table_rows[...]
+    table = table_ref[...]
     for block in range(9):
         z_at, x_at = place(block // 3, slab), place(block % 3, strip)
 
@@ -247,20 +241,6 @@
     base = rows2.shape[0]
     for c in range(ny // 128):
         payload_ref[base + 8 * c : base + 8 * c + 8, :] = plane[:, 128 * c : 128 * c + 128]
-
-    def keep0(i, carry):
-        for out, ref in zip(outs0, (err, src, inv, fx, fy, fz)):
-            out[i] = ref[zl - 2 + i]
-        return carry
-
-    lax.fori_loop(0, zl + 4, keep0, 0, unroll=3)
-
-    def keep1(i, carry):
-        for out, ref in zip(outs1, (src1, inv1, fx1, fy1, fz1)):
-            out[i] = ref[zl // 2 - 2 + i]
-        return carry
-
-    lax.fori_loop(0, zl // 2 + 5, keep1, 0, unroll=3)
 
 
 def solve_blocks(block, factors, answer, strips, slabs):
@@ -443,11 +423,10 @@
     parity1 = ((xi >> 1) + (yi >> 1)) & 1
 
     def level1(k, colour):
-        i = k - (zl1 - 2)
         total = neighbour_sum(
-            at1(k), at1(k - 1), at1(k + 1), fx1[i], fy1[i], fz1[i], fz1[i + 1], 2
+            at1(k), at1(k - 1), at1(k + 1), fx1[k], fy1[k], fz1[k], fz1[k + 1], 2
         )
-        updated = (src1[i] + total) * inv1[i]
+        updated = (src1[k] + total) * inv1[k]
         e1[k] = jnp.where(parity1 == ((k + colour) & 1), updated, at1(k)).reshape(3, xl, ny)
 
     def up1(colour, reach):
@@ -461,17 +440,18 @@
     up1(1, 1)
 
     def join(i, carry):
-        e0[i] = e0_in[i] + at1((zl - 2 + i) // 2)
+        e0[i] = e0_in[i + zl - 2] + at1((zl - 2 + i) // 2)
         return carry
 
     lax.fori_loop(0, zl + 4, join, 0, unroll=3)
 
     def up0(colour, reach):
         def step(i, carry):
+            z = i + zl - 2
             total = neighbour_sum(
-                e0[i], e0[i - 1], e0[i + 1], fx0[i], fy0[i], fz0[i], fz0[i + 1], 1
+                e0[i], e0[i - 1], e0[i + 1], fx0[z], fy0[z], fz0[z], fz0[z + 1], 1
             )
-            updated = (src0[i] + total) * inv0[i]
+            updated = (src0[z] + total) * inv0[z]
             e0[i] = jnp.where(parity0 == ((i + colour) & 1), updated, e0[i])
             return carry
 
@@ -481,15 +461,6 @@
     up0(1, 0)
     for z in range(zl):
         out_ref[z] = head_ref[z] + e0[z + 2][xl : 2 * xl]
-
-
-def lay_kernel(head_ref, soil_ref, land_ref, sun_ref, out_ref):
-    zl = head_ref.shape[0]
-    out_ref[0:zl] = head_ref[...]
-    out_ref[zl : 2 * zl] = soil_ref[...].astype(jnp.float32)
-    hour = sun_ref[...].astype(jnp.float32)
-    sun_share = jnp.maximum(0.0, jnp.sin(math.pi * (hour - 6.0) / 12.0))
-    out_ref[2 * zl] = ET_PEAK * sun_share * land_ref[...].astype(jnp.float32)
 
 
 VMEM = pl.BlockSpec(memory_space=pltpu.VMEM)
@@ -505,23 +476,21 @@
     rows2 = 5 * (xl // 4) * (zl // 4)
     rows2 = -(-rows2 // 8) * 8
     out_shape = [f32(rows2 + 8 * ny // 128, 128)]
-    out_shape += [f32(zl + 4, xw, ny)] * 6 + [f32(zl // 2 + 5, xw, ny)] * 5
+    out_shape += [f32(zw, xw, ny)] * 6 + [f32(zw // 2, xw, ny)] * 5
     operands = [where, table, *state]
     if first:
         out_shape.append(f32(zw, 3, xl, ny))
     else:
         operands += [*head, sat_old]
     split = pltpu.VMEM((zw, 3, xl, ny), jnp.float32)
-    full, half = pltpu.VMEM((zw, xw, ny), jnp.float32), pltpu.VMEM((zw // 2, xw, ny), jnp.float32)
-    tall = pltpu.VMEM((zw + 1, xw, ny), jnp.float32)
+    half = pltpu.VMEM((zw // 2, xw, ny), jnp.float32)
     return pl.pallas_call(
         functools.partial(down_kernel, first, slabs, strips, zl, xl),
         out_shape=out_shape,
         in_specs=[SMEM] + [VMEM] * (len(operands) - 1),
         out_specs=[VMEM] * len(out_shape),
-        scratch_shapes=[split] * 4 + [full] * 2 + [tall] + [full] * 3 + [half] * 7
-        + [pltpu.VMEM((rows2, ny), jnp.float32), pltpu.VMEM((8, 128), jnp.float32)],
-        compiler_params=pltpu.CompilerParams(vmem_limit_bytes=44 * 1024 * 1024),
+        scratch_shapes=[split] * 4 + [half] * 2 + [pltpu.VMEM((rows2, ny), jnp.float32)],
+        compiler_params=pltpu.CompilerParams(vmem_limit_bytes=30 * 1024 * 1024),
     )(*operands)
 
 
@@ -547,7 +516,7 @@
         in_specs=[SMEM] + [VMEM] * (len(operands) - 1),
         out_specs=VMEM,
         scratch_shapes=scratch,
-        compiler_params=pltpu.CompilerParams(vmem_limit_bytes=44 * 1024 * 1024),
+        compiler_params=pltpu.CompilerParams(vmem_limit_bytes=30 * 1024 * 1024),
     )(*operands)
 
 
@@ -582,12 +551,15 @@
     zl, xl, ny = head_old.shape
     strips, slabs = lax.axis_size("xy"), lax.axis_size("gz")
     where = jnp.stack([lax.axis_index("xy"), lax.axis_index("gz")]).astype(jnp.int32)
-    own = pl.pallas_call(
-        lay_kernel,
-        out_shape=f32(2 * zl + 1, xl, ny),
-        in_specs=[VMEM] * 4,
-        out_specs=VMEM,
-    )(head_old, soil_type, land_mask, sun_bin)
+    resid, sat, alpha, shape_n, k_sat = soil_table
+    table = jnp.stack([sat - resid, alpha, shape_n, k_sat, 1.0 - 1.0 / shape_n])
+    table = jnp.pad(table, ((0, 3), (0, 128 - table.shape[1])))
+    sun_share = jnp.maximum(0.0, jnp.sin(math.pi * (sun_bin.astype(jnp.float32) - 6.0) / 12.0))
+    forcing = ET_PEAK * sun_share * land_mask.astype(jnp.float32)
+    across = ((0, 0), (0, 0))
+    soil = jnp.pad(soil_type, ((zl, 1), *across)).astype(jnp.float32)
+    own = jnp.pad(head_old, ((0, zl + 1), *across)) + soil
+    own = own + jnp.pad(forcing[None], ((2 * zl, 0), *across))
     state = neighbourhood(own)
     sizes = (slabs, strips, zl, xl, ny)
     base = -(-5 * (xl // 4) * (zl // 4) // 8) * 8
@@ -600,10 +572,10 @@
         near = [full[:, base:], partner[:, base:], odd_pairs(full[:, base:], "xy")]
         return up(*sizes, where, pieces, near, kept, head)
 
-    payload, *kept, sat_old = down(True, *sizes, where, soil_table, state)
+    payload, *kept, sat_old = down(True, *sizes, where, table, state)
     head = finish(payload, kept, head_old)
     payload, *kept = down(
-        False, *sizes, where, soil_table, state, neighbourhood(head), sat_old
+        False, *sizes, where, table, state, neighbourhood(head), sat_old
     )
     return finish(payload, kept, head)
 

time: 124 us -> 120 us (0.968)
  other arithmetic: 0.12 us -> 2.73 us
  Pallas kernels: 34.3 us -> 31.8 us
  local copies, waits for them, and re-layouts: 2.73 us -> 0.74 us
  waiting for transfers between devices: 33.8 us -> 32.4 us
    unnamed x10 -> x2, local copies, waits for them, and re-layouts: 2.69 us -> 0.01 us
    pallas_call x1 -> x0, Pallas kernels: 1.78 us -> none  [per_device(): pl.pallas_call(lay_kernel, out_shape=f32(2 * zl + 1, xl, ny), in_specs=[V...]
    ppermute x22, waiting for transfers between devices: 33.7 us -> 32.3 us  [swapped(): lax.ppermute(x, axis, [(i, i ^ mask) for i in range(lax.axis_size(axis))])]
  transfers between devices with their start and end apart: 32 -> 32, of which waited for: 12 -> 11; matrix products, arithmetic and copies ran while one was open for 0% -> 1% of each run, Pallas kernels for 0% -> 0%
where the time goes in v5:
time: 120 us
  starting transfers between devices  51.7 us (43%)
  waiting for transfers between devices  32.4 us (27%)
  Pallas kernels  31.8 us (26%)
  other arithmetic  2.73 us (2%)
    ppermute x22, starting transfers between devices, swapped(): lax.ppermute(x, axis, [(i, i ^ mask) for i in range(lax.axis_size(axis))])  44.9 us
    ppermute x22, waiting for transfers between devices, swapped(): lax.ppermute(x, axis, [(i, i ^ mask) for i in range(lax.axis_size(axis))])  32.3 us
    pallas_call x2, Pallas kernels, down(): pl.pallas_call(functools.partial(down_kernel, first, slabs, strips, zl, x...  22.7 us
    pallas_call x2, Pallas kernels, up(): pl.pallas_call(functools.partial(up_kernel, slabs, strips, zl, xl, counts...  9.13 us
    ppermute x10, starting transfers between devices, odd_pairs(): return lax.ppermute(x, axis, pairs + [(j, i) for i, j in pairs])  6.81 us
  transfers between devices with their start and end apart: 32, of which 11 were waited for; matrix products, arithmetic and copies ran while one was open for 1% of the time, Pallas kernels for 0%

profile of v5, /device:TPU:0, one launch (start us, length us, event | category | flops | bytes accessed | tf_op | source)
XLA Modules:
  0.0 119.6 jit_solution(2579898535445167716)
XLA Ops:
  0.0 0.8 multiply_bitcast_fusion
  0.8 1.0 pad_add_fusion.refs_2_
  1.8 0.7 collective-permute-start.1
  2.5 5.8 %collective-permute-start = (f32[17,8,512]{2,1,0:T(8,128)S(1)}, f32[17,8,512]{2,1,0:T(8,128)S(1)}, u32[]{:S(2)}, u32[]{:S(2)}) collective-permute-start(f32[17,8,512]{2,1,0:T(8,128)S(1)} %pad_add_fusion.refs_2_), channel_id=1, source_target_pairs={{0,4},{4,0},{8,12},{12,8},{16,20},{20,16},{24,28},{28,24},{1,5},{5... | collective-permute-start | bytes 835592 | tf_op jit(solution)/shard_map/ppermute | solution.py:524
  8.3 0.7 collective-permute-start.5
  8.9 2.9 %collective-permute-start.2 = (f32[17,8,512]{2,1,0:T(8,128)S(1)}, f32[17,8,512]{2,1,0:T(8,128)S(1)}, u32[]{:S(2)}, u32[]{:S(2)}) collective-permute-start(f32[17,8,512]{2,1,0:T(8,128)S(1)} %pad_add_fusion.refs_2_), channel_id=1, source_target_pairs={{0,1},{1,0},{2,3},{3,2},{4,5},{5,4},{6,7},{7,6},{8,9},{9,8},{10,11... | collective-permute-start | bytes 835592 | tf_op jit(solution)/shard_map/ppermute | solution.py:524
  11.8 0.0 collective-permute-done.1.refs_4_
  11.9 0.7 collective-permute-start.7
  12.5 1.3 %collective-permute-start.4 = (f32[17,8,512]{2,1,0:T(8,128)S(1)}, f32[17,8,512]{2,1,0:T(8,128)S(1)}, u32[]{:S(2)}, u32[]{:S(2)}) collective-permute-start(f32[17,8,512]{2,1,0:T(8,128)S(1)} %collective-permute-done.1.refs_4_), channel_id=1, source_target_pairs={{0,1},{1,0},{2,3},{3,2},{4,5},{5,4},{6,7},{7,6},{8,9},{9,8},{10,11... | collective-permute-start | bytes 835592 | tf_op jit(solution)/shard_map/ppermute | solution.py:524
  13.9 5.6 %collective-permute-done.refs_3_ = f32[17,8,512]{2,1,0:T(8,128)S(1)} collective-permute-done((f32[17,8,512]{2,1,0:T(8,128)S(1)}, f32[17,8,512]{2,1,0:T(8,128)S(1)}, u32[]{:S(2)}, u32[]{:S(2)}) %collective-permute-start) | collective-permute-done | bytes 278560 | tf_op jit(solution)/shard_map/ppermute | solution.py:524
  19.4 0.7 collective-permute-start.6
  20.1 0.0 collective-permute-done.5.refs_8_
  20.1 2.9 %collective-permute-start.3 = (f32[17,8,512]{2,1,0:T(8,128)S(1)}, f32[17,8,512]{2,1,0:T(8,128)S(1)}, u32[]{:S(2)}, u32[]{:S(2)}) collective-permute-start(f32[17,8,512]{2,1,0:T(8,128)S(1)} %collective-permute-done.refs_3_), channel_id=1, source_target_pairs={{0,1},{1,0},{2,3},{3,2},{4,5},{5,4},{6,7},{7,6},{8,9},{9,8},{10,11... | collective-permute-start | bytes 835592 | tf_op jit(solution)/shard_map/ppermute | solution.py:524
  23.0 0.8 slice_subtract_fusion
  23.8 0.7 unstack.18
  24.5 0.1 pad_add_fusion.1.refs_0_
  24.6 0.0 copy-start
  24.6 0.0 collective-permute-done.2.refs_5_
  24.6 0.0 collective-permute-done.7.refs_10_
  24.7 0.0 collective-permute-done.6.refs_9_
  24.7 0.0 collective-permute-done.3.refs_6_
  24.7 11.3 %shard_map.55 = (f32[56,128]{1,0:T(8,128)S(1)}, f32[24,24,512]{2,1,0:T(8,128)S(1)}, f32[24,24,512]{2,1,0:T(8,128)S(1)}, f32[24,24,512]{2,1,0:T(8,128)S(1)}, f32[...) custom-call(s32[2]{0:T(128)S(1)} %pad_add_fusion.1.refs_0_, ...), custom_call_target="tpu_custom_call" | custom-call | tf_op jit(solution)/shard_map/pallas_call | solution.py:487
  36.0 0.2 collective-permute-start.10
  36.3 4.1 %collective-permute-start.9 = (f32[56,128]{1,0:T(8,128)S(1)}, f32[56,128]{1,0:T(8,128)S(1)}, u32[]{:S(2)}, u32[]{:S(2)}) collective-permute-start(f32[56,128]{1,0:T(8,128)S(1)} %get-tuple-element.30), channel_id=1, source_target_pairs={{0,2},{1,3},{2,0},{3,1},{4,6},{5,7},{6,4},{7,5},{8,10},{9,11},{10,... | collective-permute-start | bytes 86024 | tf_op jit(solution)/shard_map/ppermute | solution.py:524
  40.4 0.0 collective-permute-done.10
  40.4 2.1 %collective-permute-done.9 = f32[56,128]{1,0:T(8,128)S(1)} collective-permute-done((f32[56,128]{1,0:T(8,128)S(1)}, f32[56,128]{1,0:T(8,128)S(1)}, u32[]{:S(2)}, u32[]{:S(2)}) %collective-permute-start.9) | collective-permute-done | bytes 28704 | tf_op jit(solution)/shard_map/ppermute | solution.py:524
  42.5 0.0 collective-permute-done.8
  42.5 2.5 %collective-permute-start.11 = (f32[4,56,128]{2,1,0:T(8,128)S(1)}, f32[4,56,128]{2,1,0:T(8,128)S(1)}, u32[]{:S(2)}, u32[]{:S(2)}) collective-permute-start(f32[4,56,128]{2,1,0:T(8,128)S(1)} %pad_maximum_fusion), channel_id=1, source_target_pairs={{0,4},{4,0},{8,12},{12,8},{16,20},{20,16},{24,28},{28,24},{1,5},{5... | collective-permute-start | bytes 344072 | tf_op jit(solution)/shard_map/ppermute | solution.py:524
  45.1 3.8 %collective-permute-done.11 = f32[4,56,128]{2,1,0:T(8,128)S(1)} collective-permute-done((f32[4,56,128]{2,1,0:T(8,128)S(1)}, f32[4,56,128]{2,1,0:T(8,128)S(1)}, u32[]{:S(2)}, u32[]{:S(2)}) %collective-permute-start.11) | collective-permute-done | bytes 114720 | tf_op jit(solution)/shard_map/ppermute | solution.py:524
  48.9 3.9 %collective-permute-start.14 = (f32[2,4,24,128]{3,2,1,0:T(8,128)S(1)}, f32[2,4,24,128]{3,2,1,0:T(8,128)S(1)}, u32[]{:S(2)}, u32[]{:S(2)}) collective-permute-start(f32[2,4,24,128]{3,2,1,0:T(8,128)S(1)} %pad_maximum_fusion.2.refs_1_), channel_id=1, source_target_pairs={{0,24},{4,28},{8,16},{12,20},{16,8},{20,12},{24,0},{28,4},{1,25},{... | collective-permute-start | bytes 294920 | tf_op jit(solution)/shard_map/ppermute | solution.py:524
  52.8 0.0 collective-permute-start.13
  52.8 0.6 collective-permute-start.12
  53.5 0.7 collective-permute-start.15
  54.1 0.0 collective-permute-done.15.refs_7_
  54.1 2.3 %collective-permute-done.14.refs_4_ = f32[2,4,24,128]{3,2,1,0:T(8,128)S(1)} collective-permute-done((f32[2,4,24,128]{3,2,1,0:T(8,128)S(1)}, f32[2,4,24,128]{3,2,1,0:T(8,128)S(1)}, u32[]{:S(2)}, u32[]{:S(2)}) %collective-permute-start.14) | collective-permute-done | bytes 98336 | tf_op jit(solution)/shard_map/ppermute | solution.py:524
  56.4 5.3 %collective-permute-done.13.refs_3_ = f32[2,4,24,128]{3,2,1,0:T(8,128)S(1)} collective-permute-done((f32[2,4,24,128]{3,2,1,0:T(8,128)S(1)}, f32[2,4,24,128]{3,2,1,0:T(8,128)S(1)}, u32[]{:S(2)}, u32[]{:S(2)}) %collective-permute-start.13) | collective-permute-done | bytes 98336 | tf_op jit(solution)/shard_map/ppermute | solution.py:524
  61.7 0.0 collective-permute-done.12.refs_2_
  61.7 4.2 %shard_map.56.refs_11_.refs_19_ = f32[8,8,512]{2,1,0:T(8,128)S(1)} custom-call(s32[2]{0:T(128)S(1)} %pad_add_fusion.1.refs_0_, f32[2,4,24,128]{3,2,1,0:T(8,128)S(1)} %pad_maximum_fusion.2.refs_1_, f32[2,4,24,128]{3,2,1,0:T(8,128)S(1)} %collective-permute-done.12.refs_2_, f32[2,4,24,128]{3,2,1,0:T(8,128)S(1)} %collective-permute-done.13.refs_3_, ...), custom_call_target="tpu_custom_call" | custom-call | tf_op jit(solution)/shard_map/pallas_call | solution.py:513
  65.9 0.7 collective-permute-start.17
  66.6 3.9 %collective-permute-start.16 = (f32[8,8,512]{2,1,0:T(8,128)S(1)}, f32[8,8,512]{2,1,0:T(8,128)S(1)}, u32[]{:S(2)}, u32[]{:S(2)}) collective-permute-start(f32[8,8,512]{2,1,0:T(8,128)S(1)} %shard_map.56.refs_11_.refs_19_), channel_id=1, source_target_pairs={{0,4},{4,0},{8,12},{12,8},{16,20},{20,16},{24,28},{28,24},{1,5},{5... | collective-permute-start | bytes 393224 | tf_op jit(solution)/shard_map/ppermute | solution.py:524
  70.6 0.7 collective-permute-start.21
  71.2 1.4 %collective-permute-start.18 = (f32[8,8,512]{2,1,0:T(8,128)S(1)}, f32[8,8,512]{2,1,0:T(8,128)S(1)}, u32[]{:S(2)}, u32[]{:S(2)}) collective-permute-start(f32[8,8,512]{2,1,0:T(8,128)S(1)} %shard_map.56.refs_11_.refs_19_), channel_id=1, source_target_pairs={{0,1},{1,0},{2,3},{3,2},{4,5},{5,4},{6,7},{7,6},{8,9},{9,8},{10,11... | collective-permute-start | bytes 393224 | tf_op jit(solution)/shard_map/ppermute | solution.py:524
  72.6 0.0 collective-permute-done.17.refs_13_
  72.6 0.7 collective-permute-start.23
  73.3 1.3 %collective-permute-start.20 = (f32[8,8,512]{2,1,0:T(8,128)S(1)}, f32[8,8,512]{2,1,0:T(8,128)S(1)}, u32[]{:S(2)}, u32[]{:S(2)}) collective-permute-start(f32[8,8,512]{2,1,0:T(8,128)S(1)} %collective-permute-done.17.refs_13_), channel_id=1, source_target_pairs={{0,1},{1,0},{2,3},{3,2},{4,5},{5,4},{6,7},{7,6},{8,9},{9,8},{10,11... | collective-permute-start | bytes 393224 | tf_op jit(solution)/shard_map/ppermute | solution.py:524
  74.6 0.0 collective-permute-done.16.refs_12_
  74.6 0.8 collective-permute-start.22
  75.5 3.1 %collective-permute-start.19 = (f32[8,8,512]{2,1,0:T(8,128)S(1)}, f32[8,8,512]{2,1,0:T(8,128)S(1)}, u32[]{:S(2)}, u32[]{:S(2)}) collective-permute-start(f32[8,8,512]{2,1,0:T(8,128)S(1)} %collective-permute-done.16.refs_12_), channel_id=1, source_target_pairs={{0,1},{1,0},{2,3},{3,2},{4,5},{5,4},{6,7},{7,6},{8,9},{9,8},{10,11... | collective-permute-start | bytes 393224 | tf_op jit(solution)/shard_map/ppermute | solution.py:524
  78.6 0.0 collective-permute-done.18.refs_14_
  78.6 1.0 collective-permute-done.19.refs_15_
  79.6 11.4 %shard_map.57 = (f32[56,128]{1,0:T(8,128)S(1)}, f32[24,24,512]{2,1,0:T(8,128)S(1)}, f32[24,24,512]{2,1,0:T(8,128)S(1)}, f32[24,24,512]{2,1,0:T(8,128)S(1)}, f32[...) custom-call(s32[2]{0:T(128)S(1)} %pad_add_fusion.1.refs_0_, ...), custom_call_target="tpu_custom_call" | custom-call | tf_op jit(solution)/shard_map/pallas_call | solution.py:487
  90.9 0.1 collective-permute-start.26
  91.0 3.1 %collective-permute-start.25 = (f32[56,128]{1,0:T(8,128)S(1)}, f32[56,128]{1,0:T(8,128)S(1)}, u32[]{:S(2)}, u32[]{:S(2)}) collective-permute-start(f32[56,128]{1,0:T(8,128)S(1)} %get-tuple-element.43), channel_id=1, source_target_pairs={{0,2},{1,3},{2,0},{3,1},{4,6},{5,7},{6,4},{7,5},{8,10},{9,11},{10,... | collective-permute-start | bytes 86024 | tf_op jit(solution)/shard_map/ppermute | solution.py:524
  94.1 0.0 collective-permute-start.24
  94.1 0.2 collective-permute-done.26
  94.3 1.9 %collective-permute-done.25 = f32[56,128]{1,0:T(8,128)S(1)} collective-permute-done((f32[56,128]{1,0:T(8,128)S(1)}, f32[56,128]{1,0:T(8,128)S(1)}, u32[]{:S(2)}, u32[]{:S(2)}) %collective-permute-start.25) | collective-permute-done | bytes 28704 | tf_op jit(solution)/shard_map/ppermute | solution.py:524
  96.2 3.0 %collective-permute-start.27 = (f32[4,56,128]{2,1,0:T(8,128)S(1)}, f32[4,56,128]{2,1,0:T(8,128)S(1)}, u32[]{:S(2)}, u32[]{:S(2)}) collective-permute-start(f32[4,56,128]{2,1,0:T(8,128)S(1)} %pad_maximum_fusion.1), channel_id=1, source_target_pairs={{0,4},{4,0},{8,12},{12,8},{16,20},{20,16},{24,28},{28,24},{1,5},{5... | collective-permute-start | bytes 344072 | tf_op jit(solution)/shard_map/ppermute | solution.py:524
  99.2 2.8 %collective-permute-done.27 = f32[4,56,128]{2,1,0:T(8,128)S(1)} collective-permute-done((f32[4,56,128]{2,1,0:T(8,128)S(1)}, f32[4,56,128]{2,1,0:T(8,128)S(1)}, u32[]{:S(2)}, u32[]{:S(2)}) %collective-permute-start.27) | collective-permute-done | bytes 114720 | tf_op jit(solution)/shard_map/ppermute | solution.py:524
  102.1 3.9 %collective-permute-start.30 = (f32[2,4,24,128]{3,2,1,0:T(8,128)S(1)}, f32[2,4,24,128]{3,2,1,0:T(8,128)S(1)}, u32[]{:S(2)}, u32[]{:S(2)}) collective-permute-start(f32[2,4,24,128]{3,2,1,0:T(8,128)S(1)} %pad_maximum_fusion.3.refs_1_), channel_id=1, source_target_pairs={{0,24},{4,28},{8,16},{12,20},{16,8},{20,12},{24,0},{28,4},{1,25},{... | collective-permute-start | bytes 294920 | tf_op jit(solution)/shard_map/ppermute | solution.py:524
  106.0 0.6 collective-permute-start.28
  106.6 0.7 collective-permute-start.31
  107.3 1.9 %collective-permute-done.30.refs_4_ = f32[2,4,24,128]{3,2,1,0:T(8,128)S(1)} collective-permute-done((f32[2,4,24,128]{3,2,1,0:T(8,128)S(1)}, f32[2,4,24,128]{3,2,1,0:T(8,128)S(1)}, u32[]{:S(2)}, u32[]{:S(2)}) %collective-permute-start.30) | collective-permute-done | bytes 98336 | tf_op jit(solution)/shard_map/ppermute | solution.py:524
  109.3 5.4 %collective-permute-done.29.refs_3_ = f32[2,4,24,128]{3,2,1,0:T(8,128)S(1)} collective-permute-done((f32[2,4,24,128]{3,2,1,0:T(8,128)S(1)}, f32[2,4,24,128]{3,2,1,0:T(8,128)S(1)}, u32[]{:S(2)}, u32[]{:S(2)}) %collective-permute-start.29) | collective-permute-done | bytes 98336 | tf_op jit(solution)/shard_map/ppermute | solution.py:524
  114.7 4.9 %shard_map.58 = f32[8,8,512]{2,1,0:T(8,128)} custom-call(s32[2]{0:T(128)S(1)} %pad_add_fusion.1.refs_0_, f32[2,4,24,128]{3,2,1,0:T(8,128)S(1)} %pad_maximum_fusion.3.refs_1_, f32[2,4,24,128]{3,2,1,0:T(8,128)S(1)} %collective-permute-done.28.refs_2_, f32[2,4,24,128]{3,2,1,0:T(8,128)S(1)} %collective-permute-done.29.refs_3_, ...), custom_call_target="tpu_custom_call" | custom-call | tf_op jit(solution)/shard_map/pallas_call | solution.py:513
  (24 shorter events, 0.1 us)
Async XLA Ops:
  1.8 10.0 %collective-permute-start.1 = (f32[17,8,512]{2,1,0:T(8,128)S(1)}, f32[17,8,512]{2,1,0:T(8,128)S(1)}, u32[]{:S(2)}, u32[]{:S(2)}) collective-permute-start(f32[17,8,512]{2,1,0:T(8,128)S(1)} %pad_add_fusion.refs_2_), channel_id=1, source_target_pairs={{4,8},{12,16},{20,24},{8,4},{16,12},{24,20},{5,9},{13,17},{21,25},... | collective-permute-start | bytes 835592 | tf_op jit(solution)/shard_map/ppermute | solution.py:530
  2.5 17.0 %collective-permute-start = (f32[17,8,512]{2,1,0:T(8,128)S(1)}, f32[17,8,512]{2,1,0:T(8,128)S(1)}, u32[]{:S(2)}, u32[]{:S(2)}) collective-permute-start(f32[17,8,512]{2,1,0:T(8,128)S(1)} %pad_add_fusion.refs_2_), channel_id=1, source_target_pairs={{0,4},{4,0},{8,12},{12,8},{16,20},{20,16},{24,28},{28,24},{1,5},{5... | collective-permute-start | bytes 835592 | tf_op jit(solution)/shard_map/ppermute | solution.py:524
  8.3 11.9 %collective-permute-start.5 = (f32[17,8,512]{2,1,0:T(8,128)S(1)}, f32[17,8,512]{2,1,0:T(8,128)S(1)}, u32[]{:S(2)}, u32[]{:S(2)}) collective-permute-start(f32[17,8,512]{2,1,0:T(8,128)S(1)} %pad_add_fusion.refs_2_), channel_id=1, source_target_pairs={{1,2},{2,1},{5,6},{6,5},{9,10},{10,9},{13,14},{14,13},{17,18},{18,... | collective-permute-start | bytes 835592 | tf_op jit(solution)/shard_map/ppermute | solution.py:530
  8.9 15.7 %collective-permute-start.2 = (f32[17,8,512]{2,1,0:T(8,128)S(1)}, f32[17,8,512]{2,1,0:T(8,128)S(1)}, u32[]{:S(2)}, u32[]{:S(2)}) collective-permute-start(f32[17,8,512]{2,1,0:T(8,128)S(1)} %pad_add_fusion.refs_2_), channel_id=1, source_target_pairs={{0,1},{1,0},{2,3},{3,2},{4,5},{5,4},{6,7},{7,6},{8,9},{9,8},{10,11... | collective-permute-start | bytes 835592 | tf_op jit(solution)/shard_map/ppermute | solution.py:524
  11.9 12.8 %collective-permute-start.7 = (f32[17,8,512]{2,1,0:T(8,128)S(1)}, f32[17,8,512]{2,1,0:T(8,128)S(1)}, u32[]{:S(2)}, u32[]{:S(2)}) collective-permute-start(f32[17,8,512]{2,1,0:T(8,128)S(1)} %collective-permute-done.1.refs_4_), channel_id=1, source_target_pairs={{1,2},{2,1},{5,6},{6,5},{9,10},{10,9},{13,14},{14,13},{17,18},{18,... | collective-permute-start | bytes 835592 | tf_op jit(solution)/shard_map/ppermute | solution.py:530
  12.5 12.1 %collective-permute-start.4 = (f32[17,8,512]{2,1,0:T(8,128)S(1)}, f32[17,8,512]{2,1,0:T(8,128)S(1)}, u32[]{:S(2)}, u32[]{:S(2)}) collective-permute-start(f32[17,8,512]{2,1,0:T(8,128)S(1)} %collective-permute-done.1.refs_4_), channel_id=1, source_target_pairs={{0,1},{1,0},{2,3},{3,2},{4,5},{5,4},{6,7},{7,6},{8,9},{9,8},{10,11... | collective-permute-start | bytes 835592 | tf_op jit(solution)/shard_map/ppermute | solution.py:524
  19.4 5.2 %collective-permute-start.6 = (f32[17,8,512]{2,1,0:T(8,128)S(1)}, f32[17,8,512]{2,1,0:T(8,128)S(1)}, u32[]{:S(2)}, u32[]{:S(2)}) collective-permute-start(f32[17,8,512]{2,1,0:T(8,128)S(1)} %collective-permute-done.refs_3_), channel_id=1, source_target_pairs={{1,2},{2,1},{5,6},{6,5},{9,10},{10,9},{13,14},{14,13},{17,18},{18,... | collective-permute-start | bytes 835592 | tf_op jit(solution)/shard_map/ppermute | solution.py:530
  20.1 4.5 %collective-permute-start.3 = (f32[17,8,512]{2,1,0:T(8,128)S(1)}, f32[17,8,512]{2,1,0:T(8,128)S(1)}, u32[]{:S(2)}, u32[]{:S(2)}) collective-permute-start(f32[17,8,512]{2,1,0:T(8,128)S(1)} %collective-permute-done.refs_3_), channel_id=1, source_target_pairs={{0,1},{1,0},{2,3},{3,2},{4,5},{5,4},{6,7},{7,6},{8,9},{9,8},{10,11... | collective-permute-start | bytes 835592 | tf_op jit(solution)/shard_map/ppermute | solution.py:524
  24.6 37.1 %copy-start = (f32[8,8,512]{2,1,0:T(8,128)S(1)}, f32[8,8,512]{2,1,0:T(8,128)}, u32[]{:S(2)}) copy-start(f32[8,8,512]{2,1,0:T(8,128)} %refs_19_.1) | copy-start | bytes 393220
  36.0 4.3 %collective-permute-start.10 = (f32[56,128]{1,0:T(8,128)S(1)}, f32[56,128]{1,0:T(8,128)S(1)}, u32[]{:S(2)}, u32[]{:S(2)}) collective-permute-start(f32[56,128]{1,0:T(8,128)S(1)} %get-tuple-element.30), channel_id=1, source_target_pairs={{0,3},{1,2},{2,1},{3,0},{4,7},{5,6},{6,5},{7,4},{8,11},{9,10},{10,... | collective-permute-start | bytes 86024 | tf_op jit(solution)/shard_map/ppermute | solution.py:524
  36.3 6.2 %collective-permute-start.9 = (f32[56,128]{1,0:T(8,128)S(1)}, f32[56,128]{1,0:T(8,128)S(1)}, u32[]{:S(2)}, u32[]{:S(2)}) collective-permute-start(f32[56,128]{1,0:T(8,128)S(1)} %get-tuple-element.30), channel_id=1, source_target_pairs={{0,2},{1,3},{2,0},{3,1},{4,6},{5,7},{6,4},{7,5},{8,10},{9,11},{10,... | collective-permute-start | bytes 86024 | tf_op jit(solution)/shard_map/ppermute | solution.py:524
  40.4 2.2 %collective-permute-start.8 = (f32[56,128]{1,0:T(8,128)S(1)}, f32[56,128]{1,0:T(8,128)S(1)}, u32[]{:S(2)}, u32[]{:S(2)}) collective-permute-start(f32[56,128]{1,0:T(8,128)S(1)} %get-tuple-element.30), channel_id=1, source_target_pairs={{0,1},{1,0},{2,3},{3,2},{4,5},{5,4},{6,7},{7,6},{8,9},{9,8},{10,11... | collective-permute-start | bytes 86024 | tf_op jit(solution)/shard_map/ppermute | solution.py:524
  42.5 6.4 %collective-permute-start.11 = (f32[4,56,128]{2,1,0:T(8,128)S(1)}, f32[4,56,128]{2,1,0:T(8,128)S(1)}, u32[]{:S(2)}, u32[]{:S(2)}) collective-permute-start(f32[4,56,128]{2,1,0:T(8,128)S(1)} %pad_maximum_fusion), channel_id=1, source_target_pairs={{0,4},{4,0},{8,12},{12,8},{16,20},{20,16},{24,28},{28,24},{1,5},{5... | collective-permute-start | bytes 344072 | tf_op jit(solution)/shard_map/ppermute | solution.py:524
  48.9 7.5 %collective-permute-start.14 = (f32[2,4,24,128]{3,2,1,0:T(8,128)S(1)}, f32[2,4,24,128]{3,2,1,0:T(8,128)S(1)}, u32[]{:S(2)}, u32[]{:S(2)}) collective-permute-start(f32[2,4,24,128]{3,2,1,0:T(8,128)S(1)} %pad_maximum_fusion.2.refs_1_), channel_id=1, source_target_pairs={{0,24},{4,28},{8,16},{12,20},{16,8},{20,12},{24,0},{28,4},{1,25},{... | collective-permute-start | bytes 294920 | tf_op jit(solution)/shard_map/ppermute | solution.py:524
  52.8 8.9 %collective-permute-start.13 = (f32[2,4,24,128]{3,2,1,0:T(8,128)S(1)}, f32[2,4,24,128]{3,2,1,0:T(8,128)S(1)}, u32[]{:S(2)}, u32[]{:S(2)}) collective-permute-start(f32[2,4,24,128]{3,2,1,0:T(8,128)S(1)} %pad_maximum_fusion.2.refs_1_), channel_id=1, source_target_pairs={{0,16},{4,20},{8,24},{12,28},{16,0},{20,4},{24,8},{28,12},{1,17},{... | collective-permute-start | bytes 294920 | tf_op jit(solution)/shard_map/ppermute | solution.py:524
  52.8 8.9 %collective-permute-start.12 = (f32[2,4,24,128]{3,2,1,0:T(8,128)S(1)}, f32[2,4,24,128]{3,2,1,0:T(8,128)S(1)}, u32[]{:S(2)}, u32[]{:S(2)}) collective-permute-start(f32[2,4,24,128]{3,2,1,0:T(8,128)S(1)} %pad_maximum_fusion.2.refs_1_), channel_id=1, source_target_pairs={{0,8},{4,12},{8,0},{12,4},{16,24},{20,28},{24,16},{28,20},{1,9},{5... | collective-permute-start | bytes 294920 | tf_op jit(solution)/shard_map/ppermute | solution.py:524
  53.5 0.7 collective-permute-start.15
  65.9 6.7 %collective-permute-start.17 = (f32[8,8,512]{2,1,0:T(8,128)S(1)}, f32[8,8,512]{2,1,0:T(8,128)S(1)}, u32[]{:S(2)}, u32[]{:S(2)}) collective-permute-start(f32[8,8,512]{2,1,0:T(8,128)S(1)} %shard_map.56.refs_11_.refs_19_), channel_id=1, source_target_pairs={{4,8},{12,16},{20,24},{8,4},{16,12},{24,20},{5,9},{13,17},{21,25},... | collective-permute-start | bytes 393224 | tf_op jit(solution)/shard_map/ppermute | solution.py:530
  66.6 8.0 %collective-permute-start.16 = (f32[8,8,512]{2,1,0:T(8,128)S(1)}, f32[8,8,512]{2,1,0:T(8,128)S(1)}, u32[]{:S(2)}, u32[]{:S(2)}) collective-permute-start(f32[8,8,512]{2,1,0:T(8,128)S(1)} %shard_map.56.refs_11_.refs_19_), channel_id=1, source_target_pairs={{0,4},{4,0},{8,12},{12,8},{16,20},{20,16},{24,28},{28,24},{1,5},{5... | collective-permute-start | bytes 393224 | tf_op jit(solution)/shard_map/ppermute | solution.py:524
  70.6 4.9 %collective-permute-start.21 = (f32[8,8,512]{2,1,0:T(8,128)S(1)}, f32[8,8,512]{2,1,0:T(8,128)S(1)}, u32[]{:S(2)}, u32[]{:S(2)}) collective-permute-start(f32[8,8,512]{2,1,0:T(8,128)S(1)} %shard_map.56.refs_11_.refs_19_), channel_id=1, source_target_pairs={{1,2},{2,1},{5,6},{6,5},{9,10},{10,9},{13,14},{14,13},{17,18},{18,... | collective-permute-start | bytes 393224 | tf_op jit(solution)/shard_map/ppermute | solution.py:530
  71.2 7.4 %collective-permute-start.18 = (f32[8,8,512]{2,1,0:T(8,128)S(1)}, f32[8,8,512]{2,1,0:T(8,128)S(1)}, u32[]{:S(2)}, u32[]{:S(2)}) collective-permute-start(f32[8,8,512]{2,1,0:T(8,128)S(1)} %shard_map.56.refs_11_.refs_19_), channel_id=1, source_target_pairs={{0,1},{1,0},{2,3},{3,2},{4,5},{5,4},{6,7},{7,6},{8,9},{9,8},{10,11... | collective-permute-start | bytes 393224 | tf_op jit(solution)/shard_map/ppermute | solution.py:524
  72.6 6.0 %collective-permute-start.23 = (f32[8,8,512]{2,1,0:T(8,128)S(1)}, f32[8,8,512]{2,1,0:T(8,128)S(1)}, u32[]{:S(2)}, u32[]{:S(2)}) collective-permute-start(f32[8,8,512]{2,1,0:T(8,128)S(1)} %collective-permute-done.17.refs_13_), channel_id=1, source_target_pairs={{1,2},{2,1},{5,6},{6,5},{9,10},{10,9},{13,14},{14,13},{17,18},{18,... | collective-permute-start | bytes 393224 | tf_op jit(solution)/shard_map/ppermute | solution.py:530
  73.3 5.3 %collective-permute-start.20 = (f32[8,8,512]{2,1,0:T(8,128)S(1)}, f32[8,8,512]{2,1,0:T(8,128)S(1)}, u32[]{:S(2)}, u32[]{:S(2)}) collective-permute-start(f32[8,8,512]{2,1,0:T(8,128)S(1)} %collective-permute-done.17.refs_13_), channel_id=1, source_target_pairs={{0,1},{1,0},{2,3},{3,2},{4,5},{5,4},{6,7},{7,6},{8,9},{9,8},{10,11... | collective-permute-start | bytes 393224 | tf_op jit(solution)/shard_map/ppermute | solution.py:524
  74.6 3.9 %collective-permute-start.22 = (f32[8,8,512]{2,1,0:T(8,128)S(1)}, f32[8,8,512]{2,1,0:T(8,128)S(1)}, u32[]{:S(2)}, u32[]{:S(2)}) collective-permute-start(f32[8,8,512]{2,1,0:T(8,128)S(1)} %collective-permute-done.16.refs_12_), channel_id=1, source_target_pairs={{1,2},{2,1},{5,6},{6,5},{9,10},{10,9},{13,14},{14,13},{17,18},{18,... | collective-permute-start | bytes 393224 | tf_op jit(solution)/shard_map/ppermute | solution.py:530
  75.5 4.1 %collective-permute-start.19 = (f32[8,8,512]{2,1,0:T(8,128)S(1)}, f32[8,8,512]{2,1,0:T(8,128)S(1)}, u32[]{:S(2)}, u32[]{:S(2)}) collective-permute-start(f32[8,8,512]{2,1,0:T(8,128)S(1)} %collective-permute-done.16.refs_12_), channel_id=1, source_target_pairs={{0,1},{1,0},{2,3},{3,2},{4,5},{5,4},{6,7},{7,6},{8,9},{9,8},{10,11... | collective-permute-start | bytes 393224 | tf_op jit(solution)/shard_map/ppermute | solution.py:524
  90.9 3.4 %collective-permute-start.26 = (f32[56,128]{1,0:T(8,128)S(1)}, f32[56,128]{1,0:T(8,128)S(1)}, u32[]{:S(2)}, u32[]{:S(2)}) collective-permute-start(f32[56,128]{1,0:T(8,128)S(1)} %get-tuple-element.43), channel_id=1, source_target_pairs={{0,3},{1,2},{2,1},{3,0},{4,7},{5,6},{6,5},{7,4},{8,11},{9,10},{10,... | collective-permute-start | bytes 86024 | tf_op jit(solution)/shard_map/ppermute | solution.py:524
  91.0 5.2 %collective-permute-start.25 = (f32[56,128]{1,0:T(8,128)S(1)}, f32[56,128]{1,0:T(8,128)S(1)}, u32[]{:S(2)}, u32[]{:S(2)}) collective-permute-start(f32[56,128]{1,0:T(8,128)S(1)} %get-tuple-element.43), channel_id=1, source_target_pairs={{0,2},{1,3},{2,0},{3,1},{4,6},{5,7},{6,4},{7,5},{8,10},{9,11},{10,... | collective-permute-start | bytes 86024 | tf_op jit(solution)/shard_map/ppermute | solution.py:524
  94.1 2.1 %collective-permute-start.24 = (f32[56,128]{1,0:T(8,128)S(1)}, f32[56,128]{1,0:T(8,128)S(1)}, u32[]{:S(2)}, u32[]{:S(2)}) collective-permute-start(f32[56,128]{1,0:T(8,128)S(1)} %get-tuple-element.43), channel_id=1, source_target_pairs={{0,1},{1,0},{2,3},{3,2},{4,5},{5,4},{6,7},{7,6},{8,9},{9,8},{10,11... | collective-permute-start | bytes 86024 | tf_op jit(solution)/shard_map/ppermute | solution.py:524
  96.2 5.9 %collective-permute-start.27 = (f32[4,56,128]{2,1,0:T(8,128)S(1)}, f32[4,56,128]{2,1,0:T(8,128)S(1)}, u32[]{:S(2)}, u32[]{:S(2)}) collective-permute-start(f32[4,56,128]{2,1,0:T(8,128)S(1)} %pad_maximum_fusion.1), channel_id=1, source_target_pairs={{0,4},{4,0},{8,12},{12,8},{16,20},{20,16},{24,28},{28,24},{1,5},{5... | collective-permute-start | bytes 344072 | tf_op jit(solution)/shard_map/ppermute | solution.py:524
  102.1 7.2 %collective-permute-start.30 = (f32[2,4,24,128]{3,2,1,0:T(8,128)S(1)}, f32[2,4,24,128]{3,2,1,0:T(8,128)S(1)}, u32[]{:S(2)}, u32[]{:S(2)}) collective-permute-start(f32[2,4,24,128]{3,2,1,0:T(8,128)S(1)} %pad_maximum_fusion.3.refs_1_), channel_id=1, source_target_pairs={{0,24},{4,28},{8,16},{12,20},{16,8},{20,12},{24,0},{28,4},{1,25},{... | collective-permute-start | bytes 294920 | tf_op jit(solution)/shard_map/ppermute | solution.py:524
  106.0 8.7 %collective-permute-start.29 = (f32[2,4,24,128]{3,2,1,0:T(8,128)S(1)}, f32[2,4,24,128]{3,2,1,0:T(8,128)S(1)}, u32[]{:S(2)}, u32[]{:S(2)}) collective-permute-start(f32[2,4,24,128]{3,2,1,0:T(8,128)S(1)} %pad_maximum_fusion.3.refs_1_), channel_id=1, source_target_pairs={{0,16},{4,20},{8,24},{12,28},{16,0},{20,4},{24,8},{28,12},{1,17},{... | collective-permute-start | bytes 294920 | tf_op jit(solution)/shard_map/ppermute | solution.py:524
  106.0 8.7 %collective-permute-start.28 = (f32[2,4,24,128]{3,2,1,0:T(8,128)S(1)}, f32[2,4,24,128]{3,2,1,0:T(8,128)S(1)}, u32[]{:S(2)}, u32[]{:S(2)}) collective-permute-start(f32[2,4,24,128]{3,2,1,0:T(8,128)S(1)} %pad_maximum_fusion.3.refs_1_), channel_id=1, source_target_pairs={{0,8},{4,12},{8,0},{12,4},{16,24},{20,28},{24,16},{28,20},{1,9},{5... | collective-permute-start | bytes 294920 | tf_op jit(solution)/shard_map/ppermute | solution.py:524
  106.6 0.7 collective-permute-start.31

commit v6 on v5

--- a/solution.py
+++ b/solution.py
@@ -524,6 +524,16 @@
     return lax.ppermute(x, axis, [(i, i ^ mask) for i in range(lax.axis_size(axis))])
 
 
+def crossed(x, strip_mask, slab_mask):
+    strips, slabs = lax.axis_size("xy"), lax.axis_size("gz")
+    pairs = [
+        (i * slabs + j, (i ^ strip_mask) * slabs + (j ^ slab_mask))
+        for i in range(strips)
+        for j in range(slabs)
+    ]
+    return lax.ppermute(x, ("xy", "gz"), pairs)
+
+
 def odd_pairs(x, axis):
     size = lax.axis_size(axis)
     pairs = [(i, i + 1) for i in range(1, size - 1, 2)]
@@ -565,9 +575,11 @@
     base = -(-5 * (xl // 4) * (zl // 4) // 8) * 8
 
     def finish(payload, kept, head):
-        slab = [payload] + [swapped(payload, "gz", m) for m in range(1, slabs)]
-        full = jnp.stack(slab)
-        partner = swapped(full, "xy", 1)
+        pair = [payload, swapped(payload, "gz", 1)]
+        pair = jnp.stack(pair)
+        far = [crossed(pair, i, j) for i, j in ((0, 2), (1, 0), (1, 2))]
+        full = jnp.concatenate([pair, far[0]])
+        partner = jnp.concatenate([far[1], far[2]])
         pieces = gather_strips(full[:, :base], partner[:, :base])
         near = [full[:, base:], partner[:, base:], odd_pairs(full[:, base:], "xy")]
         return up(*sizes, where, pieces, near, kept, head)

time: 120 us -> 118 us (0.983)
  waiting for transfers between devices: 32.4 us -> 29.2 us
    ppermute x22 -> x16, waiting for transfers between devices: 32.3 us -> 21.6 us  [swapped(): lax.ppermute(x, axis, [(i, i ^ mask) for i in range(lax.axis_size(axis))])]
    ppermute x0 -> x6, starting transfers between devices: none -> 8.97 us  [crossed(): return lax.ppermute(x, ('xy', 'gz'), pairs)]
    ppermute x22 -> x16, starting transfers between devices: 44.9 us -> 36.9 us  [swapped(): lax.ppermute(x, axis, [(i, i ^ mask) for i in range(lax.axis_size(axis))])]
    ppermute x0 -> x6, waiting for transfers between devices: none -> 7.53 us  [crossed(): return lax.ppermute(x, ('xy', 'gz'), pairs)]
  transfers between devices with their start and end apart: 32 -> 32, of which waited for: 11 -> 13; matrix products, arithmetic and copies ran while one was open for 1% -> 1% of each run, Pallas kernels for 0% -> 0%
where the time goes in v6:
time: 118 us; the launch traced here: 117 us
  starting transfers between devices  52.7 us (45%)
  Pallas kernels  31.8 us (27%)
  waiting for transfers between devices  29.2 us (25%)
  other arithmetic  2.74 us (2%)
    ppermute x16, starting transfers between devices, swapped(): lax.ppermute(x, axis, [(i, i ^ mask) for i in range(lax.axis_size(axis))])  36.9 us
    pallas_call x2, Pallas kernels, down(): pl.pallas_call(functools.partial(down_kernel, first, slabs, strips, zl, x...  22.7 us
    ppermute x16, waiting for transfers between devices, swapped(): lax.ppermute(x, axis, [(i, i ^ mask) for i in range(lax.axis_size(axis))])  21.6 us
    pallas_call x2, Pallas kernels, up(): pl.pallas_call(functools.partial(up_kernel, slabs, strips, zl, xl, counts...  9.13 us
    ppermute x6, starting transfers between devices, crossed(): return lax.ppermute(x, ('xy', 'gz'), pairs)  8.97 us
    ppermute x6, waiting for transfers between devices, crossed(): return lax.ppermute(x, ('xy', 'gz'), pairs)  7.53 us
    ppermute x10, starting transfers between devices, odd_pairs(): return lax.ppermute(x, axis, pairs + [(j, i) for i, j in pairs])  6.81 us
  transfers between devices with their start and end apart: 32, of which 13 were waited for; matrix products, arithmetic and copies ran while one was open for 1% of the time, Pallas kernels for 0%

profile of v6, /device:TPU:0, one launch (start us, length us, event | category | flops | bytes accessed | tf_op | source)
XLA Modules:
  0.0 117.5 jit_solution(18170973184300991515)
XLA Ops:
  0.0 0.8 multiply_bitcast_fusion
  0.8 1.0 pad_add_fusion.refs_2_
  1.8 0.7 collective-permute-start.1
  2.5 5.8 %collective-permute-start = (f32[17,8,512]{2,1,0:T(8,128)S(1)}, f32[17,8,512]{2,1,0:T(8,128)S(1)}, u32[]{:S(2)}, u32[]{:S(2)}) collective-permute-start(f32[17,8,512]{2,1,0:T(8,128)S(1)} %pad_add_fusion.refs_2_), channel_id=1, source_target_pairs={{0,4},{4,0},{8,12},{12,8},{16,20},{20,16},{24,28},{28,24},{1,5},{5... | collective-permute-start | bytes 835592 | tf_op jit(solution)/shard_map/ppermute | solution.py:524
  8.3 0.7 collective-permute-start.5
  8.9 2.9 %collective-permute-start.2 = (f32[17,8,512]{2,1,0:T(8,128)S(1)}, f32[17,8,512]{2,1,0:T(8,128)S(1)}, u32[]{:S(2)}, u32[]{:S(2)}) collective-permute-start(f32[17,8,512]{2,1,0:T(8,128)S(1)} %pad_add_fusion.refs_2_), channel_id=1, source_target_pairs={{0,1},{1,0},{2,3},{3,2},{4,5},{5,4},{6,7},{7,6},{8,9},{9,8},{10,11... | collective-permute-start | bytes 835592 | tf_op jit(solution)/shard_map/ppermute | solution.py:524
  11.9 0.7 collective-permute-start.7
  12.5 1.3 %collective-permute-start.4 = (f32[17,8,512]{2,1,0:T(8,128)S(1)}, f32[17,8,512]{2,1,0:T(8,128)S(1)}, u32[]{:S(2)}, u32[]{:S(2)}) collective-permute-start(f32[17,8,512]{2,1,0:T(8,128)S(1)} %collective-permute-done.1.refs_4_), channel_id=1, source_target_pairs={{0,1},{1,0},{2,3},{3,2},{4,5},{5,4},{6,7},{7,6},{8,9},{9,8},{10,11... | collective-permute-start | bytes 835592 | tf_op jit(solution)/shard_map/ppermute | solution.py:524
  13.9 5.6 %collective-permute-done.refs_3_ = f32[17,8,512]{2,1,0:T(8,128)S(1)} collective-permute-done((f32[17,8,512]{2,1,0:T(8,128)S(1)}, f32[17,8,512]{2,1,0:T(8,128)S(1)}, u32[]{:S(2)}, u32[]{:S(2)}) %collective-permute-start) | collective-permute-done | bytes 278560 | tf_op jit(solution)/shard_map/ppermute | solution.py:524
  19.4 0.7 collective-permute-start.6
  20.1 0.0 collective-permute-done.5.refs_8_
  20.1 2.9 %collective-permute-start.3 = (f32[17,8,512]{2,1,0:T(8,128)S(1)}, f32[17,8,512]{2,1,0:T(8,128)S(1)}, u32[]{:S(2)}, u32[]{:S(2)}) collective-permute-start(f32[17,8,512]{2,1,0:T(8,128)S(1)} %collective-permute-done.refs_3_), channel_id=1, source_target_pairs={{0,1},{1,0},{2,3},{3,2},{4,5},{5,4},{6,7},{7,6},{8,9},{9,8},{10,11... | collective-permute-start | bytes 835592 | tf_op jit(solution)/shard_map/ppermute | solution.py:524
  23.0 0.8 slice_subtract_fusion
  23.8 0.7 unstack.18
  24.5 0.1 pad_add_fusion.1.refs_0_
  24.6 0.0 collective-permute-done.2.refs_5_
  24.6 0.0 collective-permute-done.4.refs_7_
  24.7 0.0 collective-permute-done.6.refs_9_
  24.7 11.3 %shard_map.55 = (f32[56,128]{1,0:T(8,128)S(1)}, f32[24,24,512]{2,1,0:T(8,128)S(1)}, f32[24,24,512]{2,1,0:T(8,128)S(1)}, f32[24,24,512]{2,1,0:T(8,128)S(1)}, f32[...) custom-call(s32[2]{0:T(128)S(1)} %pad_add_fusion.1.refs_0_, ...), custom_call_target="tpu_custom_call" | custom-call | tf_op jit(solution)/shard_map/pallas_call | solution.py:487
  36.0 0.0 copy-start
  36.0 2.7 %collective-permute-start.8 = (f32[56,128]{1,0:T(8,128)S(1)}, f32[56,128]{1,0:T(8,128)S(1)}, u32[]{:S(2)}, u32[]{:S(2)}) collective-permute-start(f32[56,128]{1,0:T(8,128)S(1)} %get-tuple-element.30), channel_id=1, source_target_pairs={{0,1},{1,0},{2,3},{3,2},{4,5},{5,4},{6,7},{7,6},{8,9},{9,8},{10,11... | collective-permute-start | bytes 86024 | tf_op jit(solution)/shard_map/ppermute | solution.py:524
  38.7 0.9 collective-permute-done.8
  39.6 2.5 %collective-permute-start.10 = (f32[2,56,128]{2,1,0:T(8,128)S(1)}, f32[2,56,128]{2,1,0:T(8,128)S(1)}, u32[]{:S(2)}, u32[]{:S(2)}) collective-permute-start(f32[2,56,128]{2,1,0:T(8,128)S(1)} %pad_maximum_fusion.6), channel_id=1, source_target_pairs={{0,4},{1,5},{2,6},{3,7},{4,0},{5,1},{6,2},{7,3},{8,12},{9,13},{10,... | collective-permute-start | bytes 172040 | tf_op jit(solution)/shard_map/ppermute | solution.py:534
  42.1 1.3 %collective-permute-start.11 = (f32[2,56,128]{2,1,0:T(8,128)S(1)}, f32[2,56,128]{2,1,0:T(8,128)S(1)}, u32[]{:S(2)}, u32[]{:S(2)}) collective-permute-start(f32[2,56,128]{2,1,0:T(8,128)S(1)} %pad_maximum_fusion.6), channel_id=1, source_target_pairs={{0,6},{1,7},{2,4},{3,5},{4,2},{5,3},{6,0},{7,1},{8,14},{9,15},{10,... | collective-permute-start | bytes 172040 | tf_op jit(solution)/shard_map/ppermute | solution.py:534
  43.4 0.5 collective-permute-start.9
  43.9 0.6 collective-permute-done.10
  44.5 2.9 %collective-permute-done.11 = f32[2,56,128]{2,1,0:T(8,128)S(1)} collective-permute-done((f32[2,56,128]{2,1,0:T(8,128)S(1)}, f32[2,56,128]{2,1,0:T(8,128)S(1)}, u32[]{:S(2)}, u32[]{:S(2)}) %collective-permute-start.11) | collective-permute-done | bytes 57376 | tf_op jit(solution)/shard_map/ppermute | solution.py:534
  47.4 0.2 collective-permute-done.9
  47.6 4.1 %collective-permute-start.14 = (f32[2,4,24,128]{3,2,1,0:T(8,128)S(1)}, f32[2,4,24,128]{3,2,1,0:T(8,128)S(1)}, u32[]{:S(2)}, u32[]{:S(2)}) collective-permute-start(f32[2,4,24,128]{3,2,1,0:T(8,128)S(1)} %pad_maximum_fusion.refs_1_), channel_id=1, source_target_pairs={{0,24},{4,28},{8,16},{12,20},{16,8},{20,12},{24,0},{28,4},{1,25},{... | collective-permute-start | bytes 294920 | tf_op jit(solution)/shard_map/ppermute | solution.py:524
  51.7 0.0 collective-permute-start.13
  51.7 0.6 collective-permute-start.12
  52.4 0.7 collective-permute-start.15
  53.0 0.0 collective-permute-done.15.refs_7_
  53.0 2.0 %collective-permute-done.14.refs_4_ = f32[2,4,24,128]{3,2,1,0:T(8,128)S(1)} collective-permute-done((f32[2,4,24,128]{3,2,1,0:T(8,128)S(1)}, f32[2,4,24,128]{3,2,1,0:T(8,128)S(1)}, u32[]{:S(2)}, u32[]{:S(2)}) %collective-permute-start.14) | collective-permute-done | bytes 98336 | tf_op jit(solution)/shard_map/ppermute | solution.py:524
  55.1 4.7 %collective-permute-done.13.refs_3_ = f32[2,4,24,128]{3,2,1,0:T(8,128)S(1)} collective-permute-done((f32[2,4,24,128]{3,2,1,0:T(8,128)S(1)}, f32[2,4,24,128]{3,2,1,0:T(8,128)S(1)}, u32[]{:S(2)}, u32[]{:S(2)}) %collective-permute-start.13) | collective-permute-done | bytes 98336 | tf_op jit(solution)/shard_map/ppermute | solution.py:524
  59.7 0.0 collective-permute-done.12.refs_2_
  59.7 4.2 %shard_map.56.refs_11_.refs_19_ = f32[8,8,512]{2,1,0:T(8,128)S(1)} custom-call(s32[2]{0:T(128)S(1)} %pad_add_fusion.1.refs_0_, f32[2,4,24,128]{3,2,1,0:T(8,128)S(1)} %pad_maximum_fusion.refs_1_, f32[2,4,24,128]{3,2,1,0:T(8,128)S(1)} %collective-permute-done.12.refs_2_, f32[2,4,24,128]{3,2,1,0:T(8,128)S(1)} %collective-permute-done.13.refs_3_, ...), custom_call_target="tpu_custom_call" | custom-call | tf_op jit(solution)/shard_map/pallas_call | solution.py:513
  64.0 0.7 collective-permute-start.17
  64.7 3.8 %collective-permute-start.16 = (f32[8,8,512]{2,1,0:T(8,128)S(1)}, f32[8,8,512]{2,1,0:T(8,128)S(1)}, u32[]{:S(2)}, u32[]{:S(2)}) collective-permute-start(f32[8,8,512]{2,1,0:T(8,128)S(1)} %shard_map.56.refs_11_.refs_19_), channel_id=1, source_target_pairs={{0,4},{4,0},{8,12},{12,8},{16,20},{20,16},{24,28},{28,24},{1,5},{5... | collective-permute-start | bytes 393224 | tf_op jit(solution)/shard_map/ppermute | solution.py:524
  68.5 0.7 collective-permute-start.21
  69.2 2.4 %collective-permute-start.18 = (f32[8,8,512]{2,1,0:T(8,128)S(1)}, f32[8,8,512]{2,1,0:T(8,128)S(1)}, u32[]{:S(2)}, u32[]{:S(2)}) collective-permute-start(f32[8,8,512]{2,1,0:T(8,128)S(1)} %shard_map.56.refs_11_.refs_19_), channel_id=1, source_target_pairs={{0,1},{1,0},{2,3},{3,2},{4,5},{5,4},{6,7},{7,6},{8,9},{9,8},{10,11... | collective-permute-start | bytes 393224 | tf_op jit(solution)/shard_map/ppermute | solution.py:524
  71.5 0.7 collective-permute-start.23
  72.2 1.3 %collective-permute-start.20 = (f32[8,8,512]{2,1,0:T(8,128)S(1)}, f32[8,8,512]{2,1,0:T(8,128)S(1)}, u32[]{:S(2)}, u32[]{:S(2)}) collective-permute-start(f32[8,8,512]{2,1,0:T(8,128)S(1)} %collective-permute-done.17.refs_13_), channel_id=1, source_target_pairs={{0,1},{1,0},{2,3},{3,2},{4,5},{5,4},{6,7},{7,6},{8,9},{9,8},{10,11... | collective-permute-start | bytes 393224 | tf_op jit(solution)/shard_map/ppermute | solution.py:524
  73.6 0.8 collective-permute-start.22
  74.4 0.0 collective-permute-done.21.refs_17_
  74.4 3.1 %collective-permute-start.19 = (f32[8,8,512]{2,1,0:T(8,128)S(1)}, f32[8,8,512]{2,1,0:T(8,128)S(1)}, u32[]{:S(2)}, u32[]{:S(2)}) collective-permute-start(f32[8,8,512]{2,1,0:T(8,128)S(1)} %collective-permute-done.16.refs_12_), channel_id=1, source_target_pairs={{0,1},{1,0},{2,3},{3,2},{4,5},{5,4},{6,7},{7,6},{8,9},{9,8},{10,11... | collective-permute-start | bytes 393224 | tf_op jit(solution)/shard_map/ppermute | solution.py:524
  77.5 0.0 collective-permute-done.18.refs_14_
  77.5 0.0 collective-permute-done.22.refs_18_
  77.5 1.0 collective-permute-done.19.refs_15_
  78.5 11.4 %shard_map.57 = (f32[56,128]{1,0:T(8,128)S(1)}, f32[24,24,512]{2,1,0:T(8,128)S(1)}, f32[24,24,512]{2,1,0:T(8,128)S(1)}, f32[24,24,512]{2,1,0:T(8,128)S(1)}, f32[...) custom-call(s32[2]{0:T(128)S(1)} %pad_add_fusion.1.refs_0_, ...), custom_call_target="tpu_custom_call" | custom-call | tf_op jit(solution)/shard_map/pallas_call | solution.py:487
  89.8 1.5 %collective-permute-start.24 = (f32[56,128]{1,0:T(8,128)S(1)}, f32[56,128]{1,0:T(8,128)S(1)}, u32[]{:S(2)}, u32[]{:S(2)}) collective-permute-start(f32[56,128]{1,0:T(8,128)S(1)} %get-tuple-element.43), channel_id=1, source_target_pairs={{0,1},{1,0},{2,3},{3,2},{4,5},{5,4},{6,7},{7,6},{8,9},{9,8},{10,11... | collective-permute-start | bytes 86024 | tf_op jit(solution)/shard_map/ppermute | solution.py:524
  91.3 0.9 collective-permute-done.24
  92.2 3.1 %collective-permute-start.26 = (f32[2,56,128]{2,1,0:T(8,128)S(1)}, f32[2,56,128]{2,1,0:T(8,128)S(1)}, u32[]{:S(2)}, u32[]{:S(2)}) collective-permute-start(f32[2,56,128]{2,1,0:T(8,128)S(1)} %pad_maximum_fusion.7), channel_id=1, source_target_pairs={{0,4},{1,5},{2,6},{3,7},{4,0},{5,1},{6,2},{7,3},{8,12},{9,13},{10,... | collective-permute-start | bytes 172040 | tf_op jit(solution)/shard_map/ppermute | solution.py:534
  95.3 0.3 collective-permute-start.27
  95.6 1.2 %collective-permute-start.25 = (f32[2,56,128]{2,1,0:T(8,128)S(1)}, f32[2,56,128]{2,1,0:T(8,128)S(1)}, u32[]{:S(2)}, u32[]{:S(2)}) collective-permute-start(f32[2,56,128]{2,1,0:T(8,128)S(1)} %pad_maximum_fusion.7), channel_id=1, source_target_pairs={{0,2},{1,3},{2,0},{3,1},{4,6},{5,7},{6,4},{7,5},{8,10},{9,11},{10,... | collective-permute-start | bytes 172040 | tf_op jit(solution)/shard_map/ppermute | solution.py:534
  96.8 0.9 collective-permute-done.26
  97.7 3.0 %collective-permute-done.27 = f32[2,56,128]{2,1,0:T(8,128)S(1)} collective-permute-done((f32[2,56,128]{2,1,0:T(8,128)S(1)}, f32[2,56,128]{2,1,0:T(8,128)S(1)}, u32[]{:S(2)}, u32[]{:S(2)}) %collective-permute-start.27) | collective-permute-done | bytes 57376 | tf_op jit(solution)/shard_map/ppermute | solution.py:534
  100.8 3.2 %collective-permute-start.30 = (f32[2,4,24,128]{3,2,1,0:T(8,128)S(1)}, f32[2,4,24,128]{3,2,1,0:T(8,128)S(1)}, u32[]{:S(2)}, u32[]{:S(2)}) collective-permute-start(f32[2,4,24,128]{3,2,1,0:T(8,128)S(1)} %pad_maximum_fusion.1.refs_1_), channel_id=1, source_target_pairs={{0,24},{4,28},{8,16},{12,20},{16,8},{20,12},{24,0},{28,4},{1,25},{... | collective-permute-start | bytes 294920 | tf_op jit(solution)/shard_map/ppermute | solution.py:524
  104.0 0.0 collective-permute-start.29
  104.0 1.2 %collective-permute-start.28 = (f32[2,4,24,128]{3,2,1,0:T(8,128)S(1)}, f32[2,4,24,128]{3,2,1,0:T(8,128)S(1)}, u32[]{:S(2)}, u32[]{:S(2)}) collective-permute-start(f32[2,4,24,128]{3,2,1,0:T(8,128)S(1)} %pad_maximum_fusion.1.refs_1_), channel_id=1, source_target_pairs={{0,8},{4,12},{8,0},{12,4},{16,24},{20,28},{24,16},{28,20},{1,9},{5... | collective-permute-start | bytes 294920 | tf_op jit(solution)/shard_map/ppermute | solution.py:524
  105.2 0.7 collective-permute-start.31
  105.9 2.2 %collective-permute-done.30.refs_4_ = f32[2,4,24,128]{3,2,1,0:T(8,128)S(1)} collective-permute-done((f32[2,4,24,128]{3,2,1,0:T(8,128)S(1)}, f32[2,4,24,128]{3,2,1,0:T(8,128)S(1)}, u32[]{:S(2)}, u32[]{:S(2)}) %collective-permute-start.30) | collective-permute-done | bytes 98336 | tf_op jit(solution)/shard_map/ppermute | solution.py:524
  108.1 4.4 %collective-permute-done.29.refs_3_ = f32[2,4,24,128]{3,2,1,0:T(8,128)S(1)} collective-permute-done((f32[2,4,24,128]{3,2,1,0:T(8,128)S(1)}, f32[2,4,24,128]{3,2,1,0:T(8,128)S(1)}, u32[]{:S(2)}, u32[]{:S(2)}) %collective-permute-start.29) | collective-permute-done | bytes 98336 | tf_op jit(solution)/shard_map/ppermute | solution.py:524
  112.6 4.9 %shard_map.58 = f32[8,8,512]{2,1,0:T(8,128)} custom-call(s32[2]{0:T(128)S(1)} %pad_add_fusion.1.refs_0_, f32[2,4,24,128]{3,2,1,0:T(8,128)S(1)} %pad_maximum_fusion.1.refs_1_, f32[2,4,24,128]{3,2,1,0:T(8,128)S(1)} %collective-permute-done.28.refs_2_, f32[2,4,24,128]{3,2,1,0:T(8,128)S(1)} %collective-permute-done.29.refs_3_, ...), custom_call_target="tpu_custom_call" | custom-call | tf_op jit(solution)/shard_map/pallas_call | solution.py:513
  (28 shorter events, 0.1 us)
Async XLA Ops:
  1.8 10.0 %collective-permute-start.1 = (f32[17,8,512]{2,1,0:T(8,128)S(1)}, f32[17,8,512]{2,1,0:T(8,128)S(1)}, u32[]{:S(2)}, u32[]{:S(2)}) collective-permute-start(f32[17,8,512]{2,1,0:T(8,128)S(1)} %pad_add_fusion.refs_2_), channel_id=1, source_target_pairs={{4,8},{12,16},{20,24},{8,4},{16,12},{24,20},{5,9},{13,17},{21,25},... | collective-permute-start | bytes 835592 | tf_op jit(solution)/shard_map/ppermute | solution.py:540
  2.5 17.0 %collective-permute-start = (f32[17,8,512]{2,1,0:T(8,128)S(1)}, f32[17,8,512]{2,1,0:T(8,128)S(1)}, u32[]{:S(2)}, u32[]{:S(2)}) collective-permute-start(f32[17,8,512]{2,1,0:T(8,128)S(1)} %pad_add_fusion.refs_2_), channel_id=1, source_target_pairs={{0,4},{4,0},{8,12},{12,8},{16,20},{20,16},{24,28},{28,24},{1,5},{5... | collective-permute-start | bytes 835592 | tf_op jit(solution)/shard_map/ppermute | solution.py:524
  8.3 11.9 %collective-permute-start.5 = (f32[17,8,512]{2,1,0:T(8,128)S(1)}, f32[17,8,512]{2,1,0:T(8,128)S(1)}, u32[]{:S(2)}, u32[]{:S(2)}) collective-permute-start(f32[17,8,512]{2,1,0:T(8,128)S(1)} %pad_add_fusion.refs_2_), channel_id=1, source_target_pairs={{1,2},{2,1},{5,6},{6,5},{9,10},{10,9},{13,14},{14,13},{17,18},{18,... | collective-permute-start | bytes 835592 | tf_op jit(solution)/shard_map/ppermute | solution.py:540
  8.9 15.7 %collective-permute-start.2 = (f32[17,8,512]{2,1,0:T(8,128)S(1)}, f32[17,8,512]{2,1,0:T(8,128)S(1)}, u32[]{:S(2)}, u32[]{:S(2)}) collective-permute-start(f32[17,8,512]{2,1,0:T(8,128)S(1)} %pad_add_fusion.refs_2_), channel_id=1, source_target_pairs={{0,1},{1,0},{2,3},{3,2},{4,5},{5,4},{6,7},{7,6},{8,9},{9,8},{10,11... | collective-permute-start | bytes 835592 | tf_op jit(solution)/shard_map/ppermute | solution.py:524
  11.9 12.8 %collective-permute-start.7 = (f32[17,8,512]{2,1,0:T(8,128)S(1)}, f32[17,8,512]{2,1,0:T(8,128)S(1)}, u32[]{:S(2)}, u32[]{:S(2)}) collective-permute-start(f32[17,8,512]{2,1,0:T(8,128)S(1)} %collective-permute-done.1.refs_4_), channel_id=1, source_target_pairs={{1,2},{2,1},{5,6},{6,5},{9,10},{10,9},{13,14},{14,13},{17,18},{18,... | collective-permute-start | bytes 835592 | tf_op jit(solution)/shard_map/ppermute | solution.py:540
  12.5 12.1 %collective-permute-start.4 = (f32[17,8,512]{2,1,0:T(8,128)S(1)}, f32[17,8,512]{2,1,0:T(8,128)S(1)}, u32[]{:S(2)}, u32[]{:S(2)}) collective-permute-start(f32[17,8,512]{2,1,0:T(8,128)S(1)} %collective-permute-done.1.refs_4_), channel_id=1, source_target_pairs={{0,1},{1,0},{2,3},{3,2},{4,5},{5,4},{6,7},{7,6},{8,9},{9,8},{10,11... | collective-permute-start | bytes 835592 | tf_op jit(solution)/shard_map/ppermute | solution.py:524
  19.4 5.2 %collective-permute-start.6 = (f32[17,8,512]{2,1,0:T(8,128)S(1)}, f32[17,8,512]{2,1,0:T(8,128)S(1)}, u32[]{:S(2)}, u32[]{:S(2)}) collective-permute-start(f32[17,8,512]{2,1,0:T(8,128)S(1)} %collective-permute-done.refs_3_), channel_id=1, source_target_pairs={{1,2},{2,1},{5,6},{6,5},{9,10},{10,9},{13,14},{14,13},{17,18},{18,... | collective-permute-start | bytes 835592 | tf_op jit(solution)/shard_map/ppermute | solution.py:540
  20.1 4.5 %collective-permute-start.3 = (f32[17,8,512]{2,1,0:T(8,128)S(1)}, f32[17,8,512]{2,1,0:T(8,128)S(1)}, u32[]{:S(2)}, u32[]{:S(2)}) collective-permute-start(f32[17,8,512]{2,1,0:T(8,128)S(1)} %collective-permute-done.refs_3_), channel_id=1, source_target_pairs={{0,1},{1,0},{2,3},{3,2},{4,5},{5,4},{6,7},{7,6},{8,9},{9,8},{10,11... | collective-permute-start | bytes 835592 | tf_op jit(solution)/shard_map/ppermute | solution.py:524
  36.0 23.7 %copy-start = (f32[8,8,512]{2,1,0:T(8,128)S(1)}, f32[8,8,512]{2,1,0:T(8,128)}, u32[]{:S(2)}) copy-start(f32[8,8,512]{2,1,0:T(8,128)} %refs_19_.1) | copy-start | bytes 393220
  36.0 3.6 %collective-permute-start.8 = (f32[56,128]{1,0:T(8,128)S(1)}, f32[56,128]{1,0:T(8,128)S(1)}, u32[]{:S(2)}, u32[]{:S(2)}) collective-permute-start(f32[56,128]{1,0:T(8,128)S(1)} %get-tuple-element.30), channel_id=1, source_target_pairs={{0,1},{1,0},{2,3},{3,2},{4,5},{5,4},{6,7},{7,6},{8,9},{9,8},{10,11... | collective-permute-start | bytes 86024 | tf_op jit(solution)/shard_map/ppermute | solution.py:524
  39.6 4.9 %collective-permute-start.10 = (f32[2,56,128]{2,1,0:T(8,128)S(1)}, f32[2,56,128]{2,1,0:T(8,128)S(1)}, u32[]{:S(2)}, u32[]{:S(2)}) collective-permute-start(f32[2,56,128]{2,1,0:T(8,128)S(1)} %pad_maximum_fusion.6), channel_id=1, source_target_pairs={{0,4},{1,5},{2,6},{3,7},{4,0},{5,1},{6,2},{7,3},{8,12},{9,13},{10,... | collective-permute-start | bytes 172040 | tf_op jit(solution)/shard_map/ppermute | solution.py:534
  42.1 5.3 %collective-permute-start.11 = (f32[2,56,128]{2,1,0:T(8,128)S(1)}, f32[2,56,128]{2,1,0:T(8,128)S(1)}, u32[]{:S(2)}, u32[]{:S(2)}) collective-permute-start(f32[2,56,128]{2,1,0:T(8,128)S(1)} %pad_maximum_fusion.6), channel_id=1, source_target_pairs={{0,6},{1,7},{2,4},{3,5},{4,2},{5,3},{6,0},{7,1},{8,14},{9,15},{10,... | collective-permute-start | bytes 172040 | tf_op jit(solution)/shard_map/ppermute | solution.py:534
  43.4 4.2 %collective-permute-start.9 = (f32[2,56,128]{2,1,0:T(8,128)S(1)}, f32[2,56,128]{2,1,0:T(8,128)S(1)}, u32[]{:S(2)}, u32[]{:S(2)}) collective-permute-start(f32[2,56,128]{2,1,0:T(8,128)S(1)} %pad_maximum_fusion.6), channel_id=1, source_target_pairs={{0,2},{1,3},{2,0},{3,1},{4,6},{5,7},{6,4},{7,5},{8,10},{9,11},{10,... | collective-permute-start | bytes 172040 | tf_op jit(solution)/shard_map/ppermute | solution.py:534
  47.6 7.5 %collective-permute-start.14 = (f32[2,4,24,128]{3,2,1,0:T(8,128)S(1)}, f32[2,4,24,128]{3,2,1,0:T(8,128)S(1)}, u32[]{:S(2)}, u32[]{:S(2)}) collective-permute-start(f32[2,4,24,128]{3,2,1,0:T(8,128)S(1)} %pad_maximum_fusion.refs_1_), channel_id=1, source_target_pairs={{0,24},{4,28},{8,16},{12,20},{16,8},{20,12},{24,0},{28,4},{1,25},{... | collective-permute-start | bytes 294920 | tf_op jit(solution)/shard_map/ppermute | solution.py:524
  51.7 8.0 %collective-permute-start.13 = (f32[2,4,24,128]{3,2,1,0:T(8,128)S(1)}, f32[2,4,24,128]{3,2,1,0:T(8,128)S(1)}, u32[]{:S(2)}, u32[]{:S(2)}) collective-permute-start(f32[2,4,24,128]{3,2,1,0:T(8,128)S(1)} %pad_maximum_fusion.refs_1_), channel_id=1, source_target_pairs={{0,16},{4,20},{8,24},{12,28},{16,0},{20,4},{24,8},{28,12},{1,17},{... | collective-permute-start | bytes 294920 | tf_op jit(solution)/shard_map/ppermute | solution.py:524
  51.7 8.0 %collective-permute-start.12 = (f32[2,4,24,128]{3,2,1,0:T(8,128)S(1)}, f32[2,4,24,128]{3,2,1,0:T(8,128)S(1)}, u32[]{:S(2)}, u32[]{:S(2)}) collective-permute-start(f32[2,4,24,128]{3,2,1,0:T(8,128)S(1)} %pad_maximum_fusion.refs_1_), channel_id=1, source_target_pairs={{0,8},{4,12},{8,0},{12,4},{16,24},{20,28},{24,16},{28,20},{1,9},{5... | collective-permute-start | bytes 294920 | tf_op jit(solution)/shard_map/ppermute | solution.py:524
  52.4 0.7 collective-permute-start.15
  64.0 7.6 %collective-permute-start.17 = (f32[8,8,512]{2,1,0:T(8,128)S(1)}, f32[8,8,512]{2,1,0:T(8,128)S(1)}, u32[]{:S(2)}, u32[]{:S(2)}) collective-permute-start(f32[8,8,512]{2,1,0:T(8,128)S(1)} %shard_map.56.refs_11_.refs_19_), channel_id=1, source_target_pairs={{4,8},{12,16},{20,24},{8,4},{16,12},{24,20},{5,9},{13,17},{21,25},... | collective-permute-start | bytes 393224 | tf_op jit(solution)/shard_map/ppermute | solution.py:540
  64.7 8.9 %collective-permute-start.16 = (f32[8,8,512]{2,1,0:T(8,128)S(1)}, f32[8,8,512]{2,1,0:T(8,128)S(1)}, u32[]{:S(2)}, u32[]{:S(2)}) collective-permute-start(f32[8,8,512]{2,1,0:T(8,128)S(1)} %shard_map.56.refs_11_.refs_19_), channel_id=1, source_target_pairs={{0,4},{4,0},{8,12},{12,8},{16,20},{20,16},{24,28},{28,24},{1,5},{5... | collective-permute-start | bytes 393224 | tf_op jit(solution)/shard_map/ppermute | solution.py:524
  68.5 5.9 %collective-permute-start.21 = (f32[8,8,512]{2,1,0:T(8,128)S(1)}, f32[8,8,512]{2,1,0:T(8,128)S(1)}, u32[]{:S(2)}, u32[]{:S(2)}) collective-permute-start(f32[8,8,512]{2,1,0:T(8,128)S(1)} %shard_map.56.refs_11_.refs_19_), channel_id=1, source_target_pairs={{1,2},{2,1},{5,6},{6,5},{9,10},{10,9},{13,14},{14,13},{17,18},{18,... | collective-permute-start | bytes 393224 | tf_op jit(solution)/shard_map/ppermute | solution.py:540
  69.2 8.3 %collective-permute-start.18 = (f32[8,8,512]{2,1,0:T(8,128)S(1)}, f32[8,8,512]{2,1,0:T(8,128)S(1)}, u32[]{:S(2)}, u32[]{:S(2)}) collective-permute-start(f32[8,8,512]{2,1,0:T(8,128)S(1)} %shard_map.56.refs_11_.refs_19_), channel_id=1, source_target_pairs={{0,1},{1,0},{2,3},{3,2},{4,5},{5,4},{6,7},{7,6},{8,9},{9,8},{10,11... | collective-permute-start | bytes 393224 | tf_op jit(solution)/shard_map/ppermute | solution.py:524
  71.5 6.0 %collective-permute-start.23 = (f32[8,8,512]{2,1,0:T(8,128)S(1)}, f32[8,8,512]{2,1,0:T(8,128)S(1)}, u32[]{:S(2)}, u32[]{:S(2)}) collective-permute-start(f32[8,8,512]{2,1,0:T(8,128)S(1)} %collective-permute-done.17.refs_13_), channel_id=1, source_target_pairs={{1,2},{2,1},{5,6},{6,5},{9,10},{10,9},{13,14},{14,13},{17,18},{18,... | collective-permute-start | bytes 393224 | tf_op jit(solution)/shard_map/ppermute | solution.py:540
  72.2 5.3 %collective-permute-start.20 = (f32[8,8,512]{2,1,0:T(8,128)S(1)}, f32[8,8,512]{2,1,0:T(8,128)S(1)}, u32[]{:S(2)}, u32[]{:S(2)}) collective-permute-start(f32[8,8,512]{2,1,0:T(8,128)S(1)} %collective-permute-done.17.refs_13_), channel_id=1, source_target_pairs={{0,1},{1,0},{2,3},{3,2},{4,5},{5,4},{6,7},{7,6},{8,9},{9,8},{10,11... | collective-permute-start | bytes 393224 | tf_op jit(solution)/shard_map/ppermute | solution.py:524
  73.6 3.9 %collective-permute-start.22 = (f32[8,8,512]{2,1,0:T(8,128)S(1)}, f32[8,8,512]{2,1,0:T(8,128)S(1)}, u32[]{:S(2)}, u32[]{:S(2)}) collective-permute-start(f32[8,8,512]{2,1,0:T(8,128)S(1)} %collective-permute-done.16.refs_12_), channel_id=1, source_target_pairs={{1,2},{2,1},{5,6},{6,5},{9,10},{10,9},{13,14},{14,13},{17,18},{18,... | collective-permute-start | bytes 393224 | tf_op jit(solution)/shard_map/ppermute | solution.py:540
  74.4 4.1 %collective-permute-start.19 = (f32[8,8,512]{2,1,0:T(8,128)S(1)}, f32[8,8,512]{2,1,0:T(8,128)S(1)}, u32[]{:S(2)}, u32[]{:S(2)}) collective-permute-start(f32[8,8,512]{2,1,0:T(8,128)S(1)} %collective-permute-done.16.refs_12_), channel_id=1, source_target_pairs={{0,1},{1,0},{2,3},{3,2},{4,5},{5,4},{6,7},{7,6},{8,9},{9,8},{10,11... | collective-permute-start | bytes 393224 | tf_op jit(solution)/shard_map/ppermute | solution.py:524
  89.8 2.3 %collective-permute-start.24 = (f32[56,128]{1,0:T(8,128)S(1)}, f32[56,128]{1,0:T(8,128)S(1)}, u32[]{:S(2)}, u32[]{:S(2)}) collective-permute-start(f32[56,128]{1,0:T(8,128)S(1)} %get-tuple-element.43), channel_id=1, source_target_pairs={{0,1},{1,0},{2,3},{3,2},{4,5},{5,4},{6,7},{7,6},{8,9},{9,8},{10,11... | collective-permute-start | bytes 86024 | tf_op jit(solution)/shard_map/ppermute | solution.py:524
  92.2 5.6 %collective-permute-start.26 = (f32[2,56,128]{2,1,0:T(8,128)S(1)}, f32[2,56,128]{2,1,0:T(8,128)S(1)}, u32[]{:S(2)}, u32[]{:S(2)}) collective-permute-start(f32[2,56,128]{2,1,0:T(8,128)S(1)} %pad_maximum_fusion.7), channel_id=1, source_target_pairs={{0,4},{1,5},{2,6},{3,7},{4,0},{5,1},{6,2},{7,3},{8,12},{9,13},{10,... | collective-permute-start | bytes 172040 | tf_op jit(solution)/shard_map/ppermute | solution.py:534
  95.3 5.4 %collective-permute-start.27 = (f32[2,56,128]{2,1,0:T(8,128)S(1)}, f32[2,56,128]{2,1,0:T(8,128)S(1)}, u32[]{:S(2)}, u32[]{:S(2)}) collective-permute-start(f32[2,56,128]{2,1,0:T(8,128)S(1)} %pad_maximum_fusion.7), channel_id=1, source_target_pairs={{0,6},{1,7},{2,4},{3,5},{4,2},{5,3},{6,0},{7,1},{8,14},{9,15},{10,... | collective-permute-start | bytes 172040 | tf_op jit(solution)/shard_map/ppermute | solution.py:534
  95.6 5.1 %collective-permute-start.25 = (f32[2,56,128]{2,1,0:T(8,128)S(1)}, f32[2,56,128]{2,1,0:T(8,128)S(1)}, u32[]{:S(2)}, u32[]{:S(2)}) collective-permute-start(f32[2,56,128]{2,1,0:T(8,128)S(1)} %pad_maximum_fusion.7), channel_id=1, source_target_pairs={{0,2},{1,3},{2,0},{3,1},{4,6},{5,7},{6,4},{7,5},{8,10},{9,11},{10,... | collective-permute-start | bytes 172040 | tf_op jit(solution)/shard_map/ppermute | solution.py:534
  100.8 7.3 %collective-permute-start.30 = (f32[2,4,24,128]{3,2,1,0:T(8,128)S(1)}, f32[2,4,24,128]{3,2,1,0:T(8,128)S(1)}, u32[]{:S(2)}, u32[]{:S(2)}) collective-permute-start(f32[2,4,24,128]{3,2,1,0:T(8,128)S(1)} %pad_maximum_fusion.1.refs_1_), channel_id=1, source_target_pairs={{0,24},{4,28},{8,16},{12,20},{16,8},{20,12},{24,0},{28,4},{1,25},{... | collective-permute-start | bytes 294920 | tf_op jit(solution)/shard_map/ppermute | solution.py:524
  104.0 8.6 %collective-permute-start.29 = (f32[2,4,24,128]{3,2,1,0:T(8,128)S(1)}, f32[2,4,24,128]{3,2,1,0:T(8,128)S(1)}, u32[]{:S(2)}, u32[]{:S(2)}) collective-permute-start(f32[2,4,24,128]{3,2,1,0:T(8,128)S(1)} %pad_maximum_fusion.1.refs_1_), channel_id=1, source_target_pairs={{0,16},{4,20},{8,24},{12,28},{16,0},{20,4},{24,8},{28,12},{1,17},{... | collective-permute-start | bytes 294920 | tf_op jit(solution)/shard_map/ppermute | solution.py:524
  104.0 8.6 %collective-permute-start.28 = (f32[2,4,24,128]{3,2,1,0:T(8,128)S(1)}, f32[2,4,24,128]{3,2,1,0:T(8,128)S(1)}, u32[]{:S(2)}, u32[]{:S(2)}) collective-permute-start(f32[2,4,24,128]{3,2,1,0:T(8,128)S(1)} %pad_maximum_fusion.1.refs_1_), channel_id=1, source_target_pairs={{0,8},{4,12},{8,0},{12,4},{16,24},{20,28},{24,16},{28,20},{1,9},{5... | collective-permute-start | bytes 294920 | tf_op jit(solution)/shard_map/ppermute | solution.py:524
  105.2 0.7 collective-permute-start.31

commit v7 on v6

--- a/solution.py
+++ b/solution.py
@@ -150,7 +150,7 @@
         err[z] = jnp.where(parity0 == (z & 1), source * inverse, 0.0)
         return carry
 
-    lax.fori_loop(2, zw - 2, face_step, 0, unroll=4)
+    lax.fori_loop(2, zw - 2, face_step, 0, unroll=5)
 
     def sum0(z):
         return neighbour_sum(
@@ -169,7 +169,7 @@
         err[z] = jnp.where(parity0 == (z & 1), err[z], updated)
         return carry
 
-    lax.fori_loop(3, zw - 3, smooth_step, 0, unroll=3)
+    lax.fori_loop(3, zw - 3, smooth_step, 0, unroll=6)
 
     def coarse_step(k, carry):
         za, zb = 2 * k, 2 * k + 1
@@ -434,7 +434,7 @@
             level1(k, colour)
             return carry
 
-        lax.fori_loop(zl1 - reach, 2 * zl1 + reach, step, 0, unroll=2)
+        lax.fori_loop(zl1 - reach, 2 * zl1 + reach, step, 0, unroll=zl1 + 2 * reach)
 
     up1(0, 2)
     up1(1, 1)
@@ -443,7 +443,7 @@
         e0[i] = e0_in[i + zl - 2] + at1((zl - 2 + i) // 2)
         return carry
 
-    lax.fori_loop(0, zl + 4, join, 0, unroll=3)
+    lax.fori_loop(0, zl + 4, join, 0, unroll=6)
 
     def up0(colour, reach):
         def step(i, carry):
@@ -455,7 +455,7 @@
             e0[i] = jnp.where(parity0 == ((i + colour) & 1), updated, e0[i])
             return carry
 
-        lax.fori_loop(2 - reach, zl + 2 + reach, step, 0, unroll=2)
+        lax.fori_loop(2 - reach, zl + 2 + reach, step, 0, unroll=zl + 2 * reach)
 
     up0(0, 1)
     up0(1, 0)
@@ -541,8 +541,10 @@
 
 
 def neighbourhood(x):
-    row = [x, swapped(x, "xy", 1), odd_pairs(x, "xy")]
-    return row + [swapped(v, "gz", 1) for v in row] + [odd_pairs(v, "gz") for v in row]
+    odd = odd_pairs(x, "xy")
+    row = [x, swapped(x, "xy", 1), odd]
+    far = [odd_pairs(v, "gz") for v in row]
+    return row + [swapped(v, "gz", 1) for v in row] + far
 
 
 def gather_strips(own, partner):

time: 118 us -> 117 us (level)
  Pallas kernels: 31.8 us -> 30.4 us
    pallas_call x2, Pallas kernels: 9.13 us -> 7.8 us  [up(): pl.pallas_call(functools.partial(up_kernel, slabs, strips, zl, xl, counts...]
where the time goes in v7:
time: 117 us; the launch traced here: 116 us
  starting transfers between devices  52.7 us (45%)
  Pallas kernels  30.4 us (26%)
  waiting for transfers between devices  29.2 us (25%)
  other arithmetic  2.74 us (2%)
    ppermute x16, starting transfers between devices, swapped(): lax.ppermute(x, axis, [(i, i ^ mask) for i in range(lax.axis_size(axis))])  36.9 us
    pallas_call x2, Pallas kernels, down(): pl.pallas_call(functools.partial(down_kernel, first, slabs, strips, zl, x...  22.6 us
    ppermute x16, waiting for transfers between devices, swapped(): lax.ppermute(x, axis, [(i, i ^ mask) for i in range(lax.axis_size(axis))])  21.6 us
    ppermute x6, starting transfers between devices, crossed(): return lax.ppermute(x, ('xy', 'gz'), pairs)  8.97 us
    pallas_call x2, Pallas kernels, up(): pl.pallas_call(functools.partial(up_kernel, slabs, strips, zl, xl, counts...  7.8 us
    ppermute x6, waiting for transfers between devices, crossed(): return lax.ppermute(x, ('xy', 'gz'), pairs)  7.53 us
    ppermute x10, starting transfers between devices, odd_pairs(): return lax.ppermute(x, axis, pairs + [(j, i) for i, j in pairs])  6.81 us
  transfers between devices with their start and end apart: 32, of which 13 were waited for; matrix products, arithmetic and copies ran while one was open for 1% of the time, Pallas kernels for 0%

profile of v7, /device:TPU:0, one launch (start us, length us, event | category | flops | bytes accessed | tf_op | source)
XLA Modules:
  0.0 116.0 jit_solution(5524303187757204190)
XLA Ops:
  0.0 0.8 multiply_bitcast_fusion
  0.8 1.0 pad_add_fusion.refs_2_
  1.8 0.7 collective-permute-start.1
  2.5 5.8 %collective-permute-start = (f32[17,8,512]{2,1,0:T(8,128)S(1)}, f32[17,8,512]{2,1,0:T(8,128)S(1)}, u32[]{:S(2)}, u32[]{:S(2)}) collective-permute-start(f32[17,8,512]{2,1,0:T(8,128)S(1)} %pad_add_fusion.refs_2_), channel_id=1, source_target_pairs={{0,4},{4,0},{8,12},{12,8},{16,20},{20,16},{24,28},{28,24},{1,5},{5... | collective-permute-start | bytes 835592 | tf_op jit(solution)/shard_map/ppermute | solution.py:524
  8.3 0.7 collective-permute-start.5
  8.9 2.9 %collective-permute-start.2 = (f32[17,8,512]{2,1,0:T(8,128)S(1)}, f32[17,8,512]{2,1,0:T(8,128)S(1)}, u32[]{:S(2)}, u32[]{:S(2)}) collective-permute-start(f32[17,8,512]{2,1,0:T(8,128)S(1)} %pad_add_fusion.refs_2_), channel_id=1, source_target_pairs={{0,1},{1,0},{2,3},{3,2},{4,5},{5,4},{6,7},{7,6},{8,9},{9,8},{10,11... | collective-permute-start | bytes 835592 | tf_op jit(solution)/shard_map/ppermute | solution.py:524
  11.9 0.7 collective-permute-start.7
  12.5 1.3 %collective-permute-start.4 = (f32[17,8,512]{2,1,0:T(8,128)S(1)}, f32[17,8,512]{2,1,0:T(8,128)S(1)}, u32[]{:S(2)}, u32[]{:S(2)}) collective-permute-start(f32[17,8,512]{2,1,0:T(8,128)S(1)} %collective-permute-done.1.refs_4_), channel_id=1, source_target_pairs={{0,1},{1,0},{2,3},{3,2},{4,5},{5,4},{6,7},{7,6},{8,9},{9,8},{10,11... | collective-permute-start | bytes 835592 | tf_op jit(solution)/shard_map/ppermute | solution.py:524
  13.9 5.6 %collective-permute-done.refs_3_ = f32[17,8,512]{2,1,0:T(8,128)S(1)} collective-permute-done((f32[17,8,512]{2,1,0:T(8,128)S(1)}, f32[17,8,512]{2,1,0:T(8,128)S(1)}, u32[]{:S(2)}, u32[]{:S(2)}) %collective-permute-start) | collective-permute-done | bytes 278560 | tf_op jit(solution)/shard_map/ppermute | solution.py:524
  19.4 0.7 collective-permute-start.6
  20.1 0.0 collective-permute-done.5.refs_8_
  20.1 2.9 %collective-permute-start.3 = (f32[17,8,512]{2,1,0:T(8,128)S(1)}, f32[17,8,512]{2,1,0:T(8,128)S(1)}, u32[]{:S(2)}, u32[]{:S(2)}) collective-permute-start(f32[17,8,512]{2,1,0:T(8,128)S(1)} %collective-permute-done.refs_3_), channel_id=1, source_target_pairs={{0,1},{1,0},{2,3},{3,2},{4,5},{5,4},{6,7},{7,6},{8,9},{9,8},{10,11... | collective-permute-start | bytes 835592 | tf_op jit(solution)/shard_map/ppermute | solution.py:524
  23.0 0.8 slice_subtract_fusion
  23.8 0.7 unstack.18
  24.5 0.1 pad_add_fusion.1.refs_0_
  24.6 0.0 collective-permute-done.2.refs_5_
  24.6 0.0 collective-permute-done.4.refs_7_
  24.7 0.0 collective-permute-done.6.refs_9_
  24.7 11.3 %shard_map.55 = (f32[56,128]{1,0:T(8,128)S(1)}, f32[24,24,512]{2,1,0:T(8,128)S(1)}, f32[24,24,512]{2,1,0:T(8,128)S(1)}, f32[24,24,512]{2,1,0:T(8,128)S(1)}, f32[...) custom-call(s32[2]{0:T(128)S(1)} %pad_add_fusion.1.refs_0_, ...), custom_call_target="tpu_custom_call" | custom-call | tf_op jit(solution)/shard_map/pallas_call | solution.py:487
  35.9 0.0 copy-start
  36.0 2.7 %collective-permute-start.8 = (f32[56,128]{1,0:T(8,128)S(1)}, f32[56,128]{1,0:T(8,128)S(1)}, u32[]{:S(2)}, u32[]{:S(2)}) collective-permute-start(f32[56,128]{1,0:T(8,128)S(1)} %get-tuple-element.30), channel_id=1, source_target_pairs={{0,1},{1,0},{2,3},{3,2},{4,5},{5,4},{6,7},{7,6},{8,9},{9,8},{10,11... | collective-permute-start | bytes 86024 | tf_op jit(solution)/shard_map/ppermute | solution.py:524
  38.7 0.9 collective-permute-done.8
  39.5 2.5 %collective-permute-start.10 = (f32[2,56,128]{2,1,0:T(8,128)S(1)}, f32[2,56,128]{2,1,0:T(8,128)S(1)}, u32[]{:S(2)}, u32[]{:S(2)}) collective-permute-start(f32[2,56,128]{2,1,0:T(8,128)S(1)} %pad_maximum_fusion.6), channel_id=1, source_target_pairs={{0,4},{1,5},{2,6},{3,7},{4,0},{5,1},{6,2},{7,3},{8,12},{9,13},{10,... | collective-permute-start | bytes 172040 | tf_op jit(solution)/shard_map/ppermute | solution.py:534
  42.0 1.3 %collective-permute-start.11 = (f32[2,56,128]{2,1,0:T(8,128)S(1)}, f32[2,56,128]{2,1,0:T(8,128)S(1)}, u32[]{:S(2)}, u32[]{:S(2)}) collective-permute-start(f32[2,56,128]{2,1,0:T(8,128)S(1)} %pad_maximum_fusion.6), channel_id=1, source_target_pairs={{0,6},{1,7},{2,4},{3,5},{4,2},{5,3},{6,0},{7,1},{8,14},{9,15},{10,... | collective-permute-start | bytes 172040 | tf_op jit(solution)/shard_map/ppermute | solution.py:534
  43.3 0.5 collective-permute-start.9
  43.8 0.6 collective-permute-done.10
  44.4 2.9 %collective-permute-done.11 = f32[2,56,128]{2,1,0:T(8,128)S(1)} collective-permute-done((f32[2,56,128]{2,1,0:T(8,128)S(1)}, f32[2,56,128]{2,1,0:T(8,128)S(1)}, u32[]{:S(2)}, u32[]{:S(2)}) %collective-permute-start.11) | collective-permute-done | bytes 57376 | tf_op jit(solution)/shard_map/ppermute | solution.py:534
  47.3 0.2 collective-permute-done.9
  47.5 4.1 %collective-permute-start.14 = (f32[2,4,24,128]{3,2,1,0:T(8,128)S(1)}, f32[2,4,24,128]{3,2,1,0:T(8,128)S(1)}, u32[]{:S(2)}, u32[]{:S(2)}) collective-permute-start(f32[2,4,24,128]{3,2,1,0:T(8,128)S(1)} %pad_maximum_fusion.refs_1_), channel_id=1, source_target_pairs={{0,24},{4,28},{8,16},{12,20},{16,8},{20,12},{24,0},{28,4},{1,25},{... | collective-permute-start | bytes 294920 | tf_op jit(solution)/shard_map/ppermute | solution.py:524
  51.6 0.6 collective-permute-start.12
  52.3 0.7 collective-permute-start.15
  53.0 2.0 %collective-permute-done.14.refs_4_ = f32[2,4,24,128]{3,2,1,0:T(8,128)S(1)} collective-permute-done((f32[2,4,24,128]{3,2,1,0:T(8,128)S(1)}, f32[2,4,24,128]{3,2,1,0:T(8,128)S(1)}, u32[]{:S(2)}, u32[]{:S(2)}) %collective-permute-start.14) | collective-permute-done | bytes 98336 | tf_op jit(solution)/shard_map/ppermute | solution.py:524
  55.0 4.7 %collective-permute-done.13.refs_3_ = f32[2,4,24,128]{3,2,1,0:T(8,128)S(1)} collective-permute-done((f32[2,4,24,128]{3,2,1,0:T(8,128)S(1)}, f32[2,4,24,128]{3,2,1,0:T(8,128)S(1)}, u32[]{:S(2)}, u32[]{:S(2)}) %collective-permute-start.13) | collective-permute-done | bytes 98336 | tf_op jit(solution)/shard_map/ppermute | solution.py:524
  59.7 0.0 collective-permute-done.12.refs_2_
  59.7 3.6 %shard_map.56.refs_11_.refs_19_ = f32[8,8,512]{2,1,0:T(8,128)S(1)} custom-call(s32[2]{0:T(128)S(1)} %pad_add_fusion.1.refs_0_, f32[2,4,24,128]{3,2,1,0:T(8,128)S(1)} %pad_maximum_fusion.refs_1_, f32[2,4,24,128]{3,2,1,0:T(8,128)S(1)} %collective-permute-done.12.refs_2_, f32[2,4,24,128]{3,2,1,0:T(8,128)S(1)} %collective-permute-done.13.refs_3_, ...), custom_call_target="tpu_custom_call" | custom-call | tf_op jit(solution)/shard_map/pallas_call | solution.py:513
  63.3 0.7 collective-permute-start.17
  63.9 3.8 %collective-permute-start.16 = (f32[8,8,512]{2,1,0:T(8,128)S(1)}, f32[8,8,512]{2,1,0:T(8,128)S(1)}, u32[]{:S(2)}, u32[]{:S(2)}) collective-permute-start(f32[8,8,512]{2,1,0:T(8,128)S(1)} %shard_map.56.refs_11_.refs_19_), channel_id=1, source_target_pairs={{0,4},{4,0},{8,12},{12,8},{16,20},{20,16},{24,28},{28,24},{1,5},{5... | collective-permute-start | bytes 393224 | tf_op jit(solution)/shard_map/ppermute | solution.py:524
  67.8 0.7 collective-permute-start.21
  68.4 2.4 %collective-permute-start.18 = (f32[8,8,512]{2,1,0:T(8,128)S(1)}, f32[8,8,512]{2,1,0:T(8,128)S(1)}, u32[]{:S(2)}, u32[]{:S(2)}) collective-permute-start(f32[8,8,512]{2,1,0:T(8,128)S(1)} %shard_map.56.refs_11_.refs_19_), channel_id=1, source_target_pairs={{0,1},{1,0},{2,3},{3,2},{4,5},{5,4},{6,7},{7,6},{8,9},{9,8},{10,11... | collective-permute-start | bytes 393224 | tf_op jit(solution)/shard_map/ppermute | solution.py:524
  70.8 0.7 collective-permute-start.23
  71.5 1.3 %collective-permute-start.20 = (f32[8,8,512]{2,1,0:T(8,128)S(1)}, f32[8,8,512]{2,1,0:T(8,128)S(1)}, u32[]{:S(2)}, u32[]{:S(2)}) collective-permute-start(f32[8,8,512]{2,1,0:T(8,128)S(1)} %collective-permute-done.17.refs_13_), channel_id=1, source_target_pairs={{0,1},{1,0},{2,3},{3,2},{4,5},{5,4},{6,7},{7,6},{8,9},{9,8},{10,11... | collective-permute-start | bytes 393224 | tf_op jit(solution)/shard_map/ppermute | solution.py:524
  72.8 0.0 collective-permute-done.16.refs_12_
  72.8 0.8 collective-permute-start.22
  73.7 0.0 collective-permute-done.21.refs_17_
  73.7 3.1 %collective-permute-start.19 = (f32[8,8,512]{2,1,0:T(8,128)S(1)}, f32[8,8,512]{2,1,0:T(8,128)S(1)}, u32[]{:S(2)}, u32[]{:S(2)}) collective-permute-start(f32[8,8,512]{2,1,0:T(8,128)S(1)} %collective-permute-done.16.refs_12_), channel_id=1, source_target_pairs={{0,1},{1,0},{2,3},{3,2},{4,5},{5,4},{6,7},{7,6},{8,9},{9,8},{10,11... | collective-permute-start | bytes 393224 | tf_op jit(solution)/shard_map/ppermute | solution.py:524
  76.8 0.0 collective-permute-done.22.refs_18_
  76.8 1.0 collective-permute-done.19.refs_15_
  77.8 11.3 %shard_map.57 = (f32[56,128]{1,0:T(8,128)S(1)}, f32[24,24,512]{2,1,0:T(8,128)S(1)}, f32[24,24,512]{2,1,0:T(8,128)S(1)}, f32[24,24,512]{2,1,0:T(8,128)S(1)}, f32[...) custom-call(s32[2]{0:T(128)S(1)} %pad_add_fusion.1.refs_0_, ...), custom_call_target="tpu_custom_call" | custom-call | tf_op jit(solution)/shard_map/pallas_call | solution.py:487
  89.1 1.5 %collective-permute-start.24 = (f32[56,128]{1,0:T(8,128)S(1)}, f32[56,128]{1,0:T(8,128)S(1)}, u32[]{:S(2)}, u32[]{:S(2)}) collective-permute-start(f32[56,128]{1,0:T(8,128)S(1)} %get-tuple-element.43), channel_id=1, source_target_pairs={{0,1},{1,0},{2,3},{3,2},{4,5},{5,4},{6,7},{7,6},{8,9},{9,8},{10,11... | collective-permute-start | bytes 86024 | tf_op jit(solution)/shard_map/ppermute | solution.py:524
  90.5 0.9 collective-permute-done.24
  91.4 3.1 %collective-permute-start.26 = (f32[2,56,128]{2,1,0:T(8,128)S(1)}, f32[2,56,128]{2,1,0:T(8,128)S(1)}, u32[]{:S(2)}, u32[]{:S(2)}) collective-permute-start(f32[2,56,128]{2,1,0:T(8,128)S(1)} %pad_maximum_fusion.7), channel_id=1, source_target_pairs={{0,4},{1,5},{2,6},{3,7},{4,0},{5,1},{6,2},{7,3},{8,12},{9,13},{10,... | collective-permute-start | bytes 172040 | tf_op jit(solution)/shard_map/ppermute | solution.py:534
  94.5 0.3 collective-permute-start.27
  94.8 1.2 %collective-permute-start.25 = (f32[2,56,128]{2,1,0:T(8,128)S(1)}, f32[2,56,128]{2,1,0:T(8,128)S(1)}, u32[]{:S(2)}, u32[]{:S(2)}) collective-permute-start(f32[2,56,128]{2,1,0:T(8,128)S(1)} %pad_maximum_fusion.7), channel_id=1, source_target_pairs={{0,2},{1,3},{2,0},{3,1},{4,6},{5,7},{6,4},{7,5},{8,10},{9,11},{10,... | collective-permute-start | bytes 172040 | tf_op jit(solution)/shard_map/ppermute | solution.py:534
  96.1 0.9 collective-permute-done.26
  97.0 3.0 %collective-permute-done.27 = f32[2,56,128]{2,1,0:T(8,128)S(1)} collective-permute-done((f32[2,56,128]{2,1,0:T(8,128)S(1)}, f32[2,56,128]{2,1,0:T(8,128)S(1)}, u32[]{:S(2)}, u32[]{:S(2)}) %collective-permute-start.27) | collective-permute-done | bytes 57376 | tf_op jit(solution)/shard_map/ppermute | solution.py:534
  100.0 0.0 collective-permute-done.25
  100.0 3.2 %collective-permute-start.30 = (f32[2,4,24,128]{3,2,1,0:T(8,128)S(1)}, f32[2,4,24,128]{3,2,1,0:T(8,128)S(1)}, u32[]{:S(2)}, u32[]{:S(2)}) collective-permute-start(f32[2,4,24,128]{3,2,1,0:T(8,128)S(1)} %pad_maximum_fusion.1.refs_1_), channel_id=1, source_target_pairs={{0,24},{4,28},{8,16},{12,20},{16,8},{20,12},{24,0},{28,4},{1,25},{... | collective-permute-start | bytes 294920 | tf_op jit(solution)/shard_map/ppermute | solution.py:524
  103.2 0.0 collective-permute-start.29
  103.2 1.2 %collective-permute-start.28 = (f32[2,4,24,128]{3,2,1,0:T(8,128)S(1)}, f32[2,4,24,128]{3,2,1,0:T(8,128)S(1)}, u32[]{:S(2)}, u32[]{:S(2)}) collective-permute-start(f32[2,4,24,128]{3,2,1,0:T(8,128)S(1)} %pad_maximum_fusion.1.refs_1_), channel_id=1, source_target_pairs={{0,8},{4,12},{8,0},{12,4},{16,24},{20,28},{24,16},{28,20},{1,9},{5... | collective-permute-start | bytes 294920 | tf_op jit(solution)/shard_map/ppermute | solution.py:524
  104.5 0.7 collective-permute-start.31
  105.1 2.2 %collective-permute-done.30.refs_4_ = f32[2,4,24,128]{3,2,1,0:T(8,128)S(1)} collective-permute-done((f32[2,4,24,128]{3,2,1,0:T(8,128)S(1)}, f32[2,4,24,128]{3,2,1,0:T(8,128)S(1)}, u32[]{:S(2)}, u32[]{:S(2)}) %collective-permute-start.30) | collective-permute-done | bytes 98336 | tf_op jit(solution)/shard_map/ppermute | solution.py:524
  107.4 4.4 %collective-permute-done.29.refs_3_ = f32[2,4,24,128]{3,2,1,0:T(8,128)S(1)} collective-permute-done((f32[2,4,24,128]{3,2,1,0:T(8,128)S(1)}, f32[2,4,24,128]{3,2,1,0:T(8,128)S(1)}, u32[]{:S(2)}, u32[]{:S(2)}) %collective-permute-start.29) | collective-permute-done | bytes 98336 | tf_op jit(solution)/shard_map/ppermute | solution.py:524
  111.8 0.0 collective-permute-done.28.refs_2_
  111.8 4.2 %shard_map.58 = f32[8,8,512]{2,1,0:T(8,128)} custom-call(s32[2]{0:T(128)S(1)} %pad_add_fusion.1.refs_0_, f32[2,4,24,128]{3,2,1,0:T(8,128)S(1)} %pad_maximum_fusion.1.refs_1_, f32[2,4,24,128]{3,2,1,0:T(8,128)S(1)} %collective-permute-done.28.refs_2_, f32[2,4,24,128]{3,2,1,0:T(8,128)S(1)} %collective-permute-done.29.refs_3_, ...), custom_call_target="tpu_custom_call" | custom-call | tf_op jit(solution)/shard_map/pallas_call | solution.py:513
  (28 shorter events, 0.1 us)
Async XLA Ops:
  1.8 10.0 %collective-permute-start.1 = (f32[17,8,512]{2,1,0:T(8,128)S(1)}, f32[17,8,512]{2,1,0:T(8,128)S(1)}, u32[]{:S(2)}, u32[]{:S(2)}) collective-permute-start(f32[17,8,512]{2,1,0:T(8,128)S(1)} %pad_add_fusion.refs_2_), channel_id=1, source_target_pairs={{4,8},{12,16},{20,24},{8,4},{16,12},{24,20},{5,9},{13,17},{21,25},... | collective-permute-start | bytes 835592 | tf_op jit(solution)/shard_map/ppermute | solution.py:540
  2.5 17.0 %collective-permute-start = (f32[17,8,512]{2,1,0:T(8,128)S(1)}, f32[17,8,512]{2,1,0:T(8,128)S(1)}, u32[]{:S(2)}, u32[]{:S(2)}) collective-permute-start(f32[17,8,512]{2,1,0:T(8,128)S(1)} %pad_add_fusion.refs_2_), channel_id=1, source_target_pairs={{0,4},{4,0},{8,12},{12,8},{16,20},{20,16},{24,28},{28,24},{1,5},{5... | collective-permute-start | bytes 835592 | tf_op jit(solution)/shard_map/ppermute | solution.py:524
  8.3 11.9 %collective-permute-start.5 = (f32[17,8,512]{2,1,0:T(8,128)S(1)}, f32[17,8,512]{2,1,0:T(8,128)S(1)}, u32[]{:S(2)}, u32[]{:S(2)}) collective-permute-start(f32[17,8,512]{2,1,0:T(8,128)S(1)} %pad_add_fusion.refs_2_), channel_id=1, source_target_pairs={{1,2},{2,1},{5,6},{6,5},{9,10},{10,9},{13,14},{14,13},{17,18},{18,... | collective-permute-start | bytes 835592 | tf_op jit(solution)/shard_map/ppermute | solution.py:540
  8.9 15.7 %collective-permute-start.2 = (f32[17,8,512]{2,1,0:T(8,128)S(1)}, f32[17,8,512]{2,1,0:T(8,128)S(1)}, u32[]{:S(2)}, u32[]{:S(2)}) collective-permute-start(f32[17,8,512]{2,1,0:T(8,128)S(1)} %pad_add_fusion.refs_2_), channel_id=1, source_target_pairs={{0,1},{1,0},{2,3},{3,2},{4,5},{5,4},{6,7},{7,6},{8,9},{9,8},{10,11... | collective-permute-start | bytes 835592 | tf_op jit(solution)/shard_map/ppermute | solution.py:524
  11.9 12.8 %collective-permute-start.7 = (f32[17,8,512]{2,1,0:T(8,128)S(1)}, f32[17,8,512]{2,1,0:T(8,128)S(1)}, u32[]{:S(2)}, u32[]{:S(2)}) collective-permute-start(f32[17,8,512]{2,1,0:T(8,128)S(1)} %collective-permute-done.1.refs_4_), channel_id=1, source_target_pairs={{1,2},{2,1},{5,6},{6,5},{9,10},{10,9},{13,14},{14,13},{17,18},{18,... | collective-permute-start | bytes 835592 | tf_op jit(solution)/shard_map/ppermute | solution.py:540
  12.5 12.1 %collective-permute-start.4 = (f32[17,8,512]{2,1,0:T(8,128)S(1)}, f32[17,8,512]{2,1,0:T(8,128)S(1)}, u32[]{:S(2)}, u32[]{:S(2)}) collective-permute-start(f32[17,8,512]{2,1,0:T(8,128)S(1)} %collective-permute-done.1.refs_4_), channel_id=1, source_target_pairs={{0,1},{1,0},{2,3},{3,2},{4,5},{5,4},{6,7},{7,6},{8,9},{9,8},{10,11... | collective-permute-start | bytes 835592 | tf_op jit(solution)/shard_map/ppermute | solution.py:524
  19.4 5.2 %collective-permute-start.6 = (f32[17,8,512]{2,1,0:T(8,128)S(1)}, f32[17,8,512]{2,1,0:T(8,128)S(1)}, u32[]{:S(2)}, u32[]{:S(2)}) collective-permute-start(f32[17,8,512]{2,1,0:T(8,128)S(1)} %collective-permute-done.refs_3_), channel_id=1, source_target_pairs={{1,2},{2,1},{5,6},{6,5},{9,10},{10,9},{13,14},{14,13},{17,18},{18,... | collective-permute-start | bytes 835592 | tf_op jit(solution)/shard_map/ppermute | solution.py:540
  20.1 4.5 %collective-permute-start.3 = (f32[17,8,512]{2,1,0:T(8,128)S(1)}, f32[17,8,512]{2,1,0:T(8,128)S(1)}, u32[]{:S(2)}, u32[]{:S(2)}) collective-permute-start(f32[17,8,512]{2,1,0:T(8,128)S(1)} %collective-permute-done.refs_3_), channel_id=1, source_target_pairs={{0,1},{1,0},{2,3},{3,2},{4,5},{5,4},{6,7},{7,6},{8,9},{9,8},{10,11... | collective-permute-start | bytes 835592 | tf_op jit(solution)/shard_map/ppermute | solution.py:524
  35.9 23.7 %copy-start = (f32[8,8,512]{2,1,0:T(8,128)S(1)}, f32[8,8,512]{2,1,0:T(8,128)}, u32[]{:S(2)}) copy-start(f32[8,8,512]{2,1,0:T(8,128)} %refs_19_.1) | copy-start | bytes 393220
  36.0 3.6 %collective-permute-start.8 = (f32[56,128]{1,0:T(8,128)S(1)}, f32[56,128]{1,0:T(8,128)S(1)}, u32[]{:S(2)}, u32[]{:S(2)}) collective-permute-start(f32[56,128]{1,0:T(8,128)S(1)} %get-tuple-element.30), channel_id=1, source_target_pairs={{0,1},{1,0},{2,3},{3,2},{4,5},{5,4},{6,7},{7,6},{8,9},{9,8},{10,11... | collective-permute-start | bytes 86024 | tf_op jit(solution)/shard_map/ppermute | solution.py:524
  39.5 4.9 %collective-permute-start.10 = (f32[2,56,128]{2,1,0:T(8,128)S(1)}, f32[2,56,128]{2,1,0:T(8,128)S(1)}, u32[]{:S(2)}, u32[]{:S(2)}) collective-permute-start(f32[2,56,128]{2,1,0:T(8,128)S(1)} %pad_maximum_fusion.6), channel_id=1, source_target_pairs={{0,4},{1,5},{2,6},{3,7},{4,0},{5,1},{6,2},{7,3},{8,12},{9,13},{10,... | collective-permute-start | bytes 172040 | tf_op jit(solution)/shard_map/ppermute | solution.py:534
  42.0 5.3 %collective-permute-start.11 = (f32[2,56,128]{2,1,0:T(8,128)S(1)}, f32[2,56,128]{2,1,0:T(8,128)S(1)}, u32[]{:S(2)}, u32[]{:S(2)}) collective-permute-start(f32[2,56,128]{2,1,0:T(8,128)S(1)} %pad_maximum_fusion.6), channel_id=1, source_target_pairs={{0,6},{1,7},{2,4},{3,5},{4,2},{5,3},{6,0},{7,1},{8,14},{9,15},{10,... | collective-permute-start | bytes 172040 | tf_op jit(solution)/shard_map/ppermute | solution.py:534
  43.3 4.2 %collective-permute-start.9 = (f32[2,56,128]{2,1,0:T(8,128)S(1)}, f32[2,56,128]{2,1,0:T(8,128)S(1)}, u32[]{:S(2)}, u32[]{:S(2)}) collective-permute-start(f32[2,56,128]{2,1,0:T(8,128)S(1)} %pad_maximum_fusion.6), channel_id=1, source_target_pairs={{0,2},{1,3},{2,0},{3,1},{4,6},{5,7},{6,4},{7,5},{8,10},{9,11},{10,... | collective-permute-start | bytes 172040 | tf_op jit(solution)/shard_map/ppermute | solution.py:534
  47.5 7.5 %collective-permute-start.14 = (f32[2,4,24,128]{3,2,1,0:T(8,128)S(1)}, f32[2,4,24,128]{3,2,1,0:T(8,128)S(1)}, u32[]{:S(2)}, u32[]{:S(2)}) collective-permute-start(f32[2,4,24,128]{3,2,1,0:T(8,128)S(1)} %pad_maximum_fusion.refs_1_), channel_id=1, source_target_pairs={{0,24},{4,28},{8,16},{12,20},{16,8},{20,12},{24,0},{28,4},{1,25},{... | collective-permute-start | bytes 294920 | tf_op jit(solution)/shard_map/ppermute | solution.py:524
  51.6 8.0 %collective-permute-start.13 = (f32[2,4,24,128]{3,2,1,0:T(8,128)S(1)}, f32[2,4,24,128]{3,2,1,0:T(8,128)S(1)}, u32[]{:S(2)}, u32[]{:S(2)}) collective-permute-start(f32[2,4,24,128]{3,2,1,0:T(8,128)S(1)} %pad_maximum_fusion.refs_1_), channel_id=1, source_target_pairs={{0,16},{4,20},{8,24},{12,28},{16,0},{20,4},{24,8},{28,12},{1,17},{... | collective-permute-start | bytes 294920 | tf_op jit(solution)/shard_map/ppermute | solution.py:524
  51.6 8.0 %collective-permute-start.12 = (f32[2,4,24,128]{3,2,1,0:T(8,128)S(1)}, f32[2,4,24,128]{3,2,1,0:T(8,128)S(1)}, u32[]{:S(2)}, u32[]{:S(2)}) collective-permute-start(f32[2,4,24,128]{3,2,1,0:T(8,128)S(1)} %pad_maximum_fusion.refs_1_), channel_id=1, source_target_pairs={{0,8},{4,12},{8,0},{12,4},{16,24},{20,28},{24,16},{28,20},{1,9},{5... | collective-permute-start | bytes 294920 | tf_op jit(solution)/shard_map/ppermute | solution.py:524
  52.3 0.7 collective-permute-start.15
  63.3 7.6 %collective-permute-start.17 = (f32[8,8,512]{2,1,0:T(8,128)S(1)}, f32[8,8,512]{2,1,0:T(8,128)S(1)}, u32[]{:S(2)}, u32[]{:S(2)}) collective-permute-start(f32[8,8,512]{2,1,0:T(8,128)S(1)} %shard_map.56.refs_11_.refs_19_), channel_id=1, source_target_pairs={{4,8},{12,16},{20,24},{8,4},{16,12},{24,20},{5,9},{13,17},{21,25},... | collective-permute-start | bytes 393224 | tf_op jit(solution)/shard_map/ppermute | solution.py:540
  63.9 8.9 %collective-permute-start.16 = (f32[8,8,512]{2,1,0:T(8,128)S(1)}, f32[8,8,512]{2,1,0:T(8,128)S(1)}, u32[]{:S(2)}, u32[]{:S(2)}) collective-permute-start(f32[8,8,512]{2,1,0:T(8,128)S(1)} %shard_map.56.refs_11_.refs_19_), channel_id=1, source_target_pairs={{0,4},{4,0},{8,12},{12,8},{16,20},{20,16},{24,28},{28,24},{1,5},{5... | collective-permute-start | bytes 393224 | tf_op jit(solution)/shard_map/ppermute | solution.py:524
  67.8 5.9 %collective-permute-start.21 = (f32[8,8,512]{2,1,0:T(8,128)S(1)}, f32[8,8,512]{2,1,0:T(8,128)S(1)}, u32[]{:S(2)}, u32[]{:S(2)}) collective-permute-start(f32[8,8,512]{2,1,0:T(8,128)S(1)} %shard_map.56.refs_11_.refs_19_), channel_id=1, source_target_pairs={{1,2},{2,1},{5,6},{6,5},{9,10},{10,9},{13,14},{14,13},{17,18},{18,... | collective-permute-start | bytes 393224 | tf_op jit(solution)/shard_map/ppermute | solution.py:540
  68.4 8.3 %collective-permute-start.18 = (f32[8,8,512]{2,1,0:T(8,128)S(1)}, f32[8,8,512]{2,1,0:T(8,128)S(1)}, u32[]{:S(2)}, u32[]{:S(2)}) collective-permute-start(f32[8,8,512]{2,1,0:T(8,128)S(1)} %shard_map.56.refs_11_.refs_19_), channel_id=1, source_target_pairs={{0,1},{1,0},{2,3},{3,2},{4,5},{5,4},{6,7},{7,6},{8,9},{9,8},{10,11... | collective-permute-start | bytes 393224 | tf_op jit(solution)/shard_map/ppermute | solution.py:524
  70.8 6.0 %collective-permute-start.23 = (f32[8,8,512]{2,1,0:T(8,128)S(1)}, f32[8,8,512]{2,1,0:T(8,128)S(1)}, u32[]{:S(2)}, u32[]{:S(2)}) collective-permute-start(f32[8,8,512]{2,1,0:T(8,128)S(1)} %collective-permute-done.17.refs_13_), channel_id=1, source_target_pairs={{1,2},{2,1},{5,6},{6,5},{9,10},{10,9},{13,14},{14,13},{17,18},{18,... | collective-permute-start | bytes 393224 | tf_op jit(solution)/shard_map/ppermute | solution.py:540
  71.5 5.3 %collective-permute-start.20 = (f32[8,8,512]{2,1,0:T(8,128)S(1)}, f32[8,8,512]{2,1,0:T(8,128)S(1)}, u32[]{:S(2)}, u32[]{:S(2)}) collective-permute-start(f32[8,8,512]{2,1,0:T(8,128)S(1)} %collective-permute-done.17.refs_13_), channel_id=1, source_target_pairs={{0,1},{1,0},{2,3},{3,2},{4,5},{5,4},{6,7},{7,6},{8,9},{9,8},{10,11... | collective-permute-start | bytes 393224 | tf_op jit(solution)/shard_map/ppermute | solution.py:524
  72.8 3.9 %collective-permute-start.22 = (f32[8,8,512]{2,1,0:T(8,128)S(1)}, f32[8,8,512]{2,1,0:T(8,128)S(1)}, u32[]{:S(2)}, u32[]{:S(2)}) collective-permute-start(f32[8,8,512]{2,1,0:T(8,128)S(1)} %collective-permute-done.16.refs_12_), channel_id=1, source_target_pairs={{1,2},{2,1},{5,6},{6,5},{9,10},{10,9},{13,14},{14,13},{17,18},{18,... | collective-permute-start | bytes 393224 | tf_op jit(solution)/shard_map/ppermute | solution.py:540
  73.7 4.1 %collective-permute-start.19 = (f32[8,8,512]{2,1,0:T(8,128)S(1)}, f32[8,8,512]{2,1,0:T(8,128)S(1)}, u32[]{:S(2)}, u32[]{:S(2)}) collective-permute-start(f32[8,8,512]{2,1,0:T(8,128)S(1)} %collective-permute-done.16.refs_12_), channel_id=1, source_target_pairs={{0,1},{1,0},{2,3},{3,2},{4,5},{5,4},{6,7},{7,6},{8,9},{9,8},{10,11... | collective-permute-start | bytes 393224 | tf_op jit(solution)/shard_map/ppermute | solution.py:524
  89.1 2.3 %collective-permute-start.24 = (f32[56,128]{1,0:T(8,128)S(1)}, f32[56,128]{1,0:T(8,128)S(1)}, u32[]{:S(2)}, u32[]{:S(2)}) collective-permute-start(f32[56,128]{1,0:T(8,128)S(1)} %get-tuple-element.43), channel_id=1, source_target_pairs={{0,1},{1,0},{2,3},{3,2},{4,5},{5,4},{6,7},{7,6},{8,9},{9,8},{10,11... | collective-permute-start | bytes 86024 | tf_op jit(solution)/shard_map/ppermute | solution.py:524
  91.4 5.6 %collective-permute-start.26 = (f32[2,56,128]{2,1,0:T(8,128)S(1)}, f32[2,56,128]{2,1,0:T(8,128)S(1)}, u32[]{:S(2)}, u32[]{:S(2)}) collective-permute-start(f32[2,56,128]{2,1,0:T(8,128)S(1)} %pad_maximum_fusion.7), channel_id=1, source_target_pairs={{0,4},{1,5},{2,6},{3,7},{4,0},{5,1},{6,2},{7,3},{8,12},{9,13},{10,... | collective-permute-start | bytes 172040 | tf_op jit(solution)/shard_map/ppermute | solution.py:534
  94.5 5.4 %collective-permute-start.27 = (f32[2,56,128]{2,1,0:T(8,128)S(1)}, f32[2,56,128]{2,1,0:T(8,128)S(1)}, u32[]{:S(2)}, u32[]{:S(2)}) collective-permute-start(f32[2,56,128]{2,1,0:T(8,128)S(1)} %pad_maximum_fusion.7), channel_id=1, source_target_pairs={{0,6},{1,7},{2,4},{3,5},{4,2},{5,3},{6,0},{7,1},{8,14},{9,15},{10,... | collective-permute-start | bytes 172040 | tf_op jit(solution)/shard_map/ppermute | solution.py:534
  94.8 5.1 %collective-permute-start.25 = (f32[2,56,128]{2,1,0:T(8,128)S(1)}, f32[2,56,128]{2,1,0:T(8,128)S(1)}, u32[]{:S(2)}, u32[]{:S(2)}) collective-permute-start(f32[2,56,128]{2,1,0:T(8,128)S(1)} %pad_maximum_fusion.7), channel_id=1, source_target_pairs={{0,2},{1,3},{2,0},{3,1},{4,6},{5,7},{6,4},{7,5},{8,10},{9,11},{10,... | collective-permute-start | bytes 172040 | tf_op jit(solution)/shard_map/ppermute | solution.py:534
  100.0 7.4 %collective-permute-start.30 = (f32[2,4,24,128]{3,2,1,0:T(8,128)S(1)}, f32[2,4,24,128]{3,2,1,0:T(8,128)S(1)}, u32[]{:S(2)}, u32[]{:S(2)}) collective-permute-start(f32[2,4,24,128]{3,2,1,0:T(8,128)S(1)} %pad_maximum_fusion.1.refs_1_), channel_id=1, source_target_pairs={{0,24},{4,28},{8,16},{12,20},{16,8},{20,12},{24,0},{28,4},{1,25},{... | collective-permute-start | bytes 294920 | tf_op jit(solution)/shard_map/ppermute | solution.py:524
  103.2 8.6 %collective-permute-start.29 = (f32[2,4,24,128]{3,2,1,0:T(8,128)S(1)}, f32[2,4,24,128]{3,2,1,0:T(8,128)S(1)}, u32[]{:S(2)}, u32[]{:S(2)}) collective-permute-start(f32[2,4,24,128]{3,2,1,0:T(8,128)S(1)} %pad_maximum_fusion.1.refs_1_), channel_id=1, source_target_pairs={{0,16},{4,20},{8,24},{12,28},{16,0},{20,4},{24,8},{28,12},{1,17},{... | collective-permute-start | bytes 294920 | tf_op jit(solution)/shard_map/ppermute | solution.py:524
  103.2 8.6 %collective-permute-start.28 = (f32[2,4,24,128]{3,2,1,0:T(8,128)S(1)}, f32[2,4,24,128]{3,2,1,0:T(8,128)S(1)}, u32[]{:S(2)}, u32[]{:S(2)}) collective-permute-start(f32[2,4,24,128]{3,2,1,0:T(8,128)S(1)} %pad_maximum_fusion.1.refs_1_), channel_id=1, source_target_pairs={{0,8},{4,12},{8,0},{12,4},{16,24},{20,28},{24,16},{28,20},{1,9},{5... | collective-permute-start | bytes 294920 | tf_op jit(solution)/shard_map/ppermute | solution.py:524
  104.5 0.7 collective-permute-start.31
